TPU v7x, 1024 devices: a whole 4x8x16 slice. The times are simulated.
1024 devices in a mesh: row: 32 (over x, z_lo, core), col: 8 (over y), layer: 4 (over z_hi).
Axes of the slice: x: 4, y: 8, z: 16 (z_hi: 4, z_lo: 4; z = z_hi * 4 + z_lo), core: 2. Of those that a mesh axis runs over, the one named last changes fastest.
Arguments:
- x_blocks: bfloat16 [2048, 32, 1024], P('row', None, 'col'), may hold values from -1.5 to 1.5
- shifts: int32 [32, 32], replicated, may hold values from 0 to 63
Outputs:
- squared: bfloat16 [2048, 32, 1024], P(('row', 'layer'), None, 'col')
All inputs are finite; a program needn't handle non-finite values.
Results may differ from a plain program's by a relative error of at most 0.001.
Values may be sent and summed in bfloat16 or wider, within the bound.
No kernel may reach another device: no remote copies, remote signals or barrier semaphores. Data moves between devices by JAX's collectives and lax.ppermute only.
A program may use at most 32 MiB of HBM per device.

v0:
```python
import jax
import jax.numpy as jnp
from jax import lax
from jax.sharding import PartitionSpec as P


def passed_along(value, axis, steps):
    count = lax.axis_size(axis)
    pairs = [(source, (source + steps) % count) for source in range(count)]
    return lax.ppermute(value, axis, pairs)


def rotate_rows(blocks, amount):
    doubled = jnp.concatenate([blocks, blocks], axis=0)
    return lax.dynamic_slice_in_dim(doubled, amount, blocks.shape[0], 0)


def add_products(totals, left_blocks, right_blocks, matches):
    block_size = left_blocks.shape[1]
    product_terms = jnp.einsum(
        "pij,pjk->pik", left_blocks, right_blocks, preferred_element_type=jnp.float32
    )
    column_mask = jnp.repeat(matches, block_size)
    return totals + jnp.where(column_mask[None, None, :], product_terms, 0.0)


def local(x_blocks, shifts):
    row_count = lax.axis_size("row")
    col_count = lax.axis_size("col")
    layer_count = lax.axis_size("layer")
    row_index = lax.axis_index("row")
    col_index = lax.axis_index("col")
    layer_index = lax.axis_index("layer")
    ranges_all = col_count * layer_count
    per_row = ranges_all // row_count
    rows_local, block_size, width = x_blocks.shape
    range_rows = rows_local // per_row
    full_rows = lax.all_gather(x_blocks, "col", axis=2, tiled=True)
    own_target = col_index * layer_count + layer_index
    current = lax.dynamic_slice_in_dim(x_blocks, layer_index * block_size, block_size, 2)

    def accumulate(totals, current, turn_index):
        source_row = (row_index + turn_index) % row_count
        target_range = per_row * row_index + 0
        running = totals
        source_range = per_row * source_row + 0
        offset_now = shifts[target_range, source_range]
        left_blocks = lax.dynamic_slice_in_dim(full_rows, source_range * block_size, block_size, 2)
        right_blocks = rotate_rows(current, offset_now)
        matched = (
            offset_now + shifts[source_range, own_target] - shifts[target_range, own_target]
        ) % range_rows == 0
        running = add_products(running, left_blocks, right_blocks, matched[None])
        row_parts = [running]
        return jnp.concatenate(row_parts, axis=0)

    totals = jnp.zeros((rows_local, block_size, block_size), jnp.float32)
    totals = accumulate(totals, current, 0)

    def turn_body(turn_index, loop_state):
        totals, current = loop_state
        current = passed_along(current, "row", -1)
        return (accumulate(totals, current, turn_index), current)

    totals, current = lax.fori_loop(1, row_count, turn_body, (totals, current))
    squared = totals.astype(jnp.bfloat16)
    return lax.all_to_all(squared, "layer", split_axis=0, concat_axis=2, tiled=True)


def solution(mesh):
    return jax.shard_map(
        local,
        mesh=mesh,
        in_specs=(P("row", None, "col"), P()),
        out_specs=P(("row", "layer"), None, "col"),
        check_vma=False,
    )
```

profile of v0, /device:TPU:1, one launch (start us, length us, event | category | flops | bytes accessed | tf_op | source)
XLA Modules:
  0.0 554.5 jit_solution(17134044002963789852)
XLA Ops:
  15.2 70.8 %all-gather.2.cloned.1.call-done = bf16[64,32,1024]{2,1,0:T(8,128)(2,1)} async-done(((bf16[64,32,128]{2,1,0:T(8,128)(2,1)}), bf16[64,32,1024]{2,1,0:T(8,128)(2,1)}) %all-gather.2.cloned.1.call-update) | async-done | bytes 4194320 | tf_op jit(solution)/shard_map/all_gather | solution.py:38
  87.4 436.3 %while.18 = (s32[]{:T(128)}, f32[64,32,32]{2,1,0:T(8,128)S(1)}, bf16[64,32,32]{0,2,1:T(8,128)(2,1)S(1)}, s32[]{:T(128)}, s32[32,32]{1,0:T(8,128)}, /*index=5*/s3...) while((s32[]{:T(128)}, f32[64,32,32]{2,1,0:T(8,128)S(1)}, ...), condition=%wide.region_1.2_spmd, body=%wide.region_0.1_spmd.sunk | while | flops 4587558 | bytes 2490979 | solution.py:65
  87.4 8.0 %collective-permute-start = (bf16[64,32,32]{0,2,1:T(8,128)(2,1)S(1)}, bf16[64,32,32]{0,2,1:T(8,128)(2,1)S(1)}, u32[]{:S(2)}, u32[]{:S(2)}) collective-permute-start(bf16[64,32,32]{0,2,1:T(8,128)(2,1)S(1)} %get-tuple-element.341), channel_id=1, source_target_pairs={{0,992},{32,0},{64,32},{96,64},{128,96},{160,128},{192,160},{224,1... | collective-permute-start | bytes 393224 | tf_op jit(solution)/shard_map/while/body/eval_jaxpr/ppermute | solution.py:10
  211.7 6.6 %collective-permute-start = (bf16[64,32,32]{0,2,1:T(8,128)(2,1)S(1)}, bf16[64,32,32]{0,2,1:T(8,128)(2,1)S(1)}, u32[]{:S(2)}, u32[]{:S(2)}) collective-permute-start(bf16[64,32,32]{0,2,1:T(8,128)(2,1)S(1)} %get-tuple-element.341), channel_id=1, source_target_pairs={{0,992},{32,0},{64,32},{96,64},{128,96},{160,128},{192,160},{224,1... | collective-permute-start | bytes 393224 | tf_op jit(solution)/shard_map/while/body/eval_jaxpr/ppermute | solution.py:10
  225.9 6.6 %collective-permute-start = (bf16[64,32,32]{0,2,1:T(8,128)(2,1)S(1)}, bf16[64,32,32]{0,2,1:T(8,128)(2,1)S(1)}, u32[]{:S(2)}, u32[]{:S(2)}) collective-permute-start(bf16[64,32,32]{0,2,1:T(8,128)(2,1)S(1)} %get-tuple-element.341), channel_id=1, source_target_pairs={{0,992},{32,0},{64,32},{96,64},{128,96},{160,128},{192,160},{224,1... | collective-permute-start | bytes 393224 | tf_op jit(solution)/shard_map/while/body/eval_jaxpr/ppermute | solution.py:10
  240.1 6.6 %collective-permute-start = (bf16[64,32,32]{0,2,1:T(8,128)(2,1)S(1)}, bf16[64,32,32]{0,2,1:T(8,128)(2,1)S(1)}, u32[]{:S(2)}, u32[]{:S(2)}) collective-permute-start(bf16[64,32,32]{0,2,1:T(8,128)(2,1)S(1)} %get-tuple-element.341), channel_id=1, source_target_pairs={{0,992},{32,0},{64,32},{96,64},{128,96},{160,128},{192,160},{224,1... | collective-permute-start | bytes 393224 | tf_op jit(solution)/shard_map/while/body/eval_jaxpr/ppermute | solution.py:10
  254.2 6.6 %collective-permute-start = (bf16[64,32,32]{0,2,1:T(8,128)(2,1)S(1)}, bf16[64,32,32]{0,2,1:T(8,128)(2,1)S(1)}, u32[]{:S(2)}, u32[]{:S(2)}) collective-permute-start(bf16[64,32,32]{0,2,1:T(8,128)(2,1)S(1)} %get-tuple-element.341), channel_id=1, source_target_pairs={{0,992},{32,0},{64,32},{96,64},{128,96},{160,128},{192,160},{224,1... | collective-permute-start | bytes 393224 | tf_op jit(solution)/shard_map/while/body/eval_jaxpr/ppermute | solution.py:10
  268.4 6.6 %collective-permute-start = (bf16[64,32,32]{0,2,1:T(8,128)(2,1)S(1)}, bf16[64,32,32]{0,2,1:T(8,128)(2,1)S(1)}, u32[]{:S(2)}, u32[]{:S(2)}) collective-permute-start(bf16[64,32,32]{0,2,1:T(8,128)(2,1)S(1)} %get-tuple-element.341), channel_id=1, source_target_pairs={{0,992},{32,0},{64,32},{96,64},{128,96},{160,128},{192,160},{224,1... | collective-permute-start | bytes 393224 | tf_op jit(solution)/shard_map/while/body/eval_jaxpr/ppermute | solution.py:10
  282.6 6.6 %collective-permute-start = (bf16[64,32,32]{0,2,1:T(8,128)(2,1)S(1)}, bf16[64,32,32]{0,2,1:T(8,128)(2,1)S(1)}, u32[]{:S(2)}, u32[]{:S(2)}) collective-permute-start(bf16[64,32,32]{0,2,1:T(8,128)(2,1)S(1)} %get-tuple-element.341), channel_id=1, source_target_pairs={{0,992},{32,0},{64,32},{96,64},{128,96},{160,128},{192,160},{224,1... | collective-permute-start | bytes 393224 | tf_op jit(solution)/shard_map/while/body/eval_jaxpr/ppermute | solution.py:10
  296.8 6.6 %collective-permute-start = (bf16[64,32,32]{0,2,1:T(8,128)(2,1)S(1)}, bf16[64,32,32]{0,2,1:T(8,128)(2,1)S(1)}, u32[]{:S(2)}, u32[]{:S(2)}) collective-permute-start(bf16[64,32,32]{0,2,1:T(8,128)(2,1)S(1)} %get-tuple-element.341), channel_id=1, source_target_pairs={{0,992},{32,0},{64,32},{96,64},{128,96},{160,128},{192,160},{224,1... | collective-permute-start | bytes 393224 | tf_op jit(solution)/shard_map/while/body/eval_jaxpr/ppermute | solution.py:10
  311.0 6.6 %collective-permute-start = (bf16[64,32,32]{0,2,1:T(8,128)(2,1)S(1)}, bf16[64,32,32]{0,2,1:T(8,128)(2,1)S(1)}, u32[]{:S(2)}, u32[]{:S(2)}) collective-permute-start(bf16[64,32,32]{0,2,1:T(8,128)(2,1)S(1)} %get-tuple-element.341), channel_id=1, source_target_pairs={{0,992},{32,0},{64,32},{96,64},{128,96},{160,128},{192,160},{224,1... | collective-permute-start | bytes 393224 | tf_op jit(solution)/shard_map/while/body/eval_jaxpr/ppermute | solution.py:10
  325.1 6.6 %collective-permute-start = (bf16[64,32,32]{0,2,1:T(8,128)(2,1)S(1)}, bf16[64,32,32]{0,2,1:T(8,128)(2,1)S(1)}, u32[]{:S(2)}, u32[]{:S(2)}) collective-permute-start(bf16[64,32,32]{0,2,1:T(8,128)(2,1)S(1)} %get-tuple-element.341), channel_id=1, source_target_pairs={{0,992},{32,0},{64,32},{96,64},{128,96},{160,128},{192,160},{224,1... | collective-permute-start | bytes 393224 | tf_op jit(solution)/shard_map/while/body/eval_jaxpr/ppermute | solution.py:10
  339.3 6.6 %collective-permute-start = (bf16[64,32,32]{0,2,1:T(8,128)(2,1)S(1)}, bf16[64,32,32]{0,2,1:T(8,128)(2,1)S(1)}, u32[]{:S(2)}, u32[]{:S(2)}) collective-permute-start(bf16[64,32,32]{0,2,1:T(8,128)(2,1)S(1)} %get-tuple-element.341), channel_id=1, source_target_pairs={{0,992},{32,0},{64,32},{96,64},{128,96},{160,128},{192,160},{224,1... | collective-permute-start | bytes 393224 | tf_op jit(solution)/shard_map/while/body/eval_jaxpr/ppermute | solution.py:10
  353.5 6.6 %collective-permute-start = (bf16[64,32,32]{0,2,1:T(8,128)(2,1)S(1)}, bf16[64,32,32]{0,2,1:T(8,128)(2,1)S(1)}, u32[]{:S(2)}, u32[]{:S(2)}) collective-permute-start(bf16[64,32,32]{0,2,1:T(8,128)(2,1)S(1)} %get-tuple-element.341), channel_id=1, source_target_pairs={{0,992},{32,0},{64,32},{96,64},{128,96},{160,128},{192,160},{224,1... | collective-permute-start | bytes 393224 | tf_op jit(solution)/shard_map/while/body/eval_jaxpr/ppermute | solution.py:10
  367.7 6.6 %collective-permute-start = (bf16[64,32,32]{0,2,1:T(8,128)(2,1)S(1)}, bf16[64,32,32]{0,2,1:T(8,128)(2,1)S(1)}, u32[]{:S(2)}, u32[]{:S(2)}) collective-permute-start(bf16[64,32,32]{0,2,1:T(8,128)(2,1)S(1)} %get-tuple-element.341), channel_id=1, source_target_pairs={{0,992},{32,0},{64,32},{96,64},{128,96},{160,128},{192,160},{224,1... | collective-permute-start | bytes 393224 | tf_op jit(solution)/shard_map/while/body/eval_jaxpr/ppermute | solution.py:10
  381.9 6.6 %collective-permute-start = (bf16[64,32,32]{0,2,1:T(8,128)(2,1)S(1)}, bf16[64,32,32]{0,2,1:T(8,128)(2,1)S(1)}, u32[]{:S(2)}, u32[]{:S(2)}) collective-permute-start(bf16[64,32,32]{0,2,1:T(8,128)(2,1)S(1)} %get-tuple-element.341), channel_id=1, source_target_pairs={{0,992},{32,0},{64,32},{96,64},{128,96},{160,128},{192,160},{224,1... | collective-permute-start | bytes 393224 | tf_op jit(solution)/shard_map/while/body/eval_jaxpr/ppermute | solution.py:10
  396.0 6.6 %collective-permute-start = (bf16[64,32,32]{0,2,1:T(8,128)(2,1)S(1)}, bf16[64,32,32]{0,2,1:T(8,128)(2,1)S(1)}, u32[]{:S(2)}, u32[]{:S(2)}) collective-permute-start(bf16[64,32,32]{0,2,1:T(8,128)(2,1)S(1)} %get-tuple-element.341), channel_id=1, source_target_pairs={{0,992},{32,0},{64,32},{96,64},{128,96},{160,128},{192,160},{224,1... | collective-permute-start | bytes 393224 | tf_op jit(solution)/shard_map/while/body/eval_jaxpr/ppermute | solution.py:10
  410.2 6.6 %collective-permute-start = (bf16[64,32,32]{0,2,1:T(8,128)(2,1)S(1)}, bf16[64,32,32]{0,2,1:T(8,128)(2,1)S(1)}, u32[]{:S(2)}, u32[]{:S(2)}) collective-permute-start(bf16[64,32,32]{0,2,1:T(8,128)(2,1)S(1)} %get-tuple-element.341), channel_id=1, source_target_pairs={{0,992},{32,0},{64,32},{96,64},{128,96},{160,128},{192,160},{224,1... | collective-permute-start | bytes 393224 | tf_op jit(solution)/shard_map/while/body/eval_jaxpr/ppermute | solution.py:10
  424.4 6.6 %collective-permute-start = (bf16[64,32,32]{0,2,1:T(8,128)(2,1)S(1)}, bf16[64,32,32]{0,2,1:T(8,128)(2,1)S(1)}, u32[]{:S(2)}, u32[]{:S(2)}) collective-permute-start(bf16[64,32,32]{0,2,1:T(8,128)(2,1)S(1)} %get-tuple-element.341), channel_id=1, source_target_pairs={{0,992},{32,0},{64,32},{96,64},{128,96},{160,128},{192,160},{224,1... | collective-permute-start | bytes 393224 | tf_op jit(solution)/shard_map/while/body/eval_jaxpr/ppermute | solution.py:10
  438.6 6.6 %collective-permute-start = (bf16[64,32,32]{0,2,1:T(8,128)(2,1)S(1)}, bf16[64,32,32]{0,2,1:T(8,128)(2,1)S(1)}, u32[]{:S(2)}, u32[]{:S(2)}) collective-permute-start(bf16[64,32,32]{0,2,1:T(8,128)(2,1)S(1)} %get-tuple-element.341), channel_id=1, source_target_pairs={{0,992},{32,0},{64,32},{96,64},{128,96},{160,128},{192,160},{224,1... | collective-permute-start | bytes 393224 | tf_op jit(solution)/shard_map/while/body/eval_jaxpr/ppermute | solution.py:10
  452.8 6.6 %collective-permute-start = (bf16[64,32,32]{0,2,1:T(8,128)(2,1)S(1)}, bf16[64,32,32]{0,2,1:T(8,128)(2,1)S(1)}, u32[]{:S(2)}, u32[]{:S(2)}) collective-permute-start(bf16[64,32,32]{0,2,1:T(8,128)(2,1)S(1)} %get-tuple-element.341), channel_id=1, source_target_pairs={{0,992},{32,0},{64,32},{96,64},{128,96},{160,128},{192,160},{224,1... | collective-permute-start | bytes 393224 | tf_op jit(solution)/shard_map/while/body/eval_jaxpr/ppermute | solution.py:10
  467.0 6.6 %collective-permute-start = (bf16[64,32,32]{0,2,1:T(8,128)(2,1)S(1)}, bf16[64,32,32]{0,2,1:T(8,128)(2,1)S(1)}, u32[]{:S(2)}, u32[]{:S(2)}) collective-permute-start(bf16[64,32,32]{0,2,1:T(8,128)(2,1)S(1)} %get-tuple-element.341), channel_id=1, source_target_pairs={{0,992},{32,0},{64,32},{96,64},{128,96},{160,128},{192,160},{224,1... | collective-permute-start | bytes 393224 | tf_op jit(solution)/shard_map/while/body/eval_jaxpr/ppermute | solution.py:10
  509.5 6.6 %collective-permute-start = (bf16[64,32,32]{0,2,1:T(8,128)(2,1)S(1)}, bf16[64,32,32]{0,2,1:T(8,128)(2,1)S(1)}, u32[]{:S(2)}, u32[]{:S(2)}) collective-permute-start(bf16[64,32,32]{0,2,1:T(8,128)(2,1)S(1)} %get-tuple-element.341), channel_id=1, source_target_pairs={{0,992},{32,0},{64,32},{96,64},{128,96},{160,128},{192,160},{224,1... | collective-permute-start | bytes 393224 | tf_op jit(solution)/shard_map/while/body/eval_jaxpr/ppermute | solution.py:10
  524.3 21.7 %all_to_all.18 = bf16[4,2,8192]{2,1,0:T(2,128)(2,1)S(1)} all-to-all(bf16[4,2,8192]{2,1,0:T(2,128)(2,1)S(1)} %reshape.3), channel_id=1, replica_groups=mesh['row'=32,'col'=8,'layer'=4] {'layer'}, dimensions={0} | all-to-all | bytes 262144 | tf_op jit(solution)/shard_map/all_to_all | solution.py:67
  (209 shorter events, 191.7 us)
Async XLA Ops:
  6.5 79.5 %all-gather.2.cloned.1.call-start = ((), (), s32[]{:S(2)}) async-start(), calls=%async_computation.1 | async-start | bytes 4718592 | tf_op jit(solution)/shard_map/all_gather | solution.py:38
  87.4 13.0 %collective-permute-start = (bf16[64,32,32]{0,2,1:T(8,128)(2,1)S(1)}, bf16[64,32,32]{0,2,1:T(8,128)(2,1)S(1)}, u32[]{:S(2)}, u32[]{:S(2)}) collective-permute-start(bf16[64,32,32]{0,2,1:T(8,128)(2,1)S(1)} %get-tuple-element.341), channel_id=1, source_target_pairs={{0,992},{32,0},{64,32},{96,64},{128,96},{160,128},{192,160},{224,1... | collective-permute-start | bytes 393224 | tf_op jit(solution)/shard_map/while/body/eval_jaxpr/ppermute | solution.py:10
  126.7 11.6 %collective-permute-start = (bf16[64,32,32]{0,2,1:T(8,128)(2,1)S(1)}, bf16[64,32,32]{0,2,1:T(8,128)(2,1)S(1)}, u32[]{:S(2)}, u32[]{:S(2)}) collective-permute-start(bf16[64,32,32]{0,2,1:T(8,128)(2,1)S(1)} %get-tuple-element.341), channel_id=1, source_target_pairs={{0,992},{32,0},{64,32},{96,64},{128,96},{160,128},{192,160},{224,1... | collective-permute-start | bytes 393224 | tf_op jit(solution)/shard_map/while/body/eval_jaxpr/ppermute | solution.py:10
  155.1 11.6 %collective-permute-start = (bf16[64,32,32]{0,2,1:T(8,128)(2,1)S(1)}, bf16[64,32,32]{0,2,1:T(8,128)(2,1)S(1)}, u32[]{:S(2)}, u32[]{:S(2)}) collective-permute-start(bf16[64,32,32]{0,2,1:T(8,128)(2,1)S(1)} %get-tuple-element.341), channel_id=1, source_target_pairs={{0,992},{32,0},{64,32},{96,64},{128,96},{160,128},{192,160},{224,1... | collective-permute-start | bytes 393224 | tf_op jit(solution)/shard_map/while/body/eval_jaxpr/ppermute | solution.py:10
  211.7 11.6 %collective-permute-start = (bf16[64,32,32]{0,2,1:T(8,128)(2,1)S(1)}, bf16[64,32,32]{0,2,1:T(8,128)(2,1)S(1)}, u32[]{:S(2)}, u32[]{:S(2)}) collective-permute-start(bf16[64,32,32]{0,2,1:T(8,128)(2,1)S(1)} %get-tuple-element.341), channel_id=1, source_target_pairs={{0,992},{32,0},{64,32},{96,64},{128,96},{160,128},{192,160},{224,1... | collective-permute-start | bytes 393224 | tf_op jit(solution)/shard_map/while/body/eval_jaxpr/ppermute | solution.py:10
  225.9 11.6 %collective-permute-start = (bf16[64,32,32]{0,2,1:T(8,128)(2,1)S(1)}, bf16[64,32,32]{0,2,1:T(8,128)(2,1)S(1)}, u32[]{:S(2)}, u32[]{:S(2)}) collective-permute-start(bf16[64,32,32]{0,2,1:T(8,128)(2,1)S(1)} %get-tuple-element.341), channel_id=1, source_target_pairs={{0,992},{32,0},{64,32},{96,64},{128,96},{160,128},{192,160},{224,1... | collective-permute-start | bytes 393224 | tf_op jit(solution)/shard_map/while/body/eval_jaxpr/ppermute | solution.py:10
  240.1 11.6 %collective-permute-start = (bf16[64,32,32]{0,2,1:T(8,128)(2,1)S(1)}, bf16[64,32,32]{0,2,1:T(8,128)(2,1)S(1)}, u32[]{:S(2)}, u32[]{:S(2)}) collective-permute-start(bf16[64,32,32]{0,2,1:T(8,128)(2,1)S(1)} %get-tuple-element.341), channel_id=1, source_target_pairs={{0,992},{32,0},{64,32},{96,64},{128,96},{160,128},{192,160},{224,1... | collective-permute-start | bytes 393224 | tf_op jit(solution)/shard_map/while/body/eval_jaxpr/ppermute | solution.py:10
  254.2 11.6 %collective-permute-start = (bf16[64,32,32]{0,2,1:T(8,128)(2,1)S(1)}, bf16[64,32,32]{0,2,1:T(8,128)(2,1)S(1)}, u32[]{:S(2)}, u32[]{:S(2)}) collective-permute-start(bf16[64,32,32]{0,2,1:T(8,128)(2,1)S(1)} %get-tuple-element.341), channel_id=1, source_target_pairs={{0,992},{32,0},{64,32},{96,64},{128,96},{160,128},{192,160},{224,1... | collective-permute-start | bytes 393224 | tf_op jit(solution)/shard_map/while/body/eval_jaxpr/ppermute | solution.py:10
  268.4 11.6 %collective-permute-start = (bf16[64,32,32]{0,2,1:T(8,128)(2,1)S(1)}, bf16[64,32,32]{0,2,1:T(8,128)(2,1)S(1)}, u32[]{:S(2)}, u32[]{:S(2)}) collective-permute-start(bf16[64,32,32]{0,2,1:T(8,128)(2,1)S(1)} %get-tuple-element.341), channel_id=1, source_target_pairs={{0,992},{32,0},{64,32},{96,64},{128,96},{160,128},{192,160},{224,1... | collective-permute-start | bytes 393224 | tf_op jit(solution)/shard_map/while/body/eval_jaxpr/ppermute | solution.py:10
  282.6 11.6 %collective-permute-start = (bf16[64,32,32]{0,2,1:T(8,128)(2,1)S(1)}, bf16[64,32,32]{0,2,1:T(8,128)(2,1)S(1)}, u32[]{:S(2)}, u32[]{:S(2)}) collective-permute-start(bf16[64,32,32]{0,2,1:T(8,128)(2,1)S(1)} %get-tuple-element.341), channel_id=1, source_target_pairs={{0,992},{32,0},{64,32},{96,64},{128,96},{160,128},{192,160},{224,1... | collective-permute-start | bytes 393224 | tf_op jit(solution)/shard_map/while/body/eval_jaxpr/ppermute | solution.py:10
  296.8 11.6 %collective-permute-start = (bf16[64,32,32]{0,2,1:T(8,128)(2,1)S(1)}, bf16[64,32,32]{0,2,1:T(8,128)(2,1)S(1)}, u32[]{:S(2)}, u32[]{:S(2)}) collective-permute-start(bf16[64,32,32]{0,2,1:T(8,128)(2,1)S(1)} %get-tuple-element.341), channel_id=1, source_target_pairs={{0,992},{32,0},{64,32},{96,64},{128,96},{160,128},{192,160},{224,1... | collective-permute-start | bytes 393224 | tf_op jit(solution)/shard_map/while/body/eval_jaxpr/ppermute | solution.py:10
  311.0 11.6 %collective-permute-start = (bf16[64,32,32]{0,2,1:T(8,128)(2,1)S(1)}, bf16[64,32,32]{0,2,1:T(8,128)(2,1)S(1)}, u32[]{:S(2)}, u32[]{:S(2)}) collective-permute-start(bf16[64,32,32]{0,2,1:T(8,128)(2,1)S(1)} %get-tuple-element.341), channel_id=1, source_target_pairs={{0,992},{32,0},{64,32},{96,64},{128,96},{160,128},{192,160},{224,1... | collective-permute-start | bytes 393224 | tf_op jit(solution)/shard_map/while/body/eval_jaxpr/ppermute | solution.py:10
  325.1 11.6 %collective-permute-start = (bf16[64,32,32]{0,2,1:T(8,128)(2,1)S(1)}, bf16[64,32,32]{0,2,1:T(8,128)(2,1)S(1)}, u32[]{:S(2)}, u32[]{:S(2)}) collective-permute-start(bf16[64,32,32]{0,2,1:T(8,128)(2,1)S(1)} %get-tuple-element.341), channel_id=1, source_target_pairs={{0,992},{32,0},{64,32},{96,64},{128,96},{160,128},{192,160},{224,1... | collective-permute-start | bytes 393224 | tf_op jit(solution)/shard_map/while/body/eval_jaxpr/ppermute | solution.py:10
  339.3 11.6 %collective-permute-start = (bf16[64,32,32]{0,2,1:T(8,128)(2,1)S(1)}, bf16[64,32,32]{0,2,1:T(8,128)(2,1)S(1)}, u32[]{:S(2)}, u32[]{:S(2)}) collective-permute-start(bf16[64,32,32]{0,2,1:T(8,128)(2,1)S(1)} %get-tuple-element.341), channel_id=1, source_target_pairs={{0,992},{32,0},{64,32},{96,64},{128,96},{160,128},{192,160},{224,1... | collective-permute-start | bytes 393224 | tf_op jit(solution)/shard_map/while/body/eval_jaxpr/ppermute | solution.py:10
  353.5 11.6 %collective-permute-start = (bf16[64,32,32]{0,2,1:T(8,128)(2,1)S(1)}, bf16[64,32,32]{0,2,1:T(8,128)(2,1)S(1)}, u32[]{:S(2)}, u32[]{:S(2)}) collective-permute-start(bf16[64,32,32]{0,2,1:T(8,128)(2,1)S(1)} %get-tuple-element.341), channel_id=1, source_target_pairs={{0,992},{32,0},{64,32},{96,64},{128,96},{160,128},{192,160},{224,1... | collective-permute-start | bytes 393224 | tf_op jit(solution)/shard_map/while/body/eval_jaxpr/ppermute | solution.py:10
  367.7 11.6 %collective-permute-start = (bf16[64,32,32]{0,2,1:T(8,128)(2,1)S(1)}, bf16[64,32,32]{0,2,1:T(8,128)(2,1)S(1)}, u32[]{:S(2)}, u32[]{:S(2)}) collective-permute-start(bf16[64,32,32]{0,2,1:T(8,128)(2,1)S(1)} %get-tuple-element.341), channel_id=1, source_target_pairs={{0,992},{32,0},{64,32},{96,64},{128,96},{160,128},{192,160},{224,1... | collective-permute-start | bytes 393224 | tf_op jit(solution)/shard_map/while/body/eval_jaxpr/ppermute | solution.py:10
  381.9 11.6 %collective-permute-start = (bf16[64,32,32]{0,2,1:T(8,128)(2,1)S(1)}, bf16[64,32,32]{0,2,1:T(8,128)(2,1)S(1)}, u32[]{:S(2)}, u32[]{:S(2)}) collective-permute-start(bf16[64,32,32]{0,2,1:T(8,128)(2,1)S(1)} %get-tuple-element.341), channel_id=1, source_target_pairs={{0,992},{32,0},{64,32},{96,64},{128,96},{160,128},{192,160},{224,1... | collective-permute-start | bytes 393224 | tf_op jit(solution)/shard_map/while/body/eval_jaxpr/ppermute | solution.py:10
  396.0 11.6 %collective-permute-start = (bf16[64,32,32]{0,2,1:T(8,128)(2,1)S(1)}, bf16[64,32,32]{0,2,1:T(8,128)(2,1)S(1)}, u32[]{:S(2)}, u32[]{:S(2)}) collective-permute-start(bf16[64,32,32]{0,2,1:T(8,128)(2,1)S(1)} %get-tuple-element.341), channel_id=1, source_target_pairs={{0,992},{32,0},{64,32},{96,64},{128,96},{160,128},{192,160},{224,1... | collective-permute-start | bytes 393224 | tf_op jit(solution)/shard_map/while/body/eval_jaxpr/ppermute | solution.py:10
  410.2 11.6 %collective-permute-start = (bf16[64,32,32]{0,2,1:T(8,128)(2,1)S(1)}, bf16[64,32,32]{0,2,1:T(8,128)(2,1)S(1)}, u32[]{:S(2)}, u32[]{:S(2)}) collective-permute-start(bf16[64,32,32]{0,2,1:T(8,128)(2,1)S(1)} %get-tuple-element.341), channel_id=1, source_target_pairs={{0,992},{32,0},{64,32},{96,64},{128,96},{160,128},{192,160},{224,1... | collective-permute-start | bytes 393224 | tf_op jit(solution)/shard_map/while/body/eval_jaxpr/ppermute | solution.py:10
  424.4 11.6 %collective-permute-start = (bf16[64,32,32]{0,2,1:T(8,128)(2,1)S(1)}, bf16[64,32,32]{0,2,1:T(8,128)(2,1)S(1)}, u32[]{:S(2)}, u32[]{:S(2)}) collective-permute-start(bf16[64,32,32]{0,2,1:T(8,128)(2,1)S(1)} %get-tuple-element.341), channel_id=1, source_target_pairs={{0,992},{32,0},{64,32},{96,64},{128,96},{160,128},{192,160},{224,1... | collective-permute-start | bytes 393224 | tf_op jit(solution)/shard_map/while/body/eval_jaxpr/ppermute | solution.py:10
  438.6 11.6 %collective-permute-start = (bf16[64,32,32]{0,2,1:T(8,128)(2,1)S(1)}, bf16[64,32,32]{0,2,1:T(8,128)(2,1)S(1)}, u32[]{:S(2)}, u32[]{:S(2)}) collective-permute-start(bf16[64,32,32]{0,2,1:T(8,128)(2,1)S(1)} %get-tuple-element.341), channel_id=1, source_target_pairs={{0,992},{32,0},{64,32},{96,64},{128,96},{160,128},{192,160},{224,1... | collective-permute-start | bytes 393224 | tf_op jit(solution)/shard_map/while/body/eval_jaxpr/ppermute | solution.py:10
  452.8 11.6 %collective-permute-start = (bf16[64,32,32]{0,2,1:T(8,128)(2,1)S(1)}, bf16[64,32,32]{0,2,1:T(8,128)(2,1)S(1)}, u32[]{:S(2)}, u32[]{:S(2)}) collective-permute-start(bf16[64,32,32]{0,2,1:T(8,128)(2,1)S(1)} %get-tuple-element.341), channel_id=1, source_target_pairs={{0,992},{32,0},{64,32},{96,64},{128,96},{160,128},{192,160},{224,1... | collective-permute-start | bytes 393224 | tf_op jit(solution)/shard_map/while/body/eval_jaxpr/ppermute | solution.py:10
  467.0 11.6 %collective-permute-start = (bf16[64,32,32]{0,2,1:T(8,128)(2,1)S(1)}, bf16[64,32,32]{0,2,1:T(8,128)(2,1)S(1)}, u32[]{:S(2)}, u32[]{:S(2)}) collective-permute-start(bf16[64,32,32]{0,2,1:T(8,128)(2,1)S(1)} %get-tuple-element.341), channel_id=1, source_target_pairs={{0,992},{32,0},{64,32},{96,64},{128,96},{160,128},{192,160},{224,1... | collective-permute-start | bytes 393224 | tf_op jit(solution)/shard_map/while/body/eval_jaxpr/ppermute | solution.py:10
  509.5 11.6 %collective-permute-start = (bf16[64,32,32]{0,2,1:T(8,128)(2,1)S(1)}, bf16[64,32,32]{0,2,1:T(8,128)(2,1)S(1)}, u32[]{:S(2)}, u32[]{:S(2)}) collective-permute-start(bf16[64,32,32]{0,2,1:T(8,128)(2,1)S(1)} %get-tuple-element.341), channel_id=1, source_target_pairs={{0,992},{32,0},{64,32},{96,64},{128,96},{160,128},{192,160},{224,1... | collective-permute-start | bytes 393224 | tf_op jit(solution)/shard_map/while/body/eval_jaxpr/ppermute | solution.py:10
  (8 other events, 87.9 us)
Sparse Core Ops, SparseCore 0:
  9.9 76.0 all-gather.1
where the time goes:
time: 564 us; the launch traced here: 555 us
  starting transfers between devices  201 us (36%)
  loops' own time  113 us (20%)
  local copies, waits for them, and re-layouts  73.4 us (13%)
  waiting for transfers between devices  72.3 us (13%)
  matrix products  46.4 us (8%)
  blocking collectives  21.7 us (4%)
  between operations  17 us (3%)
  other arithmetic  9.87 us (2%)
    ppermute x31, starting transfers between devices, passed_along(): return lax.ppermute(value, axis, pairs)  201 us
    another operation x1, loops' own time, local(): totals, current = lax.fori_loop(1, row_count, turn_body, (totals, current))  113 us
    all_gather x1, waiting for transfers between devices, local(): full_rows = lax.all_gather(x_blocks, 'col', axis=2, tiled=True)  70.8 us
    dot_general x32, matrix products, add_products(): jnp.einsum('pij,pjk->pik', left_blocks, right_blocks, preferred_element_t...  46.4 us
    dynamic_slice x31, local copies, waits for them, and re-layouts, accumulate(): shifts[source_range, own_target]  42.6 us
    while x62, local copies, waits for them, and re-layouts  24.6 us
    all_to_all x1, blocking collectives, local(): lax.all_to_all(squared, 'layer', split_axis=0, concat_axis=2, tiled=True)  21.7 us
  transfers between devices with their start and end apart: 32, of which 2 were waited for; matrix products, arithmetic and copies ran while one was open for 8% of the time, Pallas kernels for 0%

commit v1 on v0

v1 whole, which is shorter than its diff:
```python
import jax
import jax.numpy as jnp
from jax import lax
from jax.experimental import pallas as pl
from jax.experimental.pallas import tpu as pltpu
from jax.sharding import PartitionSpec as P

AXES = ("row", "col", "layer")
NX, NZ, NY, NL = 4, 4, 8, 4
BS, RANGE, SPAN = 32, 64, 16
LANES = 128
NEAR = 8
STEPS = (0, 1, -1, 2)


def device_pairs(move):
    def index(x, z, core, y):
        return ((x * NZ + z % NZ) * 2 + core) * NY * NL + y * NL + z // NZ

    pairs = []
    for x in range(NX):
        for z in range(NZ * NL):
            for core in range(2):
                for y in range(NY):
                    tx, tz, tcore, ty = move(x, z, core, y)
                    pairs.append((index(x, z, core, y), index(tx % NX, tz % (NZ * NL), tcore, ty % NY)))
    return pairs


def sent(value, move):
    return lax.ppermute(value, AXES, device_pairs(move))


def other_core(x, z, core, y):
    return x, z, 1 - core, y


def along_x(step):
    return lambda x, z, core, y: (x + step, z, core, y)


def along_z(step):
    return lambda x, z, core, y: (x, z + step, core, y)


def two_along_z(x, z, core, y):
    return x, (z + 2 if core == 0 else z - 2), core, y


def target_row(row, step):
    return (((row >> 3) - step) & (NX - 1)) * NEAR + (row & (NEAR - 1))


def mask_kernel(place_ref, shifts_ref, masks_ref):
    row = place_ref[0]
    col = place_ref[1]
    near = (row >> 3) * NEAR
    lane_block = lax.broadcasted_iota(jnp.int32, (BS, LANES), 1) // BS

    def mask_step(j, carry):
        source = near + j
        for t, step in enumerate(STEPS):
            target = target_row(row, step)
            value = jnp.zeros((BS, LANES), jnp.float32)
            for b in range(4):
                own_range = col * 4 + b
                total = shifts_ref[target, source] + shifts_ref[source, own_range]
                total = (total - shifts_ref[target, own_range]) & (RANGE - 1)
                value = jnp.where(lane_block == b, jnp.where(total == 0, 1.0, 0.0), value)
            masks_ref[t, j] = value.astype(jnp.bfloat16)
        return carry

    lax.fori_loop(0, NEAR, mask_step, 0)


def product_kernel(
    place_ref, shifts_ref, masks, left_0, left_1, left_2, left_3,
    own, before, after, across, twin, twin_others,
    out_0, out_1, out_2, out_3, right, sems,
):
    row = place_ref[0]
    layer = place_ref[2]
    core = row & 1
    zl = (row >> 1) & 3
    near = (row >> 3) * NEAR

    pieces = [(own, 0, core), (before, -1, core), (after, 1, core), (across, 2, core), (twin, 0, 1 - core)]
    pieces += [(twin_others.at[pl.ds(n * RANGE, RANGE)], step, 1 - core) for n, step in enumerate((-1, 1, 2))]
    copies = []
    for n, (piece, step, parity) in enumerate(pieces):
        slot = ((zl + step) & (NZ - 1)) * 2 + parity
        copies.append(pltpu.make_async_copy(piece, right.at[slot], sems.at[n]))
    for copy in copies:
        copy.start()
    for copy in copies:
        copy.wait()

    lefts = [left_0, left_1, left_2, left_3]
    outs = [out_0, out_1, out_2, out_3]

    def position_step(p, carry):
        place = layer * SPAN + p
        for t, step in enumerate(STEPS):
            target = target_row(row, step)
            lhs = jnp.concatenate([lefts[t][0, p], lefts[t][1, p]], axis=1)
            rows = []
            for j in range(NEAR):
                q = (place + shifts_ref[target, near + j]) & (RANGE - 1)
                rows.append(right[j, q] * masks[t, j])
            rhs = jnp.concatenate(rows, axis=0)
            outs[t][p] = jnp.dot(lhs, rhs, preferred_element_type=jnp.float32)
        return carry

    lax.fori_loop(0, SPAN, position_step, 0)


def local(x_blocks, shifts):
    row = lax.axis_index("row")
    col = lax.axis_index("col")
    layer = lax.axis_index("layer")
    x = row // NEAR
    place = jnp.stack([row, col, layer]).astype(jnp.int32)
    smem = pl.BlockSpec(memory_space=pltpu.SMEM)
    vmem = pl.BlockSpec(memory_space=pltpu.VMEM)
    anywhere = pl.BlockSpec(memory_space=pl.ANY)

    before = sent(x_blocks, along_z(1))
    after = sent(x_blocks, along_z(-1))
    across = sent(x_blocks, two_along_z)
    twin = sent(x_blocks, other_core)

    mine = lax.dynamic_slice_in_dim(x_blocks, layer * SPAN, SPAN, 0)
    gathered = lax.all_to_all(jnp.broadcast_to(mine[None], (NY, SPAN, BS, LANES)), "col", 0, 0)

    def columns_of(step):
        return lax.dynamic_slice_in_dim(gathered, ((x + step) % NX) * 2, 2, 0)

    lefts = [columns_of(0)] + [sent(columns_of(step), along_x(step)) for step in STEPS[1:]]
    twin_others = sent(jnp.concatenate([before, after, across], axis=0), other_core)

    masks = pl.pallas_call(
        mask_kernel,
        out_shape=jax.ShapeDtypeStruct((len(STEPS), NEAR, BS, LANES), jnp.bfloat16),
        in_specs=[smem, smem],
        out_specs=vmem,
        name="masks",
    )(place, shifts)
    part = jax.ShapeDtypeStruct((SPAN, BS, LANES), jnp.float32)
    parts = pl.pallas_call(
        product_kernel,
        out_shape=[part] * 4,
        in_specs=[smem, smem] + [vmem] * 5 + [anywhere] * 6,
        out_specs=[vmem] * 4,
        scratch_shapes=[
            pltpu.VMEM((NEAR, RANGE, BS, LANES), jnp.bfloat16),
            pltpu.SemaphoreType.DMA((NEAR,)),
        ],
        compiler_params=pltpu.CompilerParams(vmem_limit_bytes=20 * 1024 * 1024),
        name="range_products",
    )(place, shifts, masks, *lefts, x_blocks, before, after, across, twin, twin_others)
    total = parts[0]
    for part, step in zip(parts[1:], STEPS[1:]):
        total = total + sent(part, along_x(-step))
    return total.astype(jnp.bfloat16)


def solution(mesh):
    return jax.shard_map(
        local,
        mesh=mesh,
        in_specs=(P("row", None, "col"), P()),
        out_specs=P(("row", "layer"), None, "col"),
        check_vma=False,
    )
```

time: 564 us -> 109 us (0.19); the launches traced: 555 us -> 108 us
  starting transfers between devices: 201 us -> 56.3 us
  loops' own time: 113 us -> 0 us
  local copies, waits for them, and re-layouts: 73.4 us -> 5.8 us
  matrix products: 46.4 us -> 0 us
  waiting for transfers between devices: 72.3 us -> 34.4 us
  blocking collectives: 21.7 us -> 0 us
  between operations: 17 us -> 0.23 us
  Pallas kernels: 0 us -> 8.24 us
  other arithmetic: 9.87 us -> 2.74 us
    ppermute x31 -> x11, starting transfers between devices: 201 us -> 49.4 us  [sent(): return lax.ppermute(value, AXES, device_pairs(move))]
    another operation x1 -> x0, loops' own time: 113 us -> none  [local(): totals, current = lax.fori_loop(1, row_count, turn_body, (totals, current))]
    all_gather x1 -> x0, waiting for transfers between devices: 70.8 us -> none  [local(): full_rows = lax.all_gather(x_blocks, 'col', axis=2, tiled=True)]
    dot_general x32 -> x0, matrix products: 46.4 us -> none  [add_products(): jnp.einsum('pij,pjk->pik', left_blocks, right_blocks, preferred_element_t...]
    dynamic_slice x33 -> x2, local copies, waits for them, and re-layouts: 45.3 us -> 3.03 us  [the longest x1 2.11 us: columns_of(): return lax.dynamic_slice_in_dim(gathered, (x + step) % NX * 2, 2, 0)]
    while x62 -> x0, local copies, waits for them, and re-layouts: 24.6 us -> none
    all_to_all x1 -> x0, blocking collectives: 21.7 us -> none  [local(): lax.all_to_all(squared, 'layer', split_axis=0, concat_axis=2, tiled=True)]
    ppermute x31 -> x11, waiting for transfers between devices: 0.82 us -> 21.9 us  [sent(): return lax.ppermute(value, AXES, device_pairs(move))]
  transfers between devices with their start and end apart: 32 -> 12, of which waited for: 2 -> 6; matrix products, arithmetic and copies ran while one was open for 8% -> 6% of each run, Pallas kernels for 0% -> 2%
where the time goes in v1:
time: 109 us; the launch traced here: 108 us
  starting transfers between devices  56.3 us (52%)
  waiting for transfers between devices  34.4 us (32%)
  Pallas kernels  8.24 us (8%)
  local copies, waits for them, and re-layouts  5.8 us (5%)
  other arithmetic  2.74 us (3%)
    ppermute x11, starting transfers between devices, sent(): return lax.ppermute(value, AXES, device_pairs(move))  49.4 us
    ppermute x11, waiting for transfers between devices, sent(): return lax.ppermute(value, AXES, device_pairs(move))  21.9 us
    all_to_all x1, waiting for transfers between devices, local(): lax.all_to_all(jnp.broadcast_to(mine[None], (NY, SPAN, BS, LANES)), 'col'...  12.5 us
    all_to_all x1, starting transfers between devices, local(): lax.all_to_all(jnp.broadcast_to(mine[None], (NY, SPAN, BS, LANES)), 'col'...  6.82 us
    pallas_call x1, Pallas kernels, local(): pl.pallas_call(product_kernel, out_shape=[part] * 4, in_specs=[smem, smem...  5.97 us
    pallas_call x1, Pallas kernels, local(): pl.pallas_call(mask_kernel, out_shape=jax.ShapeDtypeStruct((len(STEPS), N...  2.27 us
  transfers between devices with their start and end apart: 12, of which 6 were waited for; matrix products, arithmetic and copies ran while one was open for 6% of the time, Pallas kernels for 2%

profile of v1, /device:TPU:1, one launch (start us, length us, event | category | flops | bytes accessed | tf_op | source)
XLA Modules:
  0.0 107.7 jit_solution(822922466555759214)
XLA Ops:
  0.0 4.8 %collective-permute-start.3 = (bf16[64,32,128]{2,1,0:T(8,128)(2,1)}, bf16[64,32,128]{2,1,0:T(8,128)(2,1)S(1)}, u32[]{:S(2)}, u32[]{:S(2)}) collective-permute-start(bf16[64,32,128]{2,1,0:T(8,128)(2,1)} %own.1), channel_id=1, source_target_pairs={{0,64},{4,68},{8,72},{12,76},{16,80},{20,84},{24,88},{28,92},{32,9... | collective-permute-start | bytes 1572872 | tf_op jit(solution)/shard_map/ppermute | solution.py:31
  4.8 15.9 %collective-permute-start.4 = (bf16[64,32,128]{2,1,0:T(8,128)(2,1)}, bf16[64,32,128]{2,1,0:T(8,128)(2,1)S(1)}, u32[]{:S(2)}, u32[]{:S(2)}) collective-permute-start(bf16[64,32,128]{2,1,0:T(8,128)(2,1)} %own.1), channel_id=1, source_target_pairs={{0,195},{4,199},{8,203},{12,207},{16,211},{20,215},{24,219},{28,22... | collective-permute-start | bytes 1572872 | tf_op jit(solution)/shard_map/ppermute | solution.py:31
  20.7 3.4 %collective-permute-start.5 = (bf16[64,32,128]{2,1,0:T(8,128)(2,1)}, bf16[64,32,128]{2,1,0:T(8,128)(2,1)S(1)}, u32[]{:S(2)}, u32[]{:S(2)}) collective-permute-start(bf16[64,32,128]{2,1,0:T(8,128)(2,1)} %own.1), channel_id=1, source_target_pairs={{0,128},{4,132},{8,136},{12,140},{16,144},{20,148},{24,152},{28,15... | collective-permute-start | bytes 1572872 | tf_op jit(solution)/shard_map/ppermute | solution.py:31
  25.0 1.1 %broadcast_in_dim.2 = bf16[8,16,32,128]{3,2,1,0:T(8,128)(2,1)} broadcast(bf16[16,32,128]{2,1,0:T(8,128)(2,1)S(1)} %constant_dynamic-slice_fusion.4), dimensions={1,2,3} | broadcast | bytes 1179648 | tf_op jit(solution)/shard_map/broadcast_in_dim | solution.py:133
  26.1 6.8 %all-to-all-start = ((bf16[8,16,32,128]{3,2,1,0:T(8,128)(2,1)}), bf16[8,16,32,128]{3,2,1,0:T(8,128)(2,1)}, u32[]{:S(2)}, u32[]{:S(2)}) async-start(bf16[8,16,32,128]{3,2,1,0:T(8,128)(2,1)} %broadcast_in_dim.2), calls=%async_computation | async-start | bytes 2097152 | tf_op jit(solution)/shard_map/all_to_all | solution.py:133
  33.0 2.9 %collective-permute-done.4.after = bf16[64,32,128]{2,1,0:T(8,128)(2,1)S(1)} collective-permute-done((bf16[64,32,128]{2,1,0:T(8,128)(2,1)}, bf16[64,32,128]{2,1,0:T(8,128)(2,1)S(1)}, u32[]{:S(2)}, u32[]{:S(2)}) %collective-permute-start.4) | collective-permute-done | bytes 524320 | tf_op jit(solution)/shard_map/ppermute | solution.py:31
  35.9 8.1 %collective-permute-done.5.across = bf16[64,32,128]{2,1,0:T(8,128)(2,1)S(1)} collective-permute-done((bf16[64,32,128]{2,1,0:T(8,128)(2,1)}, bf16[64,32,128]{2,1,0:T(8,128)(2,1)S(1)}, u32[]{:S(2)}, u32[]{:S(2)}) %collective-permute-start.5) | collective-permute-done | bytes 524320 | tf_op jit(solution)/shard_map/ppermute | solution.py:31
  44.0 1.3 %pad_maximum_fusion = bf16[192,32,128]{2,1,0:T(8,128)(2,1)} fusion(bf16[64,32,128]{2,1,0:T(8,128)(2,1)S(1)} %collective-permute-done.5.across, bf16[64,32,128]{2,1,0:T(8,128)(2,1)S(1)} %collective-permute-done.4.after, bf16[64,32,128]{2,1,0:T(8,128)(2,1)S(1)} %collective-permute-done.3.before), kind=kLoop, calls=%fused_computation | loop fusion | flops 1572864 | bytes 3145728 | tf_op jit(solution)/shard_map/concatenate | solution.py:139
  45.3 2.0 %collective-permute-start.7 = (bf16[192,32,128]{2,1,0:T(8,128)(2,1)}, bf16[192,32,128]{2,1,0:T(8,128)(2,1)S(1)}, u32[]{:S(2)}, u32[]{:S(2)}) collective-permute-start(bf16[192,32,128]{2,1,0:T(8,128)(2,1)} %pad_maximum_fusion), channel_id=1, source_target_pairs={{0,32},{4,36},{8,40},{12,44},{16,48},{20,52},{24,56},{28,60},{32,0... | collective-permute-start | bytes 4718600 | tf_op jit(solution)/shard_map/ppermute | solution.py:31
  47.4 2.4 %collective-permute-start.6 = (bf16[64,32,128]{2,1,0:T(8,128)(2,1)}, bf16[64,32,128]{2,1,0:T(8,128)(2,1)}, u32[]{:S(2)}, u32[]{:S(2)}) collective-permute-start(bf16[64,32,128]{2,1,0:T(8,128)(2,1)} %own.1), channel_id=1, source_target_pairs={{0,32},{4,36},{8,40},{12,44},{16,48},{20,52},{24,56},{28,60},{32,0... | collective-permute-start | bytes 1572872 | tf_op jit(solution)/shard_map/ppermute | solution.py:31
  49.9 12.5 %all-to-all-done = bf16[8,16,32,128]{3,2,1,0:T(8,128)(2,1)} async-done(((bf16[8,16,32,128]{3,2,1,0:T(8,128)(2,1)}), bf16[8,16,32,128]{3,2,1,0:T(8,128)(2,1)}, u32[]{:S(2)}, u32[]{:S(2)}) %all-to-all-start) | async-done | bytes 1048608 | tf_op jit(solution)/shard_map/all_to_all | solution.py:133
  62.4 2.1 %constant_dynamic-slice_fusion = (bf16[2,16,32,128]{3,2,1,0:T(8,128)(2,1)}, bf16[2,16,32,128]{3,2,1,0:T(8,128)(2,1)}, bf16[2,16,32,128]{3,2,1,0:T(8,128)(2,1)}, bf16[2,16,32,128]{3,2,1,0:T(8,128)(2,1)S(1)}) fusion(bf16[8,16,32,128]{3,2,1,0:T(8,128)(2,1)} %all-to-all-done, s32[]{:T(128)S(6)} %select_n.47, s32[]{:T(128)S(6)} %select_n.45, s32[]{:T(128)S(6)} %select_n.43, ...), kind=kLoop, calls=%fused_computation.2 | loop fusion | bytes 2097168 | tf_op jit(solution)/shard_map/dynamic_slice | solution.py:136
  64.5 3.1 %collective-permute-start = (bf16[2,16,32,128]{3,2,1,0:T(8,128)(2,1)}, bf16[2,16,32,128]{3,2,1,0:T(8,128)(2,1)}, u32[]{:S(2)}, u32[]{:S(2)}) collective-permute-start(bf16[2,16,32,128]{3,2,1,0:T(8,128)(2,1)} %get-tuple-element.15), channel_id=1, source_target_pairs={{0,256},{4,260},{8,264},{12,268},{16,272},{20,276},{24,280},{28,28... | collective-permute-start | bytes 786440 | tf_op jit(solution)/shard_map/ppermute | solution.py:31
  67.6 3.4 %collective-permute-start.1 = (bf16[2,16,32,128]{3,2,1,0:T(8,128)(2,1)}, bf16[2,16,32,128]{3,2,1,0:T(8,128)(2,1)}, u32[]{:S(2)}, u32[]{:S(2)}) collective-permute-start(bf16[2,16,32,128]{3,2,1,0:T(8,128)(2,1)} %get-tuple-element.14), channel_id=1, source_target_pairs={{0,768},{4,772},{8,776},{12,780},{16,784},{20,788},{24,792},{28,79... | collective-permute-start | bytes 786440 | tf_op jit(solution)/shard_map/ppermute | solution.py:31
  71.0 3.4 %collective-permute-start.2 = (bf16[2,16,32,128]{3,2,1,0:T(8,128)(2,1)}, bf16[2,16,32,128]{3,2,1,0:T(8,128)(2,1)}, u32[]{:S(2)}, u32[]{:S(2)}) collective-permute-start(bf16[2,16,32,128]{3,2,1,0:T(8,128)(2,1)} %get-tuple-element.13), channel_id=1, source_target_pairs={{0,512},{4,516},{8,520},{12,524},{16,528},{20,532},{24,536},{28,54... | collective-permute-start | bytes 786440 | tf_op jit(solution)/shard_map/ppermute | solution.py:31
  75.1 2.3 %masks.1 = bf16[4,8,32,128]{3,2,1,0:T(8,128)(2,1)} custom-call(s32[3]{0:T(128)} %pad_add_fusion.place_ref, s32[32,32]{1,0:T(8,128)} %shifts_ref.3), custom_call_target="tpu_custom_call" | custom-call | tf_op jit(solution)/shard_map/masks/pallas_call | solution.py:141
  77.4 4.1 %collective-permute-done.2.left_3 = bf16[2,16,32,128]{3,2,1,0:T(8,128)(2,1)} collective-permute-done((bf16[2,16,32,128]{3,2,1,0:T(8,128)(2,1)}, bf16[2,16,32,128]{3,2,1,0:T(8,128)(2,1)}, u32[]{:S(2)}, u32[]{:S(2)}) %collective-permute-start.2) | collective-permute-done | bytes 262176 | tf_op jit(solution)/shard_map/ppermute | solution.py:31
  81.5 0.9 copy-done
  83.1 6.0 %range_products.1 = (f32[16,32,128]{2,1,0:T(8,128)S(1)}, f32[16,32,128]{2,1,0:T(8,128)S(1)}, f32[16,32,128]{2,1,0:T(8,128)S(1)}, f32[16,32,128]{2,1,0:T(8,128)S(1)}) custom-call(s32[3]{0:T(128)S(1)} %copy-done.2, s32[32,32]{1,0:T(8,128)S(1)} %copy-done.1, bf16[4,8,32,128]{3,2,1,0:T(8,128)(2,1)S(1)} %copy-done, ...), custom_call_target="tpu_custom_call" | custom-call | tf_op jit(solution)/shard_map/range_products/pallas_call | solution.py:149
  89.1 3.4 %collective-permute-start.10 = (f32[16,32,128]{2,1,0:T(8,128)S(1)}, f32[16,32,128]{2,1,0:T(8,128)S(1)}, u32[]{:S(2)}, u32[]{:S(2)}) collective-permute-start(f32[16,32,128]{2,1,0:T(8,128)S(1)} %get-tuple-element.12), channel_id=1, source_target_pairs={{0,512},{4,516},{8,520},{12,524},{16,528},{20,532},{24,536},{28,54... | collective-permute-start | bytes 786440 | tf_op jit(solution)/shard_map/ppermute | solution.py:31
  92.6 5.7 %collective-permute-start.8 = (f32[16,32,128]{2,1,0:T(8,128)S(1)}, f32[16,32,128]{2,1,0:T(8,128)S(1)}, u32[]{:S(2)}, u32[]{:S(2)}) collective-permute-start(f32[16,32,128]{2,1,0:T(8,128)S(1)} %get-tuple-element.10), channel_id=1, source_target_pairs={{0,768},{4,772},{8,776},{12,780},{16,784},{20,788},{24,792},{28,79... | collective-permute-start | bytes 786440 | tf_op jit(solution)/shard_map/ppermute | solution.py:31
  98.2 1.9 %collective-permute-start.9 = (f32[16,32,128]{2,1,0:T(8,128)S(1)}, f32[16,32,128]{2,1,0:T(8,128)S(1)}, u32[]{:S(2)}, u32[]{:S(2)}) collective-permute-start(f32[16,32,128]{2,1,0:T(8,128)S(1)} %get-tuple-element.11), channel_id=1, source_target_pairs={{0,256},{4,260},{8,264},{12,268},{16,272},{20,276},{24,280},{28,28... | collective-permute-start | bytes 786440 | tf_op jit(solution)/shard_map/ppermute | solution.py:31
  100.2 5.2 %collective-permute-done.8 = f32[16,32,128]{2,1,0:T(8,128)S(1)} collective-permute-done((f32[16,32,128]{2,1,0:T(8,128)S(1)}, f32[16,32,128]{2,1,0:T(8,128)S(1)}, u32[]{:S(2)}, u32[]{:S(2)}) %collective-permute-start.8) | collective-permute-done | bytes 262176 | tf_op jit(solution)/shard_map/ppermute | solution.py:31
  105.4 1.6 %collective-permute-done.9 = f32[16,32,128]{2,1,0:T(8,128)S(1)} collective-permute-done((f32[16,32,128]{2,1,0:T(8,128)S(1)}, f32[16,32,128]{2,1,0:T(8,128)S(1)}, u32[]{:S(2)}, u32[]{:S(2)}) %collective-permute-start.9) | collective-permute-done | bytes 262176 | tf_op jit(solution)/shard_map/ppermute | solution.py:31
  (14 shorter events, 3.0 us)
Async XLA Ops:
  0.0 33.0 %collective-permute-start.3 = (bf16[64,32,128]{2,1,0:T(8,128)(2,1)}, bf16[64,32,128]{2,1,0:T(8,128)(2,1)S(1)}, u32[]{:S(2)}, u32[]{:S(2)}) collective-permute-start(bf16[64,32,128]{2,1,0:T(8,128)(2,1)} %own.1), channel_id=1, source_target_pairs={{0,64},{4,68},{8,72},{12,76},{16,80},{20,84},{24,88},{28,92},{32,9... | collective-permute-start | bytes 1572872 | tf_op jit(solution)/shard_map/ppermute | solution.py:31
  4.8 31.1 %collective-permute-start.4 = (bf16[64,32,128]{2,1,0:T(8,128)(2,1)}, bf16[64,32,128]{2,1,0:T(8,128)(2,1)S(1)}, u32[]{:S(2)}, u32[]{:S(2)}) collective-permute-start(bf16[64,32,128]{2,1,0:T(8,128)(2,1)} %own.1), channel_id=1, source_target_pairs={{0,195},{4,199},{8,203},{12,207},{16,211},{20,215},{24,219},{28,22... | collective-permute-start | bytes 1572872 | tf_op jit(solution)/shard_map/ppermute | solution.py:31
  20.7 23.3 %collective-permute-start.5 = (bf16[64,32,128]{2,1,0:T(8,128)(2,1)}, bf16[64,32,128]{2,1,0:T(8,128)(2,1)S(1)}, u32[]{:S(2)}, u32[]{:S(2)}) collective-permute-start(bf16[64,32,128]{2,1,0:T(8,128)(2,1)} %own.1), channel_id=1, source_target_pairs={{0,128},{4,132},{8,136},{12,140},{16,144},{20,148},{24,152},{28,15... | collective-permute-start | bytes 1572872 | tf_op jit(solution)/shard_map/ppermute | solution.py:31
  26.1 36.3 %all-to-all-start = ((bf16[8,16,32,128]{3,2,1,0:T(8,128)(2,1)}), bf16[8,16,32,128]{3,2,1,0:T(8,128)(2,1)}, u32[]{:S(2)}, u32[]{:S(2)}) async-start(bf16[8,16,32,128]{3,2,1,0:T(8,128)(2,1)} %broadcast_in_dim.2), calls=%async_computation | async-start | bytes 2097152 | tf_op jit(solution)/shard_map/all_to_all | solution.py:133
  45.3 36.2 %copy-start.1 = (s32[32,32]{1,0:T(8,128)S(1)}, s32[32,32]{1,0:T(8,128)}, u32[]{:S(2)}) copy-start(s32[32,32]{1,0:T(8,128)} %shifts_ref.3) | copy-start | bytes 12292
  45.3 36.2 %collective-permute-start.7 = (bf16[192,32,128]{2,1,0:T(8,128)(2,1)}, bf16[192,32,128]{2,1,0:T(8,128)(2,1)S(1)}, u32[]{:S(2)}, u32[]{:S(2)}) collective-permute-start(bf16[192,32,128]{2,1,0:T(8,128)(2,1)} %pad_maximum_fusion), channel_id=1, source_target_pairs={{0,32},{4,36},{8,40},{12,44},{16,48},{20,52},{24,56},{28,60},{32,0... | collective-permute-start | bytes 4718600 | tf_op jit(solution)/shard_map/ppermute | solution.py:31
  47.4 30.0 %collective-permute-start.6 = (bf16[64,32,128]{2,1,0:T(8,128)(2,1)}, bf16[64,32,128]{2,1,0:T(8,128)(2,1)}, u32[]{:S(2)}, u32[]{:S(2)}) collective-permute-start(bf16[64,32,128]{2,1,0:T(8,128)(2,1)} %own.1), channel_id=1, source_target_pairs={{0,32},{4,36},{8,40},{12,44},{16,48},{20,52},{24,56},{28,60},{32,0... | collective-permute-start | bytes 1572872 | tf_op jit(solution)/shard_map/ppermute | solution.py:31
  64.5 12.9 %collective-permute-start = (bf16[2,16,32,128]{3,2,1,0:T(8,128)(2,1)}, bf16[2,16,32,128]{3,2,1,0:T(8,128)(2,1)}, u32[]{:S(2)}, u32[]{:S(2)}) collective-permute-start(bf16[2,16,32,128]{3,2,1,0:T(8,128)(2,1)} %get-tuple-element.15), channel_id=1, source_target_pairs={{0,256},{4,260},{8,264},{12,268},{16,272},{20,276},{24,280},{28,28... | collective-permute-start | bytes 786440 | tf_op jit(solution)/shard_map/ppermute | solution.py:31
  67.6 9.8 %collective-permute-start.1 = (bf16[2,16,32,128]{3,2,1,0:T(8,128)(2,1)}, bf16[2,16,32,128]{3,2,1,0:T(8,128)(2,1)}, u32[]{:S(2)}, u32[]{:S(2)}) collective-permute-start(bf16[2,16,32,128]{3,2,1,0:T(8,128)(2,1)} %get-tuple-element.14), channel_id=1, source_target_pairs={{0,768},{4,772},{8,776},{12,780},{16,784},{20,788},{24,792},{28,79... | collective-permute-start | bytes 786440 | tf_op jit(solution)/shard_map/ppermute | solution.py:31
  71.0 10.5 %collective-permute-start.2 = (bf16[2,16,32,128]{3,2,1,0:T(8,128)(2,1)}, bf16[2,16,32,128]{3,2,1,0:T(8,128)(2,1)}, u32[]{:S(2)}, u32[]{:S(2)}) collective-permute-start(bf16[2,16,32,128]{3,2,1,0:T(8,128)(2,1)} %get-tuple-element.13), channel_id=1, source_target_pairs={{0,512},{4,516},{8,520},{12,524},{16,528},{20,532},{24,536},{28,54... | collective-permute-start | bytes 786440 | tf_op jit(solution)/shard_map/ppermute | solution.py:31
  81.5 1.0 copy-start
  82.5 0.7 copy-start.2
  89.1 11.0 %collective-permute-start.10 = (f32[16,32,128]{2,1,0:T(8,128)S(1)}, f32[16,32,128]{2,1,0:T(8,128)S(1)}, u32[]{:S(2)}, u32[]{:S(2)}) collective-permute-start(f32[16,32,128]{2,1,0:T(8,128)S(1)} %get-tuple-element.12), channel_id=1, source_target_pairs={{0,512},{4,516},{8,520},{12,524},{16,528},{20,532},{24,536},{28,54... | collective-permute-start | bytes 786440 | tf_op jit(solution)/shard_map/ppermute | solution.py:31
  92.6 12.8 %collective-permute-start.8 = (f32[16,32,128]{2,1,0:T(8,128)S(1)}, f32[16,32,128]{2,1,0:T(8,128)S(1)}, u32[]{:S(2)}, u32[]{:S(2)}) collective-permute-start(f32[16,32,128]{2,1,0:T(8,128)S(1)} %get-tuple-element.10), channel_id=1, source_target_pairs={{0,768},{4,772},{8,776},{12,780},{16,784},{20,788},{24,792},{28,79... | collective-permute-start | bytes 786440 | tf_op jit(solution)/shard_map/ppermute | solution.py:31
  98.2 8.7 %collective-permute-start.9 = (f32[16,32,128]{2,1,0:T(8,128)S(1)}, f32[16,32,128]{2,1,0:T(8,128)S(1)}, u32[]{:S(2)}, u32[]{:S(2)}) collective-permute-start(f32[16,32,128]{2,1,0:T(8,128)S(1)} %get-tuple-element.11), channel_id=1, source_target_pairs={{0,256},{4,260},{8,264},{12,268},{16,272},{20,276},{24,280},{28,28... | collective-permute-start | bytes 786440 | tf_op jit(solution)/shard_map/ppermute | solution.py:31

commit v2 on v1

--- a/solution.py
+++ b/solution.py
@@ -10,7 +10,6 @@
 BS, RANGE, SPAN = 32, 64, 16
 LANES = 128
 NEAR = 8
-STEPS = (0, 1, -1, 2)
 
 
 def device_pairs(move):
@@ -35,10 +34,6 @@
     return x, z, 1 - core, y
 
 
-def along_x(step):
-    return lambda x, z, core, y: (x + step, z, core, y)
-
-
 def along_z(step):
     return lambda x, z, core, y: (x, z + step, core, y)
 
@@ -47,8 +42,9 @@
     return x, (z + 2 if core == 0 else z - 2), core, y
 
 
-def target_row(row, step):
-    return (((row >> 3) - step) & (NX - 1)) * NEAR + (row & (NEAR - 1))
+def swapped_along_x(value):
+    groups = [[x * NEAR + n for x in range(NX)] for n in range(NEAR)]
+    return lax.all_to_all(value, "row", 0, 0, axis_index_groups=groups)
 
 
 def mask_kernel(place_ref, shifts_ref, masks_ref):
@@ -59,8 +55,8 @@
 
     def mask_step(j, carry):
         source = near + j
-        for t, step in enumerate(STEPS):
-            target = target_row(row, step)
+        for t in range(NX):
+            target = t * NEAR + (row & (NEAR - 1))
             value = jnp.zeros((BS, LANES), jnp.float32)
             for b in range(4):
                 own_range = col * 4 + b
@@ -74,9 +70,7 @@
 
 
 def product_kernel(
-    place_ref, shifts_ref, masks, left_0, left_1, left_2, left_3,
-    own, before, after, across, twin, twin_others,
-    out_0, out_1, out_2, out_3, right, sems,
+    place_ref, shifts_ref, masks, left, own, before, after, across, twin, twin_others, out, right, sems
 ):
     row = place_ref[0]
     layer = place_ref[2]
@@ -95,20 +89,17 @@
     for copy in copies:
         copy.wait()
 
-    lefts = [left_0, left_1, left_2, left_3]
-    outs = [out_0, out_1, out_2, out_3]
-
     def position_step(p, carry):
         place = layer * SPAN + p
-        for t, step in enumerate(STEPS):
-            target = target_row(row, step)
-            lhs = jnp.concatenate([lefts[t][0, p], lefts[t][1, p]], axis=1)
+        for t in range(NX):
+            target = t * NEAR + (row & (NEAR - 1))
+            lhs = jnp.concatenate([left[t, 0, p], left[t, 1, p]], axis=1)
             rows = []
             for j in range(NEAR):
                 q = (place + shifts_ref[target, near + j]) & (RANGE - 1)
                 rows.append(right[j, q] * masks[t, j])
             rhs = jnp.concatenate(rows, axis=0)
-            outs[t][p] = jnp.dot(lhs, rhs, preferred_element_type=jnp.float32)
+            out[t, p] = jnp.dot(lhs, rhs, preferred_element_type=jnp.float32)
         return carry
 
     lax.fori_loop(0, SPAN, position_step, 0)
@@ -118,50 +109,42 @@
     row = lax.axis_index("row")
     col = lax.axis_index("col")
     layer = lax.axis_index("layer")
-    x = row // NEAR
     place = jnp.stack([row, col, layer]).astype(jnp.int32)
     smem = pl.BlockSpec(memory_space=pltpu.SMEM)
     vmem = pl.BlockSpec(memory_space=pltpu.VMEM)
     anywhere = pl.BlockSpec(memory_space=pl.ANY)
 
+    mine = lax.dynamic_slice_in_dim(x_blocks, layer * SPAN, SPAN, 0)
+    gathered = lax.all_to_all(jnp.broadcast_to(mine[None], (NY, SPAN, BS, LANES)), "col", 0, 0)
+
     before = sent(x_blocks, along_z(1))
     after = sent(x_blocks, along_z(-1))
     across = sent(x_blocks, two_along_z)
     twin = sent(x_blocks, other_core)
-
-    mine = lax.dynamic_slice_in_dim(x_blocks, layer * SPAN, SPAN, 0)
-    gathered = lax.all_to_all(jnp.broadcast_to(mine[None], (NY, SPAN, BS, LANES)), "col", 0, 0)
-
-    def columns_of(step):
-        return lax.dynamic_slice_in_dim(gathered, ((x + step) % NX) * 2, 2, 0)
-
-    lefts = [columns_of(0)] + [sent(columns_of(step), along_x(step)) for step in STEPS[1:]]
-    twin_others = sent(jnp.concatenate([before, after, across], axis=0), other_core)
-
     masks = pl.pallas_call(
         mask_kernel,
-        out_shape=jax.ShapeDtypeStruct((len(STEPS), NEAR, BS, LANES), jnp.bfloat16),
+        out_shape=jax.ShapeDtypeStruct((NX, NEAR, BS, LANES), jnp.bfloat16),
         in_specs=[smem, smem],
         out_specs=vmem,
         name="masks",
     )(place, shifts)
-    part = jax.ShapeDtypeStruct((SPAN, BS, LANES), jnp.float32)
+    before, masks = lax.optimization_barrier((before, masks))
+    twin_others = sent(jnp.concatenate([before, after, across], axis=0), other_core)
+    left = swapped_along_x(gathered.reshape(NX, 2, SPAN, BS, LANES))
+
     parts = pl.pallas_call(
         product_kernel,
-        out_shape=[part] * 4,
-        in_specs=[smem, smem] + [vmem] * 5 + [anywhere] * 6,
-        out_specs=[vmem] * 4,
+        out_shape=jax.ShapeDtypeStruct((NX, SPAN, BS, LANES), jnp.float32),
+        in_specs=[smem, smem] + [vmem] * 2 + [anywhere] * 6,
+        out_specs=vmem,
         scratch_shapes=[
             pltpu.VMEM((NEAR, RANGE, BS, LANES), jnp.bfloat16),
             pltpu.SemaphoreType.DMA((NEAR,)),
         ],
         compiler_params=pltpu.CompilerParams(vmem_limit_bytes=20 * 1024 * 1024),
         name="range_products",
-    )(place, shifts, masks, *lefts, x_blocks, before, after, across, twin, twin_others)
-    total = parts[0]
-    for part, step in zip(parts[1:], STEPS[1:]):
-        total = total + sent(part, along_x(-step))
-    return total.astype(jnp.bfloat16)
+    )(place, shifts, masks, left, x_blocks, before, after, across, twin, twin_others)
+    return jnp.sum(swapped_along_x(parts), axis=0).astype(jnp.bfloat16)
 
 
 def solution(mesh):

time: 109 us -> 101 us (0.927)
  starting transfers between devices: 56.3 us -> 39.6 us
  blocking collectives: 0 us -> 15.9 us
  waiting for transfers between devices: 34.4 us -> 27.6 us
    ppermute x11 -> x5, starting transfers between devices: 49.4 us -> 27.9 us  [sent(): return lax.ppermute(value, AXES, device_pairs(move))]
    all_to_all x0 -> x1, blocking collectives: none -> 15.9 us  [swapped_along_x(): return lax.all_to_all(value, 'row', 0, 0, axis_index_groups=groups)]
    all_to_all x1, waiting for transfers between devices: 12.5 us -> 0.01 us  [local(): lax.all_to_all(jnp.broadcast_to(mine[None], (NY, SPAN, BS, LANES)), 'col'...]
    all_to_all x0 -> x1, waiting for transfers between devices: none -> 9.39 us  [swapped_along_x(): return lax.all_to_all(value, 'row', 0, 0, axis_index_groups=groups)]
    all_to_all x0 -> x1, starting transfers between devices: none -> 4.01 us  [swapped_along_x(): return lax.all_to_all(value, 'row', 0, 0, axis_index_groups=groups)]
    ppermute x11 -> x5, waiting for transfers between devices: 21.9 us -> 18.2 us  [sent(): return lax.ppermute(value, AXES, device_pairs(move))]
    dynamic_slice x1 -> x0, local copies, waits for them, and re-layouts: 2.11 us -> none  [columns_of(): return lax.dynamic_slice_in_dim(gathered, (x + step) % NX * 2, 2, 0)]
    unnamed x6 -> x14, local copies, waits for them, and re-layouts: 1.62 us -> 2.83 us
  transfers between devices with their start and end apart: 12 -> 7, of which waited for: 6 -> 5; matrix products, arithmetic and copies ran while one was open for 6% -> 2% of each run, Pallas kernels for 2% -> 2%
where the time goes in v2:
time: 101 us; the launch traced here: 99 us
  starting transfers between devices  39.6 us (39%)
  waiting for transfers between devices  27.6 us (27%)
  blocking collectives  15.9 us (16%)
  Pallas kernels  8.17 us (8%)
  local copies, waits for them, and re-layouts  4.92 us (5%)
  other arithmetic  2.71 us (3%)
    ppermute x5, starting transfers between devices, sent(): return lax.ppermute(value, AXES, device_pairs(move))  27.9 us
    ppermute x5, waiting for transfers between devices, sent(): return lax.ppermute(value, AXES, device_pairs(move))  18.2 us
    all_to_all x1, blocking collectives, swapped_along_x(): return lax.all_to_all(value, 'row', 0, 0, axis_index_groups=groups)  15.9 us
    all_to_all x1, waiting for transfers between devices, swapped_along_x(): return lax.all_to_all(value, 'row', 0, 0, axis_index_groups=groups)  9.39 us
    all_to_all x1, starting transfers between devices, local(): lax.all_to_all(jnp.broadcast_to(mine[None], (NY, SPAN, BS, LANES)), 'col'...  7.65 us
    pallas_call x1, Pallas kernels, local(): pl.pallas_call(product_kernel, out_shape=jax.ShapeDtypeStruct((NX, SPAN,...  5.92 us
    all_to_all x1, starting transfers between devices, swapped_along_x(): return lax.all_to_all(value, 'row', 0, 0, axis_index_groups=groups)  4.01 us
    unnamed x14, local copies, waits for them, and re-layouts  2.83 us
  transfers between devices with their start and end apart: 7, of which 5 were waited for; matrix products, arithmetic and copies ran while one was open for 2% of the time, Pallas kernels for 2%

profile of v2, /device:TPU:1, one launch (start us, length us, event | category | flops | bytes accessed | tf_op | source)
XLA Modules:
  0.0 99.0 jit_solution(12917896594463176664)
XLA Ops:
  0.0 0.9 constant_dynamic-slice_fusion
  0.9 0.0 copy-start.1
  0.9 1.2 %broadcast_in_dim.2 = bf16[8,16,32,128]{3,2,1,0:T(8,128)(2,1)} broadcast(bf16[16,32,128]{2,1,0:T(8,128)(2,1)S(1)} %constant_dynamic-slice_fusion), dimensions={1,2,3} | broadcast | bytes 1179648 | tf_op jit(solution)/shard_map/broadcast_in_dim | solution.py:118
  2.1 7.7 %all-to-all-start = ((bf16[8,16,32,128]{3,2,1,0:T(8,128)(2,1)}), bf16[8,16,32,128]{3,2,1,0:T(8,128)(2,1)S(1)}, u32[]{:S(2)}, u32[]{:S(2)}) async-start(bf16[8,16,32,128]{3,2,1,0:T(8,128)(2,1)} %broadcast_in_dim.2), calls=%async_computation | async-start | bytes 2097152 | tf_op jit(solution)/shard_map/all_to_all | solution.py:118
  9.8 4.0 %collective-permute-start = (bf16[64,32,128]{2,1,0:T(8,128)(2,1)S(1)}, bf16[64,32,128]{2,1,0:T(8,128)(2,1)S(1)}, u32[]{:S(2)}, u32[]{:S(2)}) collective-permute-start(bf16[64,32,128]{2,1,0:T(8,128)(2,1)S(1)} %copy-done.1), channel_id=1, source_target_pairs={{0,64},{4,68},{8,72},{12,76},{16,80},{20,84},{24,88},{28,92},{32,9... | collective-permute-start | bytes 1572872 | tf_op jit(solution)/shard_map/ppermute | solution.py:30
  13.8 15.9 %collective-permute-start.1 = (bf16[64,32,128]{2,1,0:T(8,128)(2,1)S(1)}, bf16[64,32,128]{2,1,0:T(8,128)(2,1)S(1)}, u32[]{:S(2)}, u32[]{:S(2)}) collective-permute-start(bf16[64,32,128]{2,1,0:T(8,128)(2,1)S(1)} %copy-done.1), channel_id=1, source_target_pairs={{0,195},{4,199},{8,203},{12,207},{16,211},{20,215},{24,219},{28,22... | collective-permute-start | bytes 1572872 | tf_op jit(solution)/shard_map/ppermute | solution.py:30
  29.6 3.4 %collective-permute-start.2 = (bf16[64,32,128]{2,1,0:T(8,128)(2,1)S(1)}, bf16[64,32,128]{2,1,0:T(8,128)(2,1)S(1)}, u32[]{:S(2)}, u32[]{:S(2)}) collective-permute-start(bf16[64,32,128]{2,1,0:T(8,128)(2,1)S(1)} %copy-done.1), channel_id=1, source_target_pairs={{0,128},{4,132},{8,136},{12,140},{16,144},{20,148},{24,152},{28,15... | collective-permute-start | bytes 1572872 | tf_op jit(solution)/shard_map/ppermute | solution.py:30
  33.0 0.6 pad_add_fusion.place_ref
  33.6 2.2 %masks.1 = bf16[4,8,32,128]{3,2,1,0:T(8,128)(2,1)} custom-call(s32[3]{0:T(128)} %pad_add_fusion.place_ref, s32[32,32]{1,0:T(8,128)} %shifts_ref.3), custom_call_target="tpu_custom_call" | custom-call | tf_op jit(solution)/shard_map/masks/pallas_call | solution.py:124
  35.9 3.1 %collective-permute-done.before = bf16[64,32,128]{2,1,0:T(8,128)(2,1)S(1)} collective-permute-done((bf16[64,32,128]{2,1,0:T(8,128)(2,1)S(1)}, bf16[64,32,128]{2,1,0:T(8,128)(2,1)S(1)}, u32[]{:S(2)}, u32[]{:S(2)}) %collective-permute-start) | collective-permute-done | bytes 524320 | tf_op jit(solution)/shard_map/ppermute | solution.py:30
  39.0 5.4 %collective-permute-done.1.after = bf16[64,32,128]{2,1,0:T(8,128)(2,1)S(1)} collective-permute-done((bf16[64,32,128]{2,1,0:T(8,128)(2,1)S(1)}, bf16[64,32,128]{2,1,0:T(8,128)(2,1)S(1)}, u32[]{:S(2)}, u32[]{:S(2)}) %collective-permute-start.1) | collective-permute-done | bytes 524320 | tf_op jit(solution)/shard_map/ppermute | solution.py:30
  44.5 8.1 %collective-permute-done.2.across = bf16[64,32,128]{2,1,0:T(8,128)(2,1)S(1)} collective-permute-done((bf16[64,32,128]{2,1,0:T(8,128)(2,1)S(1)}, bf16[64,32,128]{2,1,0:T(8,128)(2,1)S(1)}, u32[]{:S(2)}, u32[]{:S(2)}) %collective-permute-start.2) | collective-permute-done | bytes 524320 | tf_op jit(solution)/shard_map/ppermute | solution.py:30
  52.6 1.3 %pad_maximum_fusion = bf16[192,32,128]{2,1,0:T(8,128)(2,1)} fusion(bf16[64,32,128]{2,1,0:T(8,128)(2,1)S(1)} %collective-permute-done.2.across, bf16[64,32,128]{2,1,0:T(8,128)(2,1)S(1)} %collective-permute-done.1.after, bf16[64,32,128]{2,1,0:T(8,128)(2,1)S(1)} %collective-permute-done.before), kind=kLoop, calls=%fused_computation | loop fusion | flops 1572864 | bytes 3145728 | tf_op jit(solution)/shard_map/concatenate | solution.py:132
  53.9 2.0 %collective-permute-start.4 = (bf16[192,32,128]{2,1,0:T(8,128)(2,1)}, bf16[192,32,128]{2,1,0:T(8,128)(2,1)}, u32[]{:S(2)}, u32[]{:S(2)}) collective-permute-start(bf16[192,32,128]{2,1,0:T(8,128)(2,1)} %pad_maximum_fusion), channel_id=1, source_target_pairs={{0,32},{4,36},{8,40},{12,44},{16,48},{20,52},{24,56},{28,60},{32,0... | collective-permute-start | bytes 4718600 | tf_op jit(solution)/shard_map/ppermute | solution.py:30
  56.0 1.0 copy-done.6
  57.0 4.0 %all-to-all-start.1 = ((bf16[4,2,16,32,128]{4,3,2,1,0:T(8,128)(2,1)}), bf16[4,2,16,32,128]{4,3,2,1,0:T(8,128)(2,1)S(1)}, u32[]{:S(2)}, u32[]{:S(2)}) async-start(bf16[4,2,16,32,128]{4,3,2,1,0:T(8,128)(2,1)} %bitcast.4), calls=%async_computation.1 | async-start | bytes 2097152 | tf_op jit(solution)/shard_map/all_to_all | solution.py:47
  61.0 2.7 %collective-permute-start.3 = (bf16[64,32,128]{2,1,0:T(8,128)(2,1)S(1)}, bf16[64,32,128]{2,1,0:T(8,128)(2,1)S(1)}, u32[]{:S(2)}, u32[]{:S(2)}) collective-permute-start(bf16[64,32,128]{2,1,0:T(8,128)(2,1)S(1)} %copy-done.1), channel_id=1, source_target_pairs={{0,32},{4,36},{8,40},{12,44},{16,48},{20,52},{24,56},{28,60},{32,0... | collective-permute-start | bytes 1572872 | tf_op jit(solution)/shard_map/ppermute | solution.py:30
  63.7 1.5 %collective-permute-done.3.twin = bf16[64,32,128]{2,1,0:T(8,128)(2,1)S(1)} collective-permute-done((bf16[64,32,128]{2,1,0:T(8,128)(2,1)S(1)}, bf16[64,32,128]{2,1,0:T(8,128)(2,1)S(1)}, u32[]{:S(2)}, u32[]{:S(2)}) %collective-permute-start.3) | collective-permute-done | bytes 524320 | tf_op jit(solution)/shard_map/ppermute | solution.py:30
  65.2 0.8 copy-done.2
  66.0 9.4 %all-to-all-done.1.left = bf16[4,2,16,32,128]{4,3,2,1,0:T(8,128)(2,1)S(1)} async-done(((bf16[4,2,16,32,128]{4,3,2,1,0:T(8,128)(2,1)}), bf16[4,2,16,32,128]{4,3,2,1,0:T(8,128)(2,1)S(1)}, u32[]{:S(2)}, u32[]{:S(2)}) %all-to-all-start.1) | async-done | bytes 1048608 | tf_op jit(solution)/shard_map/all_to_all | solution.py:47
  75.4 1.0 %copy-done.3 = bf16[64,32,128]{2,1,0:T(8,128)(2,1)S(1)} copy-done((bf16[64,32,128]{2,1,0:T(8,128)(2,1)S(1)}, bf16[64,32,128]{2,1,0:T(8,128)(2,1)}, u32[]{:S(2)}) %copy-start.3) | copy-done | bytes 524312
  76.4 5.9 %range_products.1 = f32[4,16,32,128]{3,2,1,0:T(8,128)S(1)} custom-call(s32[3]{0:T(128)S(1)} %copy-done.5, s32[32,32]{1,0:T(8,128)S(1)} %copy-done.4, bf16[4,8,32,128]{3,2,1,0:T(8,128)(2,1)S(1)} %copy-done, bf16[4,2,16,32,128]{4,3,2,1,0:T(8,128)(2,1)S(1)} %all-to-all-done.1.left, bf16[64,32,128]{2,1,0:T(8,128)(2,1)S(1)} %copy-done.1, ...), custom_call_target="tpu_custom_call" | custom-call | tf_op jit(solution)/shard_map/range_products/pallas_call | solution.py:135
  82.4 15.9 %all_to_all.15 = f32[4,16,32,128]{3,2,1,0:T(8,128)S(1)} all-to-all(f32[4,16,32,128]{3,2,1,0:T(8,128)S(1)} %range_products.1), channel_id=1, replica_groups={{0,256,512,768},{32,288,544,800},{64,320,576,832},{96,352,608,864},{128..., dimensions={0} | all-to-all | bytes 2097152 | tf_op jit(solution)/shard_map/all_to_all | solution.py:47
  98.2 0.8 reduce_sum.9
  (12 shorter events, 0.0 us)
Async XLA Ops:
  0.9 8.8 %copy-start.1 = (bf16[64,32,128]{2,1,0:T(8,128)(2,1)S(1)}, bf16[64,32,128]{2,1,0:T(8,128)(2,1)}, u32[]{:S(2)}) copy-start(bf16[64,32,128]{2,1,0:T(8,128)(2,1)} %own.1) | copy-start | bytes 1572868
  2.1 53.9 %all-to-all-start = ((bf16[8,16,32,128]{3,2,1,0:T(8,128)(2,1)}), bf16[8,16,32,128]{3,2,1,0:T(8,128)(2,1)S(1)}, u32[]{:S(2)}, u32[]{:S(2)}) async-start(bf16[8,16,32,128]{3,2,1,0:T(8,128)(2,1)} %broadcast_in_dim.2), calls=%async_computation | async-start | bytes 2097152 | tf_op jit(solution)/shard_map/all_to_all | solution.py:118
  9.8 29.3 %collective-permute-start = (bf16[64,32,128]{2,1,0:T(8,128)(2,1)S(1)}, bf16[64,32,128]{2,1,0:T(8,128)(2,1)S(1)}, u32[]{:S(2)}, u32[]{:S(2)}) collective-permute-start(bf16[64,32,128]{2,1,0:T(8,128)(2,1)S(1)} %copy-done.1), channel_id=1, source_target_pairs={{0,64},{4,68},{8,72},{12,76},{16,80},{20,84},{24,88},{28,92},{32,9... | collective-permute-start | bytes 1572872 | tf_op jit(solution)/shard_map/ppermute | solution.py:30
  13.8 30.7 %collective-permute-start.1 = (bf16[64,32,128]{2,1,0:T(8,128)(2,1)S(1)}, bf16[64,32,128]{2,1,0:T(8,128)(2,1)S(1)}, u32[]{:S(2)}, u32[]{:S(2)}) collective-permute-start(bf16[64,32,128]{2,1,0:T(8,128)(2,1)S(1)} %copy-done.1), channel_id=1, source_target_pairs={{0,195},{4,199},{8,203},{12,207},{16,211},{20,215},{24,219},{28,22... | collective-permute-start | bytes 1572872 | tf_op jit(solution)/shard_map/ppermute | solution.py:30
  29.6 23.0 %collective-permute-start.2 = (bf16[64,32,128]{2,1,0:T(8,128)(2,1)S(1)}, bf16[64,32,128]{2,1,0:T(8,128)(2,1)S(1)}, u32[]{:S(2)}, u32[]{:S(2)}) collective-permute-start(bf16[64,32,128]{2,1,0:T(8,128)(2,1)S(1)} %copy-done.1), channel_id=1, source_target_pairs={{0,128},{4,132},{8,136},{12,140},{16,144},{20,148},{24,152},{28,15... | collective-permute-start | bytes 1572872 | tf_op jit(solution)/shard_map/ppermute | solution.py:30
  53.9 21.5 %copy-start = (bf16[4,8,32,128]{3,2,1,0:T(8,128)(2,1)S(1)}, bf16[4,8,32,128]{3,2,1,0:T(8,128)(2,1)}, u32[]{:S(2)}) copy-start(bf16[4,8,32,128]{3,2,1,0:T(8,128)(2,1)} %masks.1) | copy-start | bytes 786436
  53.9 21.5 %copy-start.4 = (s32[32,32]{1,0:T(8,128)S(1)}, s32[32,32]{1,0:T(8,128)}, u32[]{:S(2)}) copy-start(s32[32,32]{1,0:T(8,128)} %shifts_ref.3) | copy-start | bytes 12292
  53.9 21.5 %copy-start.5 = (s32[3]{0:T(128)S(1)}, s32[3]{0:T(128)}, u32[]{:S(2)}) copy-start(s32[3]{0:T(128)} %pad_add_fusion.place_ref) | copy-start | bytes 40
  53.9 12.1 %collective-permute-start.4 = (bf16[192,32,128]{2,1,0:T(8,128)(2,1)}, bf16[192,32,128]{2,1,0:T(8,128)(2,1)}, u32[]{:S(2)}, u32[]{:S(2)}) collective-permute-start(bf16[192,32,128]{2,1,0:T(8,128)(2,1)} %pad_maximum_fusion), channel_id=1, source_target_pairs={{0,32},{4,36},{8,40},{12,44},{16,48},{20,52},{24,56},{28,60},{32,0... | collective-permute-start | bytes 4718600 | tf_op jit(solution)/shard_map/ppermute | solution.py:30
  56.0 1.0 %copy-start.6 = (bf16[8,16,32,128]{3,2,1,0:T(8,128)(2,1)}, bf16[8,16,32,128]{3,2,1,0:T(8,128)(2,1)S(1)}, u32[]{:S(2)}) copy-start(bf16[8,16,32,128]{3,2,1,0:T(8,128)(2,1)S(1)} %all-to-all-done) | copy-start | bytes 3145732
  57.0 18.4 %all-to-all-start.1 = ((bf16[4,2,16,32,128]{4,3,2,1,0:T(8,128)(2,1)}), bf16[4,2,16,32,128]{4,3,2,1,0:T(8,128)(2,1)S(1)}, u32[]{:S(2)}, u32[]{:S(2)}) async-start(bf16[4,2,16,32,128]{4,3,2,1,0:T(8,128)(2,1)} %bitcast.4), calls=%async_computation.1 | async-start | bytes 2097152 | tf_op jit(solution)/shard_map/all_to_all | solution.py:47
  61.0 4.2 %collective-permute-start.3 = (bf16[64,32,128]{2,1,0:T(8,128)(2,1)S(1)}, bf16[64,32,128]{2,1,0:T(8,128)(2,1)S(1)}, u32[]{:S(2)}, u32[]{:S(2)}) collective-permute-start(bf16[64,32,128]{2,1,0:T(8,128)(2,1)S(1)} %copy-done.1), channel_id=1, source_target_pairs={{0,32},{4,36},{8,40},{12,44},{16,48},{20,52},{24,56},{28,60},{32,0... | collective-permute-start | bytes 1572872 | tf_op jit(solution)/shard_map/ppermute | solution.py:30
  65.2 0.8 copy-start.2
  75.4 1.0 %copy-start.3 = (bf16[64,32,128]{2,1,0:T(8,128)(2,1)S(1)}, bf16[64,32,128]{2,1,0:T(8,128)(2,1)}, u32[]{:S(2)}) copy-start(bf16[64,32,128]{2,1,0:T(8,128)(2,1)} %copy-done.2) | copy-start | bytes 1572868

commit v3 on v2

--- a/solution.py
+++ b/solution.py
@@ -34,12 +34,19 @@
     return x, z, 1 - core, y
 
 
-def along_z(step):
-    return lambda x, z, core, y: (x, z + step, core, y)
+def along_z(turn):
+    def move(x, z, core, y):
+        if core == turn:
+            return x, z ^ 1, core, y
+        return x, (z + 1 if z % 2 else z - 1), core, y
+
+    return move
 
 
-def two_along_z(x, z, core, y):
-    return x, (z + 2 if core == 0 else z - 2), core, y
+def spread(x, z, core, y):
+    near_x, side = y // 2, y % 2
+    turn = (x - near_x) % NX
+    return near_x, z, core, (y + turn if side else y - turn)
 
 
 def swapped_along_x(value):
@@ -70,20 +77,24 @@
 
 
 def product_kernel(
-    place_ref, shifts_ref, masks, left, own, before, after, across, twin, twin_others, out, right, sems
+    place_ref, shifts_ref, masks, left, pair, far, twin_pair, twin_far, out, right, sems
 ):
     row = place_ref[0]
     layer = place_ref[2]
     core = row & 1
     zl = (row >> 1) & 3
-    near = (row >> 3) * NEAR
+    x = row >> 3
+    near = x * NEAR
 
-    pieces = [(own, 0, core), (before, -1, core), (after, 1, core), (across, 2, core), (twin, 0, 1 - core)]
-    pieces += [(twin_others.at[pl.ds(n * RANGE, RANGE)], step, 1 - core) for n, step in enumerate((-1, 1, 2))]
+    first = jnp.where(core == 0, 1, 3)
+    second = jnp.where(core == 0, 3, 1)
+    pieces = [(pair, 0, 0, core), (pair, 1, first, core), (far, 0, second, core), (far, 1, 2, core)]
+    pieces += [(twin_pair, 0, 0, 1 - core), (twin_pair, 1, second, 1 - core)]
+    pieces += [(twin_far, 0, first, 1 - core), (twin_far, 1, 2, 1 - core)]
     copies = []
-    for n, (piece, step, parity) in enumerate(pieces):
-        slot = ((zl + step) & (NZ - 1)) * 2 + parity
-        copies.append(pltpu.make_async_copy(piece, right.at[slot], sems.at[n]))
+    for n, (piece, half, turn, parity) in enumerate(pieces):
+        slot = (zl ^ turn) * 2 + parity
+        copies.append(pltpu.make_async_copy(piece.at[pl.ds(half * RANGE, RANGE)], right.at[slot], sems.at[n]))
     for copy in copies:
         copy.start()
     for copy in copies:
@@ -93,7 +104,9 @@
         place = layer * SPAN + p
         for t in range(NX):
             target = t * NEAR + (row & (NEAR - 1))
-            lhs = jnp.concatenate([left[t, 0, p], left[t, 1, p]], axis=1)
+            turn = (t - x) & (NX - 1)
+            low, high = (2 * x - turn) & (NY - 1), (2 * x + 1 + turn) & (NY - 1)
+            lhs = jnp.concatenate([left[low, p], left[high, p]], axis=1)
             rows = []
             for j in range(NEAR):
                 q = (place + shifts_ref[target, near + j]) & (RANGE - 1)
@@ -115,12 +128,7 @@
     anywhere = pl.BlockSpec(memory_space=pl.ANY)
 
     mine = lax.dynamic_slice_in_dim(x_blocks, layer * SPAN, SPAN, 0)
-    gathered = lax.all_to_all(jnp.broadcast_to(mine[None], (NY, SPAN, BS, LANES)), "col", 0, 0)
-
-    before = sent(x_blocks, along_z(1))
-    after = sent(x_blocks, along_z(-1))
-    across = sent(x_blocks, two_along_z)
-    twin = sent(x_blocks, other_core)
+    mine = sent(mine, spread)
     masks = pl.pallas_call(
         mask_kernel,
         out_shape=jax.ShapeDtypeStruct((NX, NEAR, BS, LANES), jnp.bfloat16),
@@ -128,14 +136,17 @@
         out_specs=vmem,
         name="masks",
     )(place, shifts)
-    before, masks = lax.optimization_barrier((before, masks))
-    twin_others = sent(jnp.concatenate([before, after, across], axis=0), other_core)
-    left = swapped_along_x(gathered.reshape(NX, 2, SPAN, BS, LANES))
-
+    near = sent(x_blocks, along_z(0))
+    near, masks, mine = lax.optimization_barrier((near, masks, mine))
+    left = lax.all_to_all(jnp.broadcast_to(mine[None], (NY, SPAN, BS, LANES)), "col", 0, 0)
+    pair = jnp.concatenate([x_blocks, near], axis=0)
+    far = sent(pair, along_z(1))
+    twin_pair = sent(pair, other_core)
+    twin_far = sent(far, other_core)
     parts = pl.pallas_call(
         product_kernel,
         out_shape=jax.ShapeDtypeStruct((NX, SPAN, BS, LANES), jnp.float32),
-        in_specs=[smem, smem] + [vmem] * 2 + [anywhere] * 6,
+        in_specs=[smem, smem] + [vmem] * 2 + [anywhere] * 4,
         out_specs=vmem,
         scratch_shapes=[
             pltpu.VMEM((NEAR, RANGE, BS, LANES), jnp.bfloat16),
@@ -143,7 +154,7 @@
         ],
         compiler_params=pltpu.CompilerParams(vmem_limit_bytes=20 * 1024 * 1024),
         name="range_products",
-    )(place, shifts, masks, left, x_blocks, before, after, across, twin, twin_others)
+    )(place, shifts, masks, left, pair, far, twin_pair, twin_far)
     return jnp.sum(swapped_along_x(parts), axis=0).astype(jnp.bfloat16)
 
 

time: 101 us -> 92.5 us (0.916)
  the two profiles are of different devices: /device:TPU:1 before, /device:TPU:2 now
where the time goes in v3:
time: 92.5 us; the launch traced here: 92 us
  starting transfers between devices  40.7 us (44%)
  waiting for transfers between devices  22.2 us (24%)
  blocking collectives  15 us (16%)
  Pallas kernels  8.18 us (9%)
  local copies, waits for them, and re-layouts  4.44 us (5%)
  other arithmetic  1.36 us (1%)
    ppermute x5, starting transfers between devices, sent(): return lax.ppermute(value, AXES, device_pairs(move))  30.5 us
    all_to_all x1, waiting for transfers between devices, local(): lax.all_to_all(jnp.broadcast_to(mine[None], (NY, SPAN, BS, LANES)), 'col'...  20.1 us
    all_to_all x1, blocking collectives, swapped_along_x(): return lax.all_to_all(value, 'row', 0, 0, axis_index_groups=groups)  15 us
    all_to_all x1, starting transfers between devices, local(): lax.all_to_all(jnp.broadcast_to(mine[None], (NY, SPAN, BS, LANES)), 'col'...  10.2 us
    pallas_call x1, Pallas kernels, local(): pl.pallas_call(product_kernel, out_shape=jax.ShapeDtypeStruct((NX, SPAN,...  5.95 us
    unnamed x13, local copies, waits for them, and re-layouts  2.29 us
    pallas_call x1, Pallas kernels, local(): pl.pallas_call(mask_kernel, out_shape=jax.ShapeDtypeStruct((NX, NEAR, BS,...  2.23 us
    ppermute x5, waiting for transfers between devices, sent(): return lax.ppermute(value, AXES, device_pairs(move))  2.14 us
  transfers between devices with their start and end apart: 6, of which 3 were waited for; matrix products, arithmetic and copies ran while one was open for 3% of the time, Pallas kernels for 2%

profile of v3, /device:TPU:2, one launch (start us, length us, event | category | flops | bytes accessed | tf_op | source)
XLA Modules:
  0.0 92.0 jit_solution(17146122669581461240)
XLA Ops:
  0.0 4.4 %collective-permute-start = (bf16[64,32,128]{2,1,0:T(8,128)(2,1)}, bf16[64,32,128]{2,1,0:T(8,128)(2,1)S(1)}, u32[]{:S(2)}, u32[]{:S(2)}) collective-permute-start(bf16[64,32,128]{2,1,0:T(8,128)(2,1)} %param.2), channel_id=1, source_target_pairs={{0,64},{4,68},{8,72},{12,76},{16,80},{20,84},{24,88},{28,92},{32,2... | collective-permute-start | bytes 1572872 | tf_op jit(solution)/shard_map/ppermute | solution.py:30
  4.4 0.9 constant_dynamic-slice_fusion
  5.3 5.3 %collective-permute-start.1 = (bf16[16,32,128]{2,1,0:T(8,128)(2,1)S(1)}, bf16[16,32,128]{2,1,0:T(8,128)(2,1)S(1)}, u32[]{:S(2)}, u32[]{:S(2)}) collective-permute-start(bf16[16,32,128]{2,1,0:T(8,128)(2,1)S(1)} %constant_dynamic-slice_fusion), channel_id=1, source_target_pairs={{0,0},{4,4},{8,284},{12,280},{16,520},{20,540},{24,788},{28,768},{... | collective-permute-start | bytes 393224 | tf_op jit(solution)/shard_map/ppermute | solution.py:30
  10.7 0.6 pad_add_fusion.place_ref
  11.3 2.2 %masks.1 = bf16[4,8,32,128]{3,2,1,0:T(8,128)(2,1)} custom-call(s32[3]{0:T(128)} %pad_add_fusion.place_ref, s32[32,32]{1,0:T(8,128)} %shifts_ref.3), custom_call_target="tpu_custom_call" | custom-call | tf_op jit(solution)/shard_map/masks/pallas_call | solution.py:132
  13.5 0.0 copy-done.5
  13.6 1.9 %collective-permute-done.1 = bf16[16,32,128]{2,1,0:T(8,128)(2,1)S(1)} collective-permute-done((bf16[16,32,128]{2,1,0:T(8,128)(2,1)S(1)}, bf16[16,32,128]{2,1,0:T(8,128)(2,1)S(1)}, u32[]{:S(2)}, u32[]{:S(2)}) %collective-permute-start.1) | collective-permute-done | bytes 131104 | tf_op jit(solution)/shard_map/ppermute | solution.py:30
  15.5 0.0 collective-permute-done
  15.5 0.1 constant_dynamic-update-slice_fusion.pair
  15.6 16.4 %collective-permute-start.2 = (bf16[128,32,128]{2,1,0:T(8,128)(2,1)S(1)}, bf16[128,32,128]{2,1,0:T(8,128)(2,1)S(1)}, u32[]{:S(2)}, u32[]{:S(2)}) collective-permute-start(bf16[128,32,128]{2,1,0:T(8,128)(2,1)S(1)} %constant_dynamic-update-slice_fusion.pair), channel_id=1, source_target_pairs={{0,195},{4,199},{8,203},{12,207},{16,211},{20,215},{24,219},{28,22... | collective-permute-start | bytes 3145736 | tf_op jit(solution)/shard_map/ppermute | solution.py:30
  32.0 1.2 %broadcast_in_dim.2 = bf16[8,16,32,128]{3,2,1,0:T(8,128)(2,1)} broadcast(bf16[16,32,128]{2,1,0:T(8,128)(2,1)S(1)} %collective-permute-done.1), dimensions={1,2,3} | broadcast | bytes 1179648 | tf_op jit(solution)/shard_map/broadcast_in_dim | solution.py:141
  33.2 10.2 %all-to-all-start = ((bf16[8,16,32,128]{3,2,1,0:T(8,128)(2,1)}), bf16[8,16,32,128]{3,2,1,0:T(8,128)(2,1)S(1)}, u32[]{:S(2)}, u32[]{:S(2)}) async-start(bf16[8,16,32,128]{3,2,1,0:T(8,128)(2,1)} %broadcast_in_dim.2), calls=%async_computation | async-start | bytes 2097152 | tf_op jit(solution)/shard_map/all_to_all | solution.py:141
  43.4 1.9 %collective-permute-start.3 = (bf16[128,32,128]{2,1,0:T(8,128)(2,1)S(1)}, bf16[128,32,128]{2,1,0:T(8,128)(2,1)S(1)}, u32[]{:S(2)}, u32[]{:S(2)}) collective-permute-start(bf16[128,32,128]{2,1,0:T(8,128)(2,1)S(1)} %constant_dynamic-update-slice_fusion.pair), channel_id=1, source_target_pairs={{0,32},{4,36},{8,40},{12,44},{16,48},{20,52},{24,56},{28,60},{32,0... | collective-permute-start | bytes 3145736 | tf_op jit(solution)/shard_map/ppermute | solution.py:30
  45.3 0.0 collective-permute-done.2.far
  45.3 2.4 %collective-permute-start.4 = (bf16[128,32,128]{2,1,0:T(8,128)(2,1)S(1)}, bf16[128,32,128]{2,1,0:T(8,128)(2,1)}, u32[]{:S(2)}, u32[]{:S(2)}) collective-permute-start(bf16[128,32,128]{2,1,0:T(8,128)(2,1)S(1)} %collective-permute-done.2.far), channel_id=1, source_target_pairs={{0,32},{4,36},{8,40},{12,44},{16,48},{20,52},{24,56},{28,60},{32,0... | collective-permute-start | bytes 3145736 | tf_op jit(solution)/shard_map/ppermute | solution.py:30
  47.7 0.2 collective-permute-done.3.twin_pair
  47.9 1.0 %copy-done = bf16[128,32,128]{2,1,0:T(8,128)(2,1)} copy-done((bf16[128,32,128]{2,1,0:T(8,128)(2,1)}, bf16[128,32,128]{2,1,0:T(8,128)(2,1)S(1)}, u32[]{:S(2)}) %copy-start) | copy-done | bytes 1048600
  48.9 20.1 %all-to-all-done.left = bf16[8,16,32,128]{3,2,1,0:T(8,128)(2,1)S(1)} async-done(((bf16[8,16,32,128]{3,2,1,0:T(8,128)(2,1)}), bf16[8,16,32,128]{3,2,1,0:T(8,128)(2,1)S(1)}, u32[]{:S(2)}, u32[]{:S(2)}) %all-to-all-start) | async-done | bytes 1048608 | tf_op jit(solution)/shard_map/all_to_all | solution.py:141
  69.0 0.0 collective-permute-done.4.twin_far
  69.0 0.0 copy-done.2
  69.1 1.2 %copy-done.1 = bf16[128,32,128]{2,1,0:T(8,128)(2,1)S(1)} copy-done((bf16[128,32,128]{2,1,0:T(8,128)(2,1)S(1)}, bf16[128,32,128]{2,1,0:T(8,128)(2,1)}, u32[]{:S(2)}) %copy-start.1) | copy-done | bytes 1048600
  70.3 6.0 %range_products.1 = f32[4,16,32,128]{3,2,1,0:T(8,128)S(1)} custom-call(s32[3]{0:T(128)S(1)} %copy-done.4, s32[32,32]{1,0:T(8,128)S(1)} %copy-done.3, bf16[4,8,32,128]{3,2,1,0:T(8,128)(2,1)S(1)} %copy-done.2, bf16[8,16,32,128]{3,2,1,0:T(8,128)(2,1)S(1)} %all-to-all-done.left, bf16[128,32,128]{2,1,0:T(8,128)(2,1)S(1)} %constant_dynamic-update-slice_fusion.pair, ...), custom_call_target="tpu_custom_call" | custom-call | tf_op jit(solution)/shard_map/range_products/pallas_call | solution.py:146
  76.2 15.0 %all_to_all.10 = f32[4,16,32,128]{3,2,1,0:T(8,128)S(1)} all-to-all(f32[4,16,32,128]{3,2,1,0:T(8,128)S(1)} %range_products.1), channel_id=1, replica_groups={{0,256,512,768},{32,288,544,800},{64,320,576,832},{96,352,608,864},{128..., dimensions={0} | all-to-all | bytes 2097152 | tf_op jit(solution)/shard_map/all_to_all | solution.py:54
  91.2 0.8 reduce_sum.9
  (9 shorter events, 0.0 us)
Async XLA Ops:
  0.0 13.5 %copy-start.5 = (bf16[64,32,128]{2,1,0:T(8,128)(2,1)S(1)}, bf16[64,32,128]{2,1,0:T(8,128)(2,1)}, u32[]{:S(2)}) copy-start(bf16[64,32,128]{2,1,0:T(8,128)(2,1)} %param.2) | copy-start | bytes 1572868
  0.0 15.5 %collective-permute-start = (bf16[64,32,128]{2,1,0:T(8,128)(2,1)}, bf16[64,32,128]{2,1,0:T(8,128)(2,1)S(1)}, u32[]{:S(2)}, u32[]{:S(2)}) collective-permute-start(bf16[64,32,128]{2,1,0:T(8,128)(2,1)} %param.2), channel_id=1, source_target_pairs={{0,64},{4,68},{8,72},{12,76},{16,80},{20,84},{24,88},{28,92},{32,2... | collective-permute-start | bytes 1572872 | tf_op jit(solution)/shard_map/ppermute | solution.py:30
  5.3 10.2 %collective-permute-start.1 = (bf16[16,32,128]{2,1,0:T(8,128)(2,1)S(1)}, bf16[16,32,128]{2,1,0:T(8,128)(2,1)S(1)}, u32[]{:S(2)}, u32[]{:S(2)}) collective-permute-start(bf16[16,32,128]{2,1,0:T(8,128)(2,1)S(1)} %constant_dynamic-slice_fusion), channel_id=1, source_target_pairs={{0,0},{4,4},{8,284},{12,280},{16,520},{20,540},{24,788},{28,768},{... | collective-permute-start | bytes 393224 | tf_op jit(solution)/shard_map/ppermute | solution.py:30
  15.6 29.7 %collective-permute-start.2 = (bf16[128,32,128]{2,1,0:T(8,128)(2,1)S(1)}, bf16[128,32,128]{2,1,0:T(8,128)(2,1)S(1)}, u32[]{:S(2)}, u32[]{:S(2)}) collective-permute-start(bf16[128,32,128]{2,1,0:T(8,128)(2,1)S(1)} %constant_dynamic-update-slice_fusion.pair), channel_id=1, source_target_pairs={{0,195},{4,199},{8,203},{12,207},{16,211},{20,215},{24,219},{28,22... | collective-permute-start | bytes 3145736 | tf_op jit(solution)/shard_map/ppermute | solution.py:30
  33.2 35.9 %copy-start.2 = (bf16[4,8,32,128]{3,2,1,0:T(8,128)(2,1)S(1)}, bf16[4,8,32,128]{3,2,1,0:T(8,128)(2,1)}, u32[]{:S(2)}) copy-start(bf16[4,8,32,128]{3,2,1,0:T(8,128)(2,1)} %masks.1) | copy-start | bytes 786436
  33.2 35.9 %copy-start.3 = (s32[32,32]{1,0:T(8,128)S(1)}, s32[32,32]{1,0:T(8,128)}, u32[]{:S(2)}) copy-start(s32[32,32]{1,0:T(8,128)} %shifts_ref.3) | copy-start | bytes 12292
  33.2 35.9 %copy-start.4 = (s32[3]{0:T(128)S(1)}, s32[3]{0:T(128)}, u32[]{:S(2)}) copy-start(s32[3]{0:T(128)} %pad_add_fusion.place_ref) | copy-start | bytes 40
  33.2 35.9 %all-to-all-start = ((bf16[8,16,32,128]{3,2,1,0:T(8,128)(2,1)}), bf16[8,16,32,128]{3,2,1,0:T(8,128)(2,1)S(1)}, u32[]{:S(2)}, u32[]{:S(2)}) async-start(bf16[8,16,32,128]{3,2,1,0:T(8,128)(2,1)} %broadcast_in_dim.2), calls=%async_computation | async-start | bytes 2097152 | tf_op jit(solution)/shard_map/all_to_all | solution.py:141
  43.4 4.5 %collective-permute-start.3 = (bf16[128,32,128]{2,1,0:T(8,128)(2,1)S(1)}, bf16[128,32,128]{2,1,0:T(8,128)(2,1)S(1)}, u32[]{:S(2)}, u32[]{:S(2)}) collective-permute-start(bf16[128,32,128]{2,1,0:T(8,128)(2,1)S(1)} %constant_dynamic-update-slice_fusion.pair), channel_id=1, source_target_pairs={{0,32},{4,36},{8,40},{12,44},{16,48},{20,52},{24,56},{28,60},{32,0... | collective-permute-start | bytes 3145736 | tf_op jit(solution)/shard_map/ppermute | solution.py:30
  45.3 23.7 %collective-permute-start.4 = (bf16[128,32,128]{2,1,0:T(8,128)(2,1)S(1)}, bf16[128,32,128]{2,1,0:T(8,128)(2,1)}, u32[]{:S(2)}, u32[]{:S(2)}) collective-permute-start(bf16[128,32,128]{2,1,0:T(8,128)(2,1)S(1)} %collective-permute-done.2.far), channel_id=1, source_target_pairs={{0,32},{4,36},{8,40},{12,44},{16,48},{20,52},{24,56},{28,60},{32,0... | collective-permute-start | bytes 3145736 | tf_op jit(solution)/shard_map/ppermute | solution.py:30
  47.9 1.0 %copy-start = (bf16[128,32,128]{2,1,0:T(8,128)(2,1)}, bf16[128,32,128]{2,1,0:T(8,128)(2,1)S(1)}, u32[]{:S(2)}) copy-start(bf16[128,32,128]{2,1,0:T(8,128)(2,1)S(1)} %collective-permute-done.3.twin_pair) | copy-start | bytes 3145732
  69.1 1.2 %copy-start.1 = (bf16[128,32,128]{2,1,0:T(8,128)(2,1)S(1)}, bf16[128,32,128]{2,1,0:T(8,128)(2,1)}, u32[]{:S(2)}) copy-start(bf16[128,32,128]{2,1,0:T(8,128)(2,1)} %copy-done) | copy-start | bytes 3145732

commit v4 on v3

--- a/solution.py
+++ b/solution.py
@@ -39,6 +39,19 @@
         if core == turn:
             return x, z ^ 1, core, y
         return x, (z + 1 if z % 2 else z - 1), core, y
+
+    return move
+
+
+def neighbour(y, turn):
+    return (y ^ 1 if turn == 0 else ((y + 1) ^ 1) - 1) & (NY - 1)
+
+
+def along_y(*turns):
+    def move(x, z, core, y):
+        for turn in turns:
+            y = neighbour(y, turn ^ core)
+        return x, z, core, y
 
     return move
 
@@ -77,9 +90,11 @@
 
 
 def product_kernel(
-    place_ref, shifts_ref, masks, left, pair, far, twin_pair, twin_far, out, right, sems
+    place_ref, shifts_ref, masks, left_pair, left_far, left_back, left_on, pair, far, twin_pair, twin_far,
+    out, left, right, sems,
 ):
     row = place_ref[0]
+    col = place_ref[1]
     layer = place_ref[2]
     core = row & 1
     zl = (row >> 1) & 3
@@ -95,6 +110,18 @@
     for n, (piece, half, turn, parity) in enumerate(pieces):
         slot = (zl ^ turn) * 2 + parity
         copies.append(pltpu.make_async_copy(piece.at[pl.ds(half * RANGE, RANGE)], right.at[slot], sems.at[n]))
+    def turned(*turns):
+        y = col
+        for turn in turns:
+            y = jnp.where(core == turn, y ^ 1, ((y + 1) ^ 1) - 1) & (NY - 1)
+        return y
+
+    lefts = [(left_pair, turned(), turned(0)), (left_far, turned(1), turned(1, 0))]
+    lefts += [(left_back, turned(0, 1), turned(0, 1, 0)), (left_on, turned(1, 0, 1), turned(1, 0, 1, 0))]
+    for n, (piece, *slots) in enumerate(lefts):
+        for half, slot in enumerate(slots):
+            from_piece = piece.at[pl.ds(half * SPAN, SPAN)]
+            copies.append(pltpu.make_async_copy(from_piece, left.at[slot], sems.at[NEAR + 2 * n + half]))
     for copy in copies:
         copy.start()
     for copy in copies:
@@ -138,23 +165,30 @@
     )(place, shifts)
     near = sent(x_blocks, along_z(0))
     near, masks, mine = lax.optimization_barrier((near, masks, mine))
-    left = lax.all_to_all(jnp.broadcast_to(mine[None], (NY, SPAN, BS, LANES)), "col", 0, 0)
+    left_next = sent(mine, along_y(0))
     pair = jnp.concatenate([x_blocks, near], axis=0)
     far = sent(pair, along_z(1))
+    pair, left_next = lax.optimization_barrier((pair, left_next))
+    left_pair = jnp.concatenate([mine, left_next], axis=0)
+    left_far = sent(left_pair, along_y(1))
+    left_back = sent(left_far, along_y(0))
+    left_on = sent(left_far, along_y(0, 1))
     twin_pair = sent(pair, other_core)
+    far, left_pair = lax.optimization_barrier((far, left_pair))
     twin_far = sent(far, other_core)
     parts = pl.pallas_call(
         product_kernel,
         out_shape=jax.ShapeDtypeStruct((NX, SPAN, BS, LANES), jnp.float32),
-        in_specs=[smem, smem] + [vmem] * 2 + [anywhere] * 4,
+        in_specs=[smem, smem] + [vmem] + [anywhere] * 8,
         out_specs=vmem,
         scratch_shapes=[
+            pltpu.VMEM((NY, SPAN, BS, LANES), jnp.bfloat16),
             pltpu.VMEM((NEAR, RANGE, BS, LANES), jnp.bfloat16),
-            pltpu.SemaphoreType.DMA((NEAR,)),
+            pltpu.SemaphoreType.DMA((NEAR + NY,)),
         ],
         compiler_params=pltpu.CompilerParams(vmem_limit_bytes=20 * 1024 * 1024),
         name="range_products",
-    )(place, shifts, masks, left, pair, far, twin_pair, twin_far)
+    )(place, shifts, masks, left_pair, left_far, left_back, left_on, pair, far, twin_pair, twin_far)
     return jnp.sum(swapped_along_x(parts), axis=0).astype(jnp.bfloat16)
 
 

time: 92.5 us -> 99.3 us (1.074)
  the two profiles are of different devices: /device:TPU:2 before, /device:TPU:1 now
where the time goes in v4:
time: 99.3 us; the launch traced here: 98.8 us
  starting transfers between devices  50.3 us (51%)
  waiting for transfers between devices  18.8 us (19%)
  blocking collectives  18.4 us (19%)
  Pallas kernels  8.61 us (9%)
  other arithmetic  1.35 us (1%)
  local copies, waits for them, and re-layouts  1.07 us (1%)
    ppermute x9, starting transfers between devices, sent(): return lax.ppermute(value, AXES, device_pairs(move))  50.3 us
    ppermute x9, waiting for transfers between devices, sent(): return lax.ppermute(value, AXES, device_pairs(move))  18.8 us
    all_to_all x1, blocking collectives, swapped_along_x(): return lax.all_to_all(value, 'row', 0, 0, axis_index_groups=groups)  18.4 us
    pallas_call x1, Pallas kernels, local(): pl.pallas_call(product_kernel, out_shape=jax.ShapeDtypeStruct((NX, SPAN,...  6.37 us
    pallas_call x1, Pallas kernels, local(): pl.pallas_call(mask_kernel, out_shape=jax.ShapeDtypeStruct((NX, NEAR, BS,...  2.24 us
  transfers between devices with their start and end apart: 9, of which 6 were waited for; matrix products, arithmetic and copies ran while one was open for 2% of the time, Pallas kernels for 2%

profile of v4, /device:TPU:1, one launch (start us, length us, event | category | flops | bytes accessed | tf_op | source)
XLA Modules:
  0.0 98.8 jit_solution(2326559118464315758)
XLA Ops:
  0.0 18.9 %collective-permute-start = (bf16[64,32,128]{2,1,0:T(8,128)(2,1)}, bf16[64,32,128]{2,1,0:T(8,128)(2,1)S(1)}, u32[]{:S(2)}, u32[]{:S(2)}) collective-permute-start(bf16[64,32,128]{2,1,0:T(8,128)(2,1)} %param.2), channel_id=1, source_target_pairs={{0,64},{4,68},{8,72},{12,76},{16,80},{20,84},{24,88},{28,92},{32,2... | collective-permute-start | bytes 1572872 | tf_op jit(solution)/shard_map/ppermute | solution.py:30
  18.9 0.9 constant_dynamic-slice_fusion
  19.8 0.7 collective-permute-start.1
  20.5 0.6 pad_add_fusion.place_ref
  21.1 2.2 %masks.1 = bf16[4,8,32,128]{3,2,1,0:T(8,128)(2,1)} custom-call(s32[3]{0:T(128)} %pad_add_fusion.place_ref, s32[32,32]{1,0:T(8,128)} %shifts_ref.3), custom_call_target="tpu_custom_call" | custom-call | tf_op jit(solution)/shard_map/masks/pallas_call | solution.py:159
  23.4 2.3 %collective-permute-done = bf16[64,32,128]{2,1,0:T(8,128)(2,1)S(1)} collective-permute-done((bf16[64,32,128]{2,1,0:T(8,128)(2,1)}, bf16[64,32,128]{2,1,0:T(8,128)(2,1)S(1)}, u32[]{:S(2)}, u32[]{:S(2)}) %collective-permute-start) | collective-permute-done | bytes 524320 | tf_op jit(solution)/shard_map/ppermute | solution.py:30
  25.7 0.1 constant_dynamic-update-slice_fusion.pair
  25.8 2.1 %collective-permute-start.2 = (bf16[128,32,128]{2,1,0:T(8,128)(2,1)S(1)}, bf16[128,32,128]{2,1,0:T(8,128)(2,1)S(1)}, u32[]{:S(2)}, u32[]{:S(2)}) collective-permute-start(bf16[128,32,128]{2,1,0:T(8,128)(2,1)S(1)} %constant_dynamic-update-slice_fusion.pair), channel_id=1, source_target_pairs={{0,195},{4,199},{8,203},{12,207},{16,211},{20,215},{24,219},{28,22... | collective-permute-start | bytes 3145736 | tf_op jit(solution)/shard_map/ppermute | solution.py:30
  27.8 7.1 %collective-permute-start.3 = (bf16[16,32,128]{2,1,0:T(8,128)(2,1)S(1)}, bf16[16,32,128]{2,1,0:T(8,128)(2,1)S(1)}, u32[]{:S(2)}, u32[]{:S(2)}) collective-permute-start(bf16[16,32,128]{2,1,0:T(8,128)(2,1)S(1)} %collective-permute-done.1), channel_id=1, source_target_pairs={{0,4},{4,0},{8,12},{12,8},{16,20},{20,16},{24,28},{28,24},{32,60},... | collective-permute-start | bytes 393224 | tf_op jit(solution)/shard_map/ppermute | solution.py:30
  34.9 0.0 copy-start.1
  34.9 2.6 %collective-permute-done.3 = bf16[16,32,128]{2,1,0:T(8,128)(2,1)S(1)} collective-permute-done((bf16[16,32,128]{2,1,0:T(8,128)(2,1)S(1)}, bf16[16,32,128]{2,1,0:T(8,128)(2,1)S(1)}, u32[]{:S(2)}, u32[]{:S(2)}) %collective-permute-start.3) | collective-permute-done | bytes 131104 | tf_op jit(solution)/shard_map/ppermute | solution.py:30
  37.5 2.6 %collective-permute-start.7 = (bf16[128,32,128]{2,1,0:T(8,128)(2,1)S(1)}, bf16[128,32,128]{2,1,0:T(8,128)(2,1)S(1)}, u32[]{:S(2)}, u32[]{:S(2)}) collective-permute-start(bf16[128,32,128]{2,1,0:T(8,128)(2,1)S(1)} %constant_dynamic-update-slice_fusion.pair), channel_id=1, source_target_pairs={{0,32},{4,36},{8,40},{12,44},{16,48},{20,52},{24,56},{28,60},{32,0... | collective-permute-start | bytes 3145736 | tf_op jit(solution)/shard_map/ppermute | solution.py:30
  40.2 1.6 %collective-permute-done.2.far = bf16[128,32,128]{2,1,0:T(8,128)(2,1)S(1)} collective-permute-done((bf16[128,32,128]{2,1,0:T(8,128)(2,1)S(1)}, bf16[128,32,128]{2,1,0:T(8,128)(2,1)S(1)}, u32[]{:S(2)}, u32[]{:S(2)}) %collective-permute-start.2) | collective-permute-done | bytes 1048608 | tf_op jit(solution)/shard_map/ppermute | solution.py:30
  41.7 4.3 %collective-permute-start.8 = (bf16[128,32,128]{2,1,0:T(8,128)(2,1)S(1)}, bf16[128,32,128]{2,1,0:T(8,128)(2,1)S(1)}, u32[]{:S(2)}, u32[]{:S(2)}) collective-permute-start(bf16[128,32,128]{2,1,0:T(8,128)(2,1)S(1)} %collective-permute-done.2.far), channel_id=1, source_target_pairs={{0,32},{4,36},{8,40},{12,44},{16,48},{20,52},{24,56},{28,60},{32,0... | collective-permute-start | bytes 3145736 | tf_op jit(solution)/shard_map/ppermute | solution.py:30
  46.0 3.2 %collective-permute-start.4 = (bf16[32,32,128]{2,1,0:T(8,128)(2,1)S(1)}, bf16[32,32,128]{2,1,0:T(8,128)(2,1)S(1)}, u32[]{:S(2)}, u32[]{:S(2)}) collective-permute-start(bf16[32,32,128]{2,1,0:T(8,128)(2,1)S(1)} %constant_dynamic-update-slice_fusion.2.left_pair), channel_id=1, source_target_pairs={{0,28},{4,8},{8,4},{12,16},{16,12},{20,24},{24,20},{28,0},{32,36},... | collective-permute-start | bytes 786440 | tf_op jit(solution)/shard_map/ppermute | solution.py:30
  49.2 3.9 %collective-permute-done.4.left_far = bf16[32,32,128]{2,1,0:T(8,128)(2,1)S(1)} collective-permute-done((bf16[32,32,128]{2,1,0:T(8,128)(2,1)S(1)}, bf16[32,32,128]{2,1,0:T(8,128)(2,1)S(1)}, u32[]{:S(2)}, u32[]{:S(2)}) %collective-permute-start.4) | collective-permute-done | bytes 262176 | tf_op jit(solution)/shard_map/ppermute | solution.py:30
  53.1 9.7 %collective-permute-start.6 = (bf16[32,32,128]{2,1,0:T(8,128)(2,1)S(1)}, bf16[32,32,128]{2,1,0:T(8,128)(2,1)S(1)}, u32[]{:S(2)}, u32[]{:S(2)}) collective-permute-start(bf16[32,32,128]{2,1,0:T(8,128)(2,1)S(1)} %collective-permute-done.4.left_far), channel_id=1, source_target_pairs={{0,8},{4,28},{8,16},{12,4},{16,24},{20,12},{24,0},{28,20},{32,56},... | collective-permute-start | bytes 786440 | tf_op jit(solution)/shard_map/ppermute | solution.py:30
  62.8 1.9 %collective-permute-start.5 = (bf16[32,32,128]{2,1,0:T(8,128)(2,1)S(1)}, bf16[32,32,128]{2,1,0:T(8,128)(2,1)S(1)}, u32[]{:S(2)}, u32[]{:S(2)}) collective-permute-start(bf16[32,32,128]{2,1,0:T(8,128)(2,1)S(1)} %collective-permute-done.4.left_far), channel_id=1, source_target_pairs={{0,4},{4,0},{8,12},{12,8},{16,20},{20,16},{24,28},{28,24},{32,60},... | collective-permute-start | bytes 786440 | tf_op jit(solution)/shard_map/ppermute | solution.py:30
  64.7 4.2 %collective-permute-done.6.left_on = bf16[32,32,128]{2,1,0:T(8,128)(2,1)S(1)} collective-permute-done((bf16[32,32,128]{2,1,0:T(8,128)(2,1)S(1)}, bf16[32,32,128]{2,1,0:T(8,128)(2,1)S(1)}, u32[]{:S(2)}, u32[]{:S(2)}) %collective-permute-start.6) | collective-permute-done | bytes 262176 | tf_op jit(solution)/shard_map/ppermute | solution.py:30
  68.9 4.3 %collective-permute-done.5.left_back = bf16[32,32,128]{2,1,0:T(8,128)(2,1)S(1)} collective-permute-done((bf16[32,32,128]{2,1,0:T(8,128)(2,1)S(1)}, bf16[32,32,128]{2,1,0:T(8,128)(2,1)S(1)}, u32[]{:S(2)}, u32[]{:S(2)}) %collective-permute-start.5) | collective-permute-done | bytes 262176 | tf_op jit(solution)/shard_map/ppermute | solution.py:30
  73.2 0.0 collective-permute-done.7.twin_pair
  73.2 6.4 %range_products.1 = f32[4,16,32,128]{3,2,1,0:T(8,128)S(1)} custom-call(s32[3]{0:T(128)S(1)} %copy-done.2, s32[32,32]{1,0:T(8,128)S(1)} %copy-done.1, bf16[4,8,32,128]{3,2,1,0:T(8,128)(2,1)S(1)} %copy-done, bf16[32,32,128]{2,1,0:T(8,128)(2,1)S(1)} %constant_dynamic-update-slice_fusion.2.left_pair, bf16[32,32,128]{2,1,0:T(8,128)(2,1)S(1)} %collective-permute-done.4.left_far, ...), custom_call_target="tpu_custom_call" | custom-call | tf_op jit(solution)/shard_map/range_products/pallas_call | solution.py:179
  79.6 18.4 %all_to_all.5 = f32[4,16,32,128]{3,2,1,0:T(8,128)S(1)} all-to-all(f32[4,16,32,128]{3,2,1,0:T(8,128)S(1)} %range_products.1), channel_id=1, replica_groups={{0,256,512,768},{32,288,544,800},{64,320,576,832},{96,352,608,864},{128..., dimensions={0} | all-to-all | bytes 2097152 | tf_op jit(solution)/shard_map/all_to_all | solution.py:67
  98.0 0.8 reduce_sum.9
  (12 shorter events, 0.1 us)
Async XLA Ops:
  0.0 23.3 %copy-start.3 = (bf16[64,32,128]{2,1,0:T(8,128)(2,1)S(1)}, bf16[64,32,128]{2,1,0:T(8,128)(2,1)}, u32[]{:S(2)}) copy-start(bf16[64,32,128]{2,1,0:T(8,128)(2,1)} %param.2) | copy-start | bytes 1572868
  0.0 25.7 %collective-permute-start = (bf16[64,32,128]{2,1,0:T(8,128)(2,1)}, bf16[64,32,128]{2,1,0:T(8,128)(2,1)S(1)}, u32[]{:S(2)}, u32[]{:S(2)}) collective-permute-start(bf16[64,32,128]{2,1,0:T(8,128)(2,1)} %param.2), channel_id=1, source_target_pairs={{0,64},{4,68},{8,72},{12,76},{16,80},{20,84},{24,88},{28,92},{32,2... | collective-permute-start | bytes 1572872 | tf_op jit(solution)/shard_map/ppermute | solution.py:30
  19.8 3.6 %collective-permute-start.1 = (bf16[16,32,128]{2,1,0:T(8,128)(2,1)S(1)}, bf16[16,32,128]{2,1,0:T(8,128)(2,1)S(1)}, u32[]{:S(2)}, u32[]{:S(2)}) collective-permute-start(bf16[16,32,128]{2,1,0:T(8,128)(2,1)S(1)} %constant_dynamic-slice_fusion), channel_id=1, source_target_pairs={{0,0},{4,4},{8,284},{12,280},{16,520},{20,540},{24,788},{28,768},{... | collective-permute-start | bytes 393224 | tf_op jit(solution)/shard_map/ppermute | solution.py:30
  25.7 47.5 %copy-start = (bf16[4,8,32,128]{3,2,1,0:T(8,128)(2,1)S(1)}, bf16[4,8,32,128]{3,2,1,0:T(8,128)(2,1)}, u32[]{:S(2)}) copy-start(bf16[4,8,32,128]{3,2,1,0:T(8,128)(2,1)} %masks.1) | copy-start | bytes 786436
  25.8 16.0 %collective-permute-start.2 = (bf16[128,32,128]{2,1,0:T(8,128)(2,1)S(1)}, bf16[128,32,128]{2,1,0:T(8,128)(2,1)S(1)}, u32[]{:S(2)}, u32[]{:S(2)}) collective-permute-start(bf16[128,32,128]{2,1,0:T(8,128)(2,1)S(1)} %constant_dynamic-update-slice_fusion.pair), channel_id=1, source_target_pairs={{0,195},{4,199},{8,203},{12,207},{16,211},{20,215},{24,219},{28,22... | collective-permute-start | bytes 3145736 | tf_op jit(solution)/shard_map/ppermute | solution.py:30
  27.8 9.7 %collective-permute-start.3 = (bf16[16,32,128]{2,1,0:T(8,128)(2,1)S(1)}, bf16[16,32,128]{2,1,0:T(8,128)(2,1)S(1)}, u32[]{:S(2)}, u32[]{:S(2)}) collective-permute-start(bf16[16,32,128]{2,1,0:T(8,128)(2,1)S(1)} %collective-permute-done.1), channel_id=1, source_target_pairs={{0,4},{4,0},{8,12},{12,8},{16,20},{20,16},{24,28},{28,24},{32,60},... | collective-permute-start | bytes 393224 | tf_op jit(solution)/shard_map/ppermute | solution.py:30
  34.9 38.3 %copy-start.1 = (s32[32,32]{1,0:T(8,128)S(1)}, s32[32,32]{1,0:T(8,128)}, u32[]{:S(2)}) copy-start(s32[32,32]{1,0:T(8,128)} %shifts_ref.3) | copy-start | bytes 12292
  34.9 38.3 %copy-start.2 = (s32[3]{0:T(128)S(1)}, s32[3]{0:T(128)}, u32[]{:S(2)}) copy-start(s32[3]{0:T(128)} %pad_add_fusion.place_ref) | copy-start | bytes 40
  37.5 35.7 %collective-permute-start.7 = (bf16[128,32,128]{2,1,0:T(8,128)(2,1)S(1)}, bf16[128,32,128]{2,1,0:T(8,128)(2,1)S(1)}, u32[]{:S(2)}, u32[]{:S(2)}) collective-permute-start(bf16[128,32,128]{2,1,0:T(8,128)(2,1)S(1)} %constant_dynamic-update-slice_fusion.pair), channel_id=1, source_target_pairs={{0,32},{4,36},{8,40},{12,44},{16,48},{20,52},{24,56},{28,60},{32,0... | collective-permute-start | bytes 3145736 | tf_op jit(solution)/shard_map/ppermute | solution.py:30
  41.7 31.5 %collective-permute-start.8 = (bf16[128,32,128]{2,1,0:T(8,128)(2,1)S(1)}, bf16[128,32,128]{2,1,0:T(8,128)(2,1)S(1)}, u32[]{:S(2)}, u32[]{:S(2)}) collective-permute-start(bf16[128,32,128]{2,1,0:T(8,128)(2,1)S(1)} %collective-permute-done.2.far), channel_id=1, source_target_pairs={{0,32},{4,36},{8,40},{12,44},{16,48},{20,52},{24,56},{28,60},{32,0... | collective-permute-start | bytes 3145736 | tf_op jit(solution)/shard_map/ppermute | solution.py:30
  46.0 7.1 %collective-permute-start.4 = (bf16[32,32,128]{2,1,0:T(8,128)(2,1)S(1)}, bf16[32,32,128]{2,1,0:T(8,128)(2,1)S(1)}, u32[]{:S(2)}, u32[]{:S(2)}) collective-permute-start(bf16[32,32,128]{2,1,0:T(8,128)(2,1)S(1)} %constant_dynamic-update-slice_fusion.2.left_pair), channel_id=1, source_target_pairs={{0,28},{4,8},{8,4},{12,16},{16,12},{20,24},{24,20},{28,0},{32,36},... | collective-permute-start | bytes 786440 | tf_op jit(solution)/shard_map/ppermute | solution.py:30
  53.1 15.8 %collective-permute-start.6 = (bf16[32,32,128]{2,1,0:T(8,128)(2,1)S(1)}, bf16[32,32,128]{2,1,0:T(8,128)(2,1)S(1)}, u32[]{:S(2)}, u32[]{:S(2)}) collective-permute-start(bf16[32,32,128]{2,1,0:T(8,128)(2,1)S(1)} %collective-permute-done.4.left_far), channel_id=1, source_target_pairs={{0,8},{4,28},{8,16},{12,4},{16,24},{20,12},{24,0},{28,20},{32,56},... | collective-permute-start | bytes 786440 | tf_op jit(solution)/shard_map/ppermute | solution.py:30
  62.8 10.4 %collective-permute-start.5 = (bf16[32,32,128]{2,1,0:T(8,128)(2,1)S(1)}, bf16[32,32,128]{2,1,0:T(8,128)(2,1)S(1)}, u32[]{:S(2)}, u32[]{:S(2)}) collective-permute-start(bf16[32,32,128]{2,1,0:T(8,128)(2,1)S(1)} %collective-permute-done.4.left_far), channel_id=1, source_target_pairs={{0,4},{4,0},{8,12},{12,8},{16,20},{20,16},{24,28},{28,24},{32,60},... | collective-permute-start | bytes 786440 | tf_op jit(solution)/shard_map/ppermute | solution.py:30

commit v5 on v4

--- a/solution.py
+++ b/solution.py
@@ -90,7 +90,7 @@
 
 
 def product_kernel(
-    place_ref, shifts_ref, masks, left_pair, left_far, left_back, left_on, pair, far, twin_pair, twin_far,
+    place_ref, shifts_ref, masks, left_pair, left_far, left_back, left_on, near_blocks, twin_blocks,
     out, left, right, sems,
 ):
     row = place_ref[0]
@@ -103,9 +103,8 @@
 
     first = jnp.where(core == 0, 1, 3)
     second = jnp.where(core == 0, 3, 1)
-    pieces = [(pair, 0, 0, core), (pair, 1, first, core), (far, 0, second, core), (far, 1, 2, core)]
-    pieces += [(twin_pair, 0, 0, 1 - core), (twin_pair, 1, second, 1 - core)]
-    pieces += [(twin_far, 0, first, 1 - core), (twin_far, 1, 2, 1 - core)]
+    pieces = [(near_blocks, n, turn, core) for n, turn in enumerate((0, first, second, 2))]
+    pieces += [(twin_blocks, n, turn, 1 - core) for n, turn in enumerate((0, second, first, 2))]
     copies = []
     for n, (piece, half, turn, parity) in enumerate(pieces):
         slot = (zl ^ turn) * 2 + parity
@@ -168,27 +167,26 @@
     left_next = sent(mine, along_y(0))
     pair = jnp.concatenate([x_blocks, near], axis=0)
     far = sent(pair, along_z(1))
-    pair, left_next = lax.optimization_barrier((pair, left_next))
     left_pair = jnp.concatenate([mine, left_next], axis=0)
     left_far = sent(left_pair, along_y(1))
+    far, left_far = lax.optimization_barrier((far, left_far))
     left_back = sent(left_far, along_y(0))
     left_on = sent(left_far, along_y(0, 1))
-    twin_pair = sent(pair, other_core)
-    far, left_pair = lax.optimization_barrier((far, left_pair))
-    twin_far = sent(far, other_core)
+    right = jnp.concatenate([pair, far], axis=0)
+    twin = sent(right, other_core)
     parts = pl.pallas_call(
         product_kernel,
         out_shape=jax.ShapeDtypeStruct((NX, SPAN, BS, LANES), jnp.float32),
-        in_specs=[smem, smem] + [vmem] + [anywhere] * 8,
+        in_specs=[smem, smem] + [vmem] + [anywhere] * 6,
         out_specs=vmem,
         scratch_shapes=[
             pltpu.VMEM((NY, SPAN, BS, LANES), jnp.bfloat16),
             pltpu.VMEM((NEAR, RANGE, BS, LANES), jnp.bfloat16),
             pltpu.SemaphoreType.DMA((NEAR + NY,)),
         ],
-        compiler_params=pltpu.CompilerParams(vmem_limit_bytes=20 * 1024 * 1024),
+        compiler_params=pltpu.CompilerParams(vmem_limit_bytes=12 * 1024 * 1024),
         name="range_products",
-    )(place, shifts, masks, left_pair, left_far, left_back, left_on, pair, far, twin_pair, twin_far)
+    )(place, shifts, masks, left_pair, left_far, left_back, left_on, right, twin)
     return jnp.sum(swapped_along_x(parts), axis=0).astype(jnp.bfloat16)
 
 

time: 99.3 us -> 97.5 us (0.982)
  starting transfers between devices: 50.3 us -> 47.6 us
  waiting for transfers between devices: 18.8 us -> 16.9 us
  blocking collectives: 18.4 us -> 20 us
  other arithmetic: 1.35 us -> 2.56 us
    ppermute x9 -> x8, starting transfers between devices: 50.3 us -> 47.6 us  [sent(): return lax.ppermute(value, AXES, device_pairs(move))]
    ppermute x9 -> x8, waiting for transfers between devices: 18.8 us -> 16.9 us  [sent(): return lax.ppermute(value, AXES, device_pairs(move))]
    all_to_all x1, blocking collectives: 18.4 us -> 20 us  [swapped_along_x(): return lax.all_to_all(value, 'row', 0, 0, axis_index_groups=groups)]
    concatenate x0 -> x1, other arithmetic: none -> 1.13 us  [local(): pair = jnp.concatenate([x_blocks, near], axis=0)]
  transfers between devices with their start and end apart: 9 -> 8, of which waited for: 6 -> 4; matrix products, arithmetic and copies ran while one was open for 2% -> 2% of each run, Pallas kernels for 2% -> 2%
where the time goes in v5:
time: 97.5 us; the launch traced here: 97 us
  starting transfers between devices  47.6 us (49%)
  blocking collectives  20 us (21%)
  waiting for transfers between devices  16.9 us (17%)
  Pallas kernels  8.52 us (9%)
  other arithmetic  2.56 us (3%)
  local copies, waits for them, and re-layouts  1.21 us (1%)
    ppermute x8, starting transfers between devices, sent(): return lax.ppermute(value, AXES, device_pairs(move))  47.6 us
    all_to_all x1, blocking collectives, swapped_along_x(): return lax.all_to_all(value, 'row', 0, 0, axis_index_groups=groups)  20 us
    ppermute x8, waiting for transfers between devices, sent(): return lax.ppermute(value, AXES, device_pairs(move))  16.9 us
    pallas_call x1, Pallas kernels, local(): pl.pallas_call(product_kernel, out_shape=jax.ShapeDtypeStruct((NX, SPAN,...  6.3 us
    pallas_call x1, Pallas kernels, local(): pl.pallas_call(mask_kernel, out_shape=jax.ShapeDtypeStruct((NX, NEAR, BS,...  2.23 us
  transfers between devices with their start and end apart: 8, of which 4 were waited for; matrix products, arithmetic and copies ran while one was open for 2% of the time, Pallas kernels for 2%

profile of v5, /device:TPU:1, one launch (start us, length us, event | category | flops | bytes accessed | tf_op | source)
XLA Modules:
  0.0 97.0 jit_solution(8227678345519939773)
XLA Ops:
  0.0 18.9 %collective-permute-start = (bf16[64,32,128]{2,1,0:T(8,128)(2,1)}, bf16[64,32,128]{2,1,0:T(8,128)(2,1)S(1)}, u32[]{:S(2)}, u32[]{:S(2)}) collective-permute-start(bf16[64,32,128]{2,1,0:T(8,128)(2,1)} %param.2), channel_id=1, source_target_pairs={{0,64},{4,68},{8,72},{12,76},{16,80},{20,84},{24,88},{28,92},{32,2... | collective-permute-start | bytes 1572872 | tf_op jit(solution)/shard_map/ppermute | solution.py:30
  18.9 0.9 constant_dynamic-slice_fusion
  19.8 0.7 collective-permute-start.1
  20.5 0.7 pad_add_fusion.place_ref
  21.2 2.2 %masks.1 = bf16[4,8,32,128]{3,2,1,0:T(8,128)(2,1)} custom-call(s32[3]{0:T(128)} %pad_add_fusion.place_ref, s32[32,32]{1,0:T(8,128)} %shifts_ref.3), custom_call_target="tpu_custom_call" | custom-call | tf_op jit(solution)/shard_map/masks/pallas_call | solution.py:158
  23.4 0.0 collective-permute-done.1
  23.4 2.3 %collective-permute-done = bf16[64,32,128]{2,1,0:T(8,128)(2,1)S(1)} collective-permute-done((bf16[64,32,128]{2,1,0:T(8,128)(2,1)}, bf16[64,32,128]{2,1,0:T(8,128)(2,1)S(1)}, u32[]{:S(2)}, u32[]{:S(2)}) %collective-permute-start) | collective-permute-done | bytes 524320 | tf_op jit(solution)/shard_map/ppermute | solution.py:30
  25.7 1.1 %pad_maximum_fusion = bf16[128,32,128]{2,1,0:T(8,128)(2,1)S(1)} fusion(bf16[64,32,128]{2,1,0:T(8,128)(2,1)S(1)} %collective-permute-done, bf16[64,32,128]{2,1,0:T(8,128)(2,1)} %param.2), kind=kLoop, calls=%fused_computation | loop fusion | flops 524288 | bytes 2097152 | tf_op jit(solution)/shard_map/concatenate | solution.py:168
  26.8 1.9 %collective-permute-start.3 = (bf16[128,32,128]{2,1,0:T(8,128)(2,1)S(1)}, bf16[128,32,128]{2,1,0:T(8,128)(2,1)S(1)}, u32[]{:S(2)}, u32[]{:S(2)}) collective-permute-start(bf16[128,32,128]{2,1,0:T(8,128)(2,1)S(1)} %pad_maximum_fusion), channel_id=1, source_target_pairs={{0,195},{4,199},{8,203},{12,207},{16,211},{20,215},{24,219},{28,22... | collective-permute-start | bytes 3145736 | tf_op jit(solution)/shard_map/ppermute | solution.py:30
  28.7 7.1 %collective-permute-start.2 = (bf16[16,32,128]{2,1,0:T(8,128)(2,1)S(1)}, bf16[16,32,128]{2,1,0:T(8,128)(2,1)S(1)}, u32[]{:S(2)}, u32[]{:S(2)}) collective-permute-start(bf16[16,32,128]{2,1,0:T(8,128)(2,1)S(1)} %collective-permute-done.1), channel_id=1, source_target_pairs={{0,4},{4,0},{8,12},{12,8},{16,20},{20,16},{24,28},{28,24},{32,60},... | collective-permute-start | bytes 393224 | tf_op jit(solution)/shard_map/ppermute | solution.py:30
  35.8 2.6 %collective-permute-done.2 = bf16[16,32,128]{2,1,0:T(8,128)(2,1)S(1)} collective-permute-done((bf16[16,32,128]{2,1,0:T(8,128)(2,1)S(1)}, bf16[16,32,128]{2,1,0:T(8,128)(2,1)S(1)}, u32[]{:S(2)}, u32[]{:S(2)}) %collective-permute-start.2) | collective-permute-done | bytes 131104 | tf_op jit(solution)/shard_map/ppermute | solution.py:30
  38.5 0.0 copy-start.1
  38.5 2.3 %collective-permute-start.4 = (bf16[32,32,128]{2,1,0:T(8,128)(2,1)S(1)}, bf16[32,32,128]{2,1,0:T(8,128)(2,1)S(1)}, u32[]{:S(2)}, u32[]{:S(2)}) collective-permute-start(bf16[32,32,128]{2,1,0:T(8,128)(2,1)S(1)} %constant_dynamic-update-slice_fusion.left_pair), channel_id=1, source_target_pairs={{0,28},{4,8},{8,4},{12,16},{16,12},{20,24},{24,20},{28,0},{32,36},... | collective-permute-start | bytes 786440 | tf_op jit(solution)/shard_map/ppermute | solution.py:30
  40.9 0.1 constant_dynamic-update-slice_fusion.3
  41.0 4.8 %collective-permute-done.4.left_far = bf16[32,32,128]{2,1,0:T(8,128)(2,1)S(1)} collective-permute-done((bf16[32,32,128]{2,1,0:T(8,128)(2,1)S(1)}, bf16[32,32,128]{2,1,0:T(8,128)(2,1)S(1)}, u32[]{:S(2)}, u32[]{:S(2)}) %collective-permute-start.4) | collective-permute-done | bytes 262176 | tf_op jit(solution)/shard_map/ppermute | solution.py:30
  45.8 0.0 collective-permute-done.3
  45.8 0.1 constant_dynamic-update-slice_fusion.2.near_blocks
  45.9 8.0 %collective-permute-start.7 = (bf16[256,32,128]{2,1,0:T(8,128)(2,1)S(1)}, bf16[256,32,128]{2,1,0:T(8,128)(2,1)S(1)}, u32[]{:S(2)}, u32[]{:S(2)}) collective-permute-start(bf16[256,32,128]{2,1,0:T(8,128)(2,1)S(1)} %constant_dynamic-update-slice_fusion.2.near_blocks), channel_id=1, source_target_pairs={{0,32},{4,36},{8,40},{12,44},{16,48},{20,52},{24,56},{28,60},{32,0... | collective-permute-start | bytes 6291464 | tf_op jit(solution)/shard_map/ppermute | solution.py:30
  53.9 4.9 %collective-permute-start.5 = (bf16[32,32,128]{2,1,0:T(8,128)(2,1)S(1)}, bf16[32,32,128]{2,1,0:T(8,128)(2,1)S(1)}, u32[]{:S(2)}, u32[]{:S(2)}) collective-permute-start(bf16[32,32,128]{2,1,0:T(8,128)(2,1)S(1)} %collective-permute-done.4.left_far), channel_id=1, source_target_pairs={{0,4},{4,0},{8,12},{12,8},{16,20},{20,16},{24,28},{28,24},{32,60},... | collective-permute-start | bytes 786440 | tf_op jit(solution)/shard_map/ppermute | solution.py:30
  58.8 3.8 %collective-permute-start.6 = (bf16[32,32,128]{2,1,0:T(8,128)(2,1)S(1)}, bf16[32,32,128]{2,1,0:T(8,128)(2,1)S(1)}, u32[]{:S(2)}, u32[]{:S(2)}) collective-permute-start(bf16[32,32,128]{2,1,0:T(8,128)(2,1)S(1)} %collective-permute-done.4.left_far), channel_id=1, source_target_pairs={{0,8},{4,28},{8,16},{12,4},{16,24},{20,12},{24,0},{28,20},{32,56},... | collective-permute-start | bytes 786440 | tf_op jit(solution)/shard_map/ppermute | solution.py:30
  62.6 7.3 %collective-permute-done.6.left_on = bf16[32,32,128]{2,1,0:T(8,128)(2,1)S(1)} collective-permute-done((bf16[32,32,128]{2,1,0:T(8,128)(2,1)S(1)}, bf16[32,32,128]{2,1,0:T(8,128)(2,1)S(1)}, u32[]{:S(2)}, u32[]{:S(2)}) %collective-permute-start.6) | collective-permute-done | bytes 262176 | tf_op jit(solution)/shard_map/ppermute | solution.py:30
  69.9 6.3 %range_products.1 = f32[4,16,32,128]{3,2,1,0:T(8,128)S(1)} custom-call(s32[3]{0:T(128)S(1)} %copy-done.2, s32[32,32]{1,0:T(8,128)S(1)} %copy-done.1, bf16[4,8,32,128]{3,2,1,0:T(8,128)(2,1)S(1)} %copy-done, bf16[32,32,128]{2,1,0:T(8,128)(2,1)S(1)} %constant_dynamic-update-slice_fusion.left_pair, bf16[32,32,128]{2,1,0:T(8,128)(2,1)S(1)} %collective-permute-done.4.left_far, ...), custom_call_target="tpu_custom_call" | custom-call | tf_op jit(solution)/shard_map/range_products/pallas_call | solution.py:177
  76.2 20.0 %all_to_all.5 = f32[4,16,32,128]{3,2,1,0:T(8,128)S(1)} all-to-all(f32[4,16,32,128]{3,2,1,0:T(8,128)S(1)} %range_products.1), channel_id=1, replica_groups={{0,256,512,768},{32,288,544,800},{64,320,576,832},{96,352,608,864},{128..., dimensions={0} | all-to-all | bytes 2097152 | tf_op jit(solution)/shard_map/all_to_all | solution.py:67
  96.2 0.8 reduce_sum.9
  (12 shorter events, 0.1 us)
Async XLA Ops:
  0.0 40.9 %copy-start.3 = (bf16[64,32,128]{2,1,0:T(8,128)(2,1)S(1)}, bf16[64,32,128]{2,1,0:T(8,128)(2,1)}, u32[]{:S(2)}) copy-start(bf16[64,32,128]{2,1,0:T(8,128)(2,1)} %param.2) | copy-start | bytes 1572868
  0.0 25.7 %collective-permute-start = (bf16[64,32,128]{2,1,0:T(8,128)(2,1)}, bf16[64,32,128]{2,1,0:T(8,128)(2,1)S(1)}, u32[]{:S(2)}, u32[]{:S(2)}) collective-permute-start(bf16[64,32,128]{2,1,0:T(8,128)(2,1)} %param.2), channel_id=1, source_target_pairs={{0,64},{4,68},{8,72},{12,76},{16,80},{20,84},{24,88},{28,92},{32,2... | collective-permute-start | bytes 1572872 | tf_op jit(solution)/shard_map/ppermute | solution.py:30
  19.8 3.6 %collective-permute-start.1 = (bf16[16,32,128]{2,1,0:T(8,128)(2,1)S(1)}, bf16[16,32,128]{2,1,0:T(8,128)(2,1)S(1)}, u32[]{:S(2)}, u32[]{:S(2)}) collective-permute-start(bf16[16,32,128]{2,1,0:T(8,128)(2,1)S(1)} %constant_dynamic-slice_fusion), channel_id=1, source_target_pairs={{0,0},{4,4},{8,284},{12,280},{16,520},{20,540},{24,788},{28,768},{... | collective-permute-start | bytes 393224 | tf_op jit(solution)/shard_map/ppermute | solution.py:30
  26.8 19.0 %collective-permute-start.3 = (bf16[128,32,128]{2,1,0:T(8,128)(2,1)S(1)}, bf16[128,32,128]{2,1,0:T(8,128)(2,1)S(1)}, u32[]{:S(2)}, u32[]{:S(2)}) collective-permute-start(bf16[128,32,128]{2,1,0:T(8,128)(2,1)S(1)} %pad_maximum_fusion), channel_id=1, source_target_pairs={{0,195},{4,199},{8,203},{12,207},{16,211},{20,215},{24,219},{28,22... | collective-permute-start | bytes 3145736 | tf_op jit(solution)/shard_map/ppermute | solution.py:30
  28.7 9.7 %collective-permute-start.2 = (bf16[16,32,128]{2,1,0:T(8,128)(2,1)S(1)}, bf16[16,32,128]{2,1,0:T(8,128)(2,1)S(1)}, u32[]{:S(2)}, u32[]{:S(2)}) collective-permute-start(bf16[16,32,128]{2,1,0:T(8,128)(2,1)S(1)} %collective-permute-done.1), channel_id=1, source_target_pairs={{0,4},{4,0},{8,12},{12,8},{16,20},{20,16},{24,28},{28,24},{32,60},... | collective-permute-start | bytes 393224 | tf_op jit(solution)/shard_map/ppermute | solution.py:30
  38.5 31.4 %copy-start = (bf16[4,8,32,128]{3,2,1,0:T(8,128)(2,1)S(1)}, bf16[4,8,32,128]{3,2,1,0:T(8,128)(2,1)}, u32[]{:S(2)}) copy-start(bf16[4,8,32,128]{3,2,1,0:T(8,128)(2,1)} %masks.1) | copy-start | bytes 786436
  38.5 31.4 %copy-start.1 = (s32[32,32]{1,0:T(8,128)S(1)}, s32[32,32]{1,0:T(8,128)}, u32[]{:S(2)}) copy-start(s32[32,32]{1,0:T(8,128)} %shifts_ref.3) | copy-start | bytes 12292
  38.5 31.4 %copy-start.2 = (s32[3]{0:T(128)S(1)}, s32[3]{0:T(128)}, u32[]{:S(2)}) copy-start(s32[3]{0:T(128)} %pad_add_fusion.place_ref) | copy-start | bytes 40
  38.5 7.2 %collective-permute-start.4 = (bf16[32,32,128]{2,1,0:T(8,128)(2,1)S(1)}, bf16[32,32,128]{2,1,0:T(8,128)(2,1)S(1)}, u32[]{:S(2)}, u32[]{:S(2)}) collective-permute-start(bf16[32,32,128]{2,1,0:T(8,128)(2,1)S(1)} %constant_dynamic-update-slice_fusion.left_pair), channel_id=1, source_target_pairs={{0,28},{4,8},{8,4},{12,16},{16,12},{20,24},{24,20},{28,0},{32,36},... | collective-permute-start | bytes 786440 | tf_op jit(solution)/shard_map/ppermute | solution.py:30
  45.9 24.0 %collective-permute-start.7 = (bf16[256,32,128]{2,1,0:T(8,128)(2,1)S(1)}, bf16[256,32,128]{2,1,0:T(8,128)(2,1)S(1)}, u32[]{:S(2)}, u32[]{:S(2)}) collective-permute-start(bf16[256,32,128]{2,1,0:T(8,128)(2,1)S(1)} %constant_dynamic-update-slice_fusion.2.near_blocks), channel_id=1, source_target_pairs={{0,32},{4,36},{8,40},{12,44},{16,48},{20,52},{24,56},{28,60},{32,0... | collective-permute-start | bytes 6291464 | tf_op jit(solution)/shard_map/ppermute | solution.py:30
  53.9 8.7 %collective-permute-start.5 = (bf16[32,32,128]{2,1,0:T(8,128)(2,1)S(1)}, bf16[32,32,128]{2,1,0:T(8,128)(2,1)S(1)}, u32[]{:S(2)}, u32[]{:S(2)}) collective-permute-start(bf16[32,32,128]{2,1,0:T(8,128)(2,1)S(1)} %collective-permute-done.4.left_far), channel_id=1, source_target_pairs={{0,4},{4,0},{8,12},{12,8},{16,20},{20,16},{24,28},{28,24},{32,60},... | collective-permute-start | bytes 786440 | tf_op jit(solution)/shard_map/ppermute | solution.py:30
  58.8 11.1 %collective-permute-start.6 = (bf16[32,32,128]{2,1,0:T(8,128)(2,1)S(1)}, bf16[32,32,128]{2,1,0:T(8,128)(2,1)S(1)}, u32[]{:S(2)}, u32[]{:S(2)}) collective-permute-start(bf16[32,32,128]{2,1,0:T(8,128)(2,1)S(1)} %collective-permute-done.4.left_far), channel_id=1, source_target_pairs={{0,8},{4,28},{8,16},{12,4},{16,24},{20,12},{24,0},{28,20},{32,56},... | collective-permute-start | bytes 786440 | tf_op jit(solution)/shard_map/ppermute | solution.py:30

commit v6 on v3

--- a/solution.py
+++ b/solution.py
@@ -21,7 +21,10 @@
         for z in range(NZ * NL):
             for core in range(2):
                 for y in range(NY):
-                    tx, tz, tcore, ty = move(x, z, core, y)
+                    target = move(x, z, core, y)
+                    if target is None:
+                        continue
+                    tx, tz, tcore, ty = target
                     pairs.append((index(x, z, core, y), index(tx % NX, tz % (NZ * NL), tcore, ty % NY)))
     return pairs
 
@@ -36,9 +39,17 @@
 
 def along_z(turn):
     def move(x, z, core, y):
-        if core == turn:
-            return x, z ^ 1, core, y
-        return x, (z + 1 if z % 2 else z - 1), core, y
+        target = z ^ 1 if core == turn else (z + 1 if z % 2 else z - 1)
+        return (x, target, core, y) if 0 <= target < NZ * NL else None
+
+    return move
+
+
+def to_ends(turn):
+    ends = {NZ - 1: 0, NZ * NL - NZ: NZ * NL - 1}
+
+    def move(x, z, core, y):
+        return (x, ends[z], core, y) if core != turn and z in ends else None
 
     return move
 
@@ -136,11 +147,11 @@
         out_specs=vmem,
         name="masks",
     )(place, shifts)
-    near = sent(x_blocks, along_z(0))
+    near = sent(x_blocks, along_z(0)) + sent(x_blocks, to_ends(0))
     near, masks, mine = lax.optimization_barrier((near, masks, mine))
     left = lax.all_to_all(jnp.broadcast_to(mine[None], (NY, SPAN, BS, LANES)), "col", 0, 0)
     pair = jnp.concatenate([x_blocks, near], axis=0)
-    far = sent(pair, along_z(1))
+    far = sent(pair, along_z(1)) + sent(pair, to_ends(1))
     twin_pair = sent(pair, other_core)
     twin_far = sent(far, other_core)
     parts = pl.pallas_call(
@@ -152,7 +163,7 @@
             pltpu.VMEM((NEAR, RANGE, BS, LANES), jnp.bfloat16),
             pltpu.SemaphoreType.DMA((NEAR,)),
         ],
-        compiler_params=pltpu.CompilerParams(vmem_limit_bytes=20 * 1024 * 1024),
+        compiler_params=pltpu.CompilerParams(vmem_limit_bytes=12 * 1024 * 1024),
         name="range_products",
     )(place, shifts, masks, left, pair, far, twin_pair, twin_far)
     return jnp.sum(swapped_along_x(parts), axis=0).astype(jnp.bfloat16)

time: 92.5 us -> 87.7 us (0.948)
  the two profiles are of different devices: /device:TPU:2 before, /device:TPU:1 now
where the time goes in v6:
time: 87.7 us; the launch traced here: 87.1 us
  waiting for transfers between devices  23.8 us (27%)
  starting transfers between devices  23.7 us (27%)
  blocking collectives  21.7 us (25%)
  Pallas kernels  8.19 us (9%)
  local copies, waits for them, and re-layouts  6.24 us (7%)
  other arithmetic  3.3 us (4%)
    all_to_all x1, blocking collectives, swapped_along_x(): return lax.all_to_all(value, 'row', 0, 0, axis_index_groups=groups)  21.7 us
    ppermute x7, waiting for transfers between devices, sent(): return lax.ppermute(value, AXES, device_pairs(move))  19.9 us
    ppermute x7, starting transfers between devices, sent(): return lax.ppermute(value, AXES, device_pairs(move))  17.2 us
    all_to_all x1, starting transfers between devices, local(): lax.all_to_all(jnp.broadcast_to(mine[None], (NY, SPAN, BS, LANES)), 'col'...  6.53 us
    pallas_call x1, Pallas kernels, local(): pl.pallas_call(product_kernel, out_shape=jax.ShapeDtypeStruct((NX, SPAN,...  5.95 us
    all_to_all x1, waiting for transfers between devices, local(): lax.all_to_all(jnp.broadcast_to(mine[None], (NY, SPAN, BS, LANES)), 'col'...  3.89 us
    unnamed x15, local copies, waits for them, and re-layouts  3.2 us
    pallas_call x1, Pallas kernels, local(): pl.pallas_call(mask_kernel, out_shape=jax.ShapeDtypeStruct((NX, NEAR, BS,...  2.23 us
  transfers between devices with their start and end apart: 8, of which 3 were waited for; matrix products, arithmetic and copies ran while one was open for 6% of the time, Pallas kernels for 3%

profile of v6, /device:TPU:1, one launch (start us, length us, event | category | flops | bytes accessed | tf_op | source)
XLA Modules:
  0.0 87.1 jit_solution(13895578271416291229)
XLA Ops:
  0.0 1.4 %collective-permute-start.1 = (bf16[64,32,128]{2,1,0:T(8,128)(2,1)}, bf16[64,32,128]{2,1,0:T(8,128)(2,1)S(1)}, u32[]{:S(2)}, u32[]{:S(2)}) collective-permute-start(bf16[64,32,128]{2,1,0:T(8,128)(2,1)} %param.2), channel_id=1, source_target_pairs={{224,32},{228,36},{232,40},{236,44},{240,48},{244,52},{248,56},{25... | collective-permute-start | bytes 1572872 | tf_op jit(solution)/shard_map/ppermute | solution.py:33
  1.4 0.7 collective-permute-start
  2.1 0.9 %constant_dynamic-slice_fusion = bf16[16,32,128]{2,1,0:T(8,128)(2,1)S(1)} fusion(bf16[64,32,128]{2,1,0:T(8,128)(2,1)} %param.2, s32[]{:T(128)S(6)} %select_n.3), kind=kLoop, calls=%fused_computation.3 | loop fusion | bytes 262148 | tf_op jit(solution)/shard_map/dynamic_slice | solution.py:141
  3.0 1.3 %collective-permute-start.2 = (bf16[16,32,128]{2,1,0:T(8,128)(2,1)S(1)}, bf16[16,32,128]{2,1,0:T(8,128)(2,1)}, u32[]{:S(2)}, u32[]{:S(2)}) collective-permute-start(bf16[16,32,128]{2,1,0:T(8,128)(2,1)S(1)} %constant_dynamic-slice_fusion), channel_id=1, source_target_pairs={{0,0},{4,4},{8,284},{12,280},{16,520},{20,540},{24,788},{28,768},{... | collective-permute-start | bytes 393224 | tf_op jit(solution)/shard_map/ppermute | solution.py:33
  4.4 0.6 pad_add_fusion.place_ref
  4.9 2.2 %masks.1 = bf16[4,8,32,128]{3,2,1,0:T(8,128)(2,1)} custom-call(s32[3]{0:T(128)} %pad_add_fusion.place_ref, s32[32,32]{1,0:T(8,128)} %shifts_ref.3), custom_call_target="tpu_custom_call" | custom-call | tf_op jit(solution)/shard_map/masks/pallas_call | solution.py:143
  7.2 11.0 %collective-permute-done.1 = bf16[64,32,128]{2,1,0:T(8,128)(2,1)S(1)} collective-permute-done((bf16[64,32,128]{2,1,0:T(8,128)(2,1)}, bf16[64,32,128]{2,1,0:T(8,128)(2,1)S(1)}, u32[]{:S(2)}, u32[]{:S(2)}) %collective-permute-start.1) | collective-permute-done | bytes 524320 | tf_op jit(solution)/shard_map/ppermute | solution.py:33
  18.2 0.1 add.9
  18.3 0.1 constant_dynamic-update-slice_fusion.pair
  18.4 0.7 collective-permute-start.4
  19.1 4.2 %collective-permute-start.3 = (bf16[128,32,128]{2,1,0:T(8,128)(2,1)S(1)}, bf16[128,32,128]{2,1,0:T(8,128)(2,1)}, u32[]{:S(2)}, u32[]{:S(2)}) collective-permute-start(bf16[128,32,128]{2,1,0:T(8,128)(2,1)S(1)} %constant_dynamic-update-slice_fusion.pair), channel_id=1, source_target_pairs={{32,96},{36,100},{40,104},{44,108},{48,112},{52,116},{56,120},{60,... | collective-permute-start | bytes 3145736 | tf_op jit(solution)/shard_map/ppermute | solution.py:33
  23.3 2.1 %broadcast_in_dim.2 = bf16[8,16,32,128]{3,2,1,0:T(8,128)(2,1)} broadcast(bf16[16,32,128]{2,1,0:T(8,128)(2,1)} %collective-permute-done.2), dimensions={1,2,3} | broadcast | bytes 1179648 | tf_op jit(solution)/shard_map/broadcast_in_dim | solution.py:152
  25.4 6.5 %all-to-all-start = ((bf16[8,16,32,128]{3,2,1,0:T(8,128)(2,1)}), bf16[8,16,32,128]{3,2,1,0:T(8,128)(2,1)S(1)}, u32[]{:S(2)}, u32[]{:S(2)}) async-start(bf16[8,16,32,128]{3,2,1,0:T(8,128)(2,1)} %broadcast_in_dim.2), calls=%async_computation | async-start | bytes 2097152 | tf_op jit(solution)/shard_map/all_to_all | solution.py:152
  31.9 6.5 %collective-permute-start.5 = (bf16[128,32,128]{2,1,0:T(8,128)(2,1)S(1)}, bf16[128,32,128]{2,1,0:T(8,128)(2,1)S(1)}, u32[]{:S(2)}, u32[]{:S(2)}) collective-permute-start(bf16[128,32,128]{2,1,0:T(8,128)(2,1)S(1)} %constant_dynamic-update-slice_fusion.pair), channel_id=1, source_target_pairs={{0,32},{4,36},{8,40},{12,44},{16,48},{20,52},{24,56},{28,60},{32,0... | collective-permute-start | bytes 3145736 | tf_op jit(solution)/shard_map/ppermute | solution.py:33
  38.4 1.0 %copy-done.5 = bf16[128,32,128]{2,1,0:T(8,128)(2,1)} copy-done((bf16[128,32,128]{2,1,0:T(8,128)(2,1)}, bf16[128,32,128]{2,1,0:T(8,128)(2,1)S(1)}, u32[]{:S(2)}) %copy-start.5) | copy-done | bytes 1048600
  39.4 8.9 %collective-permute-done.3 = bf16[128,32,128]{2,1,0:T(8,128)(2,1)} collective-permute-done((bf16[128,32,128]{2,1,0:T(8,128)(2,1)S(1)}, bf16[128,32,128]{2,1,0:T(8,128)(2,1)}, u32[]{:S(2)}, u32[]{:S(2)}) %collective-permute-start.3) | collective-permute-done | bytes 1048608 | tf_op jit(solution)/shard_map/ppermute | solution.py:33
  48.3 1.8 %add.11.far = bf16[128,32,128]{2,1,0:T(8,128)(2,1)S(1)} add(bf16[128,32,128]{2,1,0:T(8,128)(2,1)} %collective-permute-done.3, bf16[128,32,128]{2,1,0:T(8,128)(2,1)} %copy-done.5) | non-fusion elementwise | flops 524288 | bytes 3145728 | tf_op jit(solution)/shard_map/add | solution.py:154
  50.2 2.4 %collective-permute-start.6 = (bf16[128,32,128]{2,1,0:T(8,128)(2,1)S(1)}, bf16[128,32,128]{2,1,0:T(8,128)(2,1)}, u32[]{:S(2)}, u32[]{:S(2)}) collective-permute-start(bf16[128,32,128]{2,1,0:T(8,128)(2,1)S(1)} %add.11.far), channel_id=1, source_target_pairs={{0,32},{4,36},{8,40},{12,44},{16,48},{20,52},{24,56},{28,60},{32,0... | collective-permute-start | bytes 3145736 | tf_op jit(solution)/shard_map/ppermute | solution.py:33
  52.6 1.0 %copy-done = bf16[128,32,128]{2,1,0:T(8,128)(2,1)} copy-done((bf16[128,32,128]{2,1,0:T(8,128)(2,1)}, bf16[128,32,128]{2,1,0:T(8,128)(2,1)S(1)}, u32[]{:S(2)}) %copy-start) | copy-done | bytes 1048600
  53.5 3.9 %all-to-all-done.left = bf16[8,16,32,128]{3,2,1,0:T(8,128)(2,1)S(1)} async-done(((bf16[8,16,32,128]{3,2,1,0:T(8,128)(2,1)}), bf16[8,16,32,128]{3,2,1,0:T(8,128)(2,1)S(1)}, u32[]{:S(2)}, u32[]{:S(2)}) %all-to-all-start) | async-done | bytes 1048608 | tf_op jit(solution)/shard_map/all_to_all | solution.py:152
  57.4 1.2 %copy-done.1 = bf16[128,32,128]{2,1,0:T(8,128)(2,1)S(1)} copy-done((bf16[128,32,128]{2,1,0:T(8,128)(2,1)S(1)}, bf16[128,32,128]{2,1,0:T(8,128)(2,1)}, u32[]{:S(2)}) %copy-start.1) | copy-done | bytes 1048600
  58.7 6.0 %range_products.1 = f32[4,16,32,128]{3,2,1,0:T(8,128)S(1)} custom-call(s32[3]{0:T(128)S(1)} %copy-done.4, s32[32,32]{1,0:T(8,128)S(1)} %copy-done.3, bf16[4,8,32,128]{3,2,1,0:T(8,128)(2,1)S(1)} %copy-done.2, bf16[8,16,32,128]{3,2,1,0:T(8,128)(2,1)S(1)} %all-to-all-done.left, bf16[128,32,128]{2,1,0:T(8,128)(2,1)S(1)} %constant_dynamic-update-slice_fusion.pair, ...), custom_call_target="tpu_custom_call" | custom-call | tf_op jit(solution)/shard_map/range_products/pallas_call | solution.py:157
  64.6 21.7 %all_to_all.10 = f32[4,16,32,128]{3,2,1,0:T(8,128)S(1)} all-to-all(f32[4,16,32,128]{3,2,1,0:T(8,128)S(1)} %range_products.1), channel_id=1, replica_groups={{0,256,512,768},{32,288,544,800},{64,320,576,832},{96,352,608,864},{128..., dimensions={0} | all-to-all | bytes 2097152 | tf_op jit(solution)/shard_map/all_to_all | solution.py:65
  86.4 0.8 reduce_sum.9
  (17 shorter events, 0.1 us)
Async XLA Ops:
  0.0 7.2 %copy-start.6 = (bf16[64,32,128]{2,1,0:T(8,128)(2,1)S(1)}, bf16[64,32,128]{2,1,0:T(8,128)(2,1)}, u32[]{:S(2)}) copy-start(bf16[64,32,128]{2,1,0:T(8,128)(2,1)} %param.2) | copy-start | bytes 1572868
  0.0 18.2 %collective-permute-start.1 = (bf16[64,32,128]{2,1,0:T(8,128)(2,1)}, bf16[64,32,128]{2,1,0:T(8,128)(2,1)S(1)}, u32[]{:S(2)}, u32[]{:S(2)}) collective-permute-start(bf16[64,32,128]{2,1,0:T(8,128)(2,1)} %param.2), channel_id=1, source_target_pairs={{224,32},{228,36},{232,40},{236,44},{240,48},{244,52},{248,56},{25... | collective-permute-start | bytes 1572872 | tf_op jit(solution)/shard_map/ppermute | solution.py:33
  1.4 16.8 %collective-permute-start = (bf16[64,32,128]{2,1,0:T(8,128)(2,1)}, bf16[64,32,128]{2,1,0:T(8,128)(2,1)S(1)}, u32[]{:S(2)}, u32[]{:S(2)}) collective-permute-start(bf16[64,32,128]{2,1,0:T(8,128)(2,1)} %param.2), channel_id=1, source_target_pairs={{0,64},{4,68},{8,72},{12,76},{16,80},{20,84},{24,88},{28,92},{64,0... | collective-permute-start | bytes 1572872 | tf_op jit(solution)/shard_map/ppermute | solution.py:33
  3.0 15.3 %collective-permute-start.2 = (bf16[16,32,128]{2,1,0:T(8,128)(2,1)S(1)}, bf16[16,32,128]{2,1,0:T(8,128)(2,1)}, u32[]{:S(2)}, u32[]{:S(2)}) collective-permute-start(bf16[16,32,128]{2,1,0:T(8,128)(2,1)S(1)} %constant_dynamic-slice_fusion), channel_id=1, source_target_pairs={{0,0},{4,4},{8,284},{12,280},{16,520},{20,540},{24,788},{28,768},{... | collective-permute-start | bytes 393224 | tf_op jit(solution)/shard_map/ppermute | solution.py:33
  18.4 20.0 %collective-permute-start.4 = (bf16[128,32,128]{2,1,0:T(8,128)(2,1)S(1)}, bf16[128,32,128]{2,1,0:T(8,128)(2,1)S(1)}, u32[]{:S(2)}, u32[]{:S(2)}) collective-permute-start(bf16[128,32,128]{2,1,0:T(8,128)(2,1)S(1)} %constant_dynamic-update-slice_fusion.pair), channel_id=1, source_target_pairs={{192,0},{196,4},{200,8},{204,12},{208,16},{212,20},{216,24},{220,2... | collective-permute-start | bytes 3145736 | tf_op jit(solution)/shard_map/ppermute | solution.py:33
  19.1 29.2 %collective-permute-start.3 = (bf16[128,32,128]{2,1,0:T(8,128)(2,1)S(1)}, bf16[128,32,128]{2,1,0:T(8,128)(2,1)}, u32[]{:S(2)}, u32[]{:S(2)}) collective-permute-start(bf16[128,32,128]{2,1,0:T(8,128)(2,1)S(1)} %constant_dynamic-update-slice_fusion.pair), channel_id=1, source_target_pairs={{32,96},{36,100},{40,104},{44,108},{48,112},{52,116},{56,120},{60,... | collective-permute-start | bytes 3145736 | tf_op jit(solution)/shard_map/ppermute | solution.py:33
  25.4 32.0 %all-to-all-start = ((bf16[8,16,32,128]{3,2,1,0:T(8,128)(2,1)}), bf16[8,16,32,128]{3,2,1,0:T(8,128)(2,1)S(1)}, u32[]{:S(2)}, u32[]{:S(2)}) async-start(bf16[8,16,32,128]{3,2,1,0:T(8,128)(2,1)} %broadcast_in_dim.2), calls=%async_computation | async-start | bytes 2097152 | tf_op jit(solution)/shard_map/all_to_all | solution.py:152
  31.9 25.5 %copy-start.2 = (bf16[4,8,32,128]{3,2,1,0:T(8,128)(2,1)S(1)}, bf16[4,8,32,128]{3,2,1,0:T(8,128)(2,1)}, u32[]{:S(2)}) copy-start(bf16[4,8,32,128]{3,2,1,0:T(8,128)(2,1)} %masks.1) | copy-start | bytes 786436
  31.9 25.5 %copy-start.3 = (s32[32,32]{1,0:T(8,128)S(1)}, s32[32,32]{1,0:T(8,128)}, u32[]{:S(2)}) copy-start(s32[32,32]{1,0:T(8,128)} %shifts_ref.3) | copy-start | bytes 12292
  31.9 25.5 %copy-start.4 = (s32[3]{0:T(128)S(1)}, s32[3]{0:T(128)}, u32[]{:S(2)}) copy-start(s32[3]{0:T(128)} %pad_add_fusion.place_ref) | copy-start | bytes 40
  31.9 20.6 %collective-permute-start.5 = (bf16[128,32,128]{2,1,0:T(8,128)(2,1)S(1)}, bf16[128,32,128]{2,1,0:T(8,128)(2,1)S(1)}, u32[]{:S(2)}, u32[]{:S(2)}) collective-permute-start(bf16[128,32,128]{2,1,0:T(8,128)(2,1)S(1)} %constant_dynamic-update-slice_fusion.pair), channel_id=1, source_target_pairs={{0,32},{4,36},{8,40},{12,44},{16,48},{20,52},{24,56},{28,60},{32,0... | collective-permute-start | bytes 3145736 | tf_op jit(solution)/shard_map/ppermute | solution.py:33
  38.4 1.0 %copy-start.5 = (bf16[128,32,128]{2,1,0:T(8,128)(2,1)}, bf16[128,32,128]{2,1,0:T(8,128)(2,1)S(1)}, u32[]{:S(2)}) copy-start(bf16[128,32,128]{2,1,0:T(8,128)(2,1)S(1)} %collective-permute-done.4) | copy-start | bytes 3145732
  50.2 7.3 %collective-permute-start.6 = (bf16[128,32,128]{2,1,0:T(8,128)(2,1)S(1)}, bf16[128,32,128]{2,1,0:T(8,128)(2,1)}, u32[]{:S(2)}, u32[]{:S(2)}) collective-permute-start(bf16[128,32,128]{2,1,0:T(8,128)(2,1)S(1)} %add.11.far), channel_id=1, source_target_pairs={{0,32},{4,36},{8,40},{12,44},{16,48},{20,52},{24,56},{28,60},{32,0... | collective-permute-start | bytes 3145736 | tf_op jit(solution)/shard_map/ppermute | solution.py:33
  52.5 1.0 %copy-start = (bf16[128,32,128]{2,1,0:T(8,128)(2,1)}, bf16[128,32,128]{2,1,0:T(8,128)(2,1)S(1)}, u32[]{:S(2)}) copy-start(bf16[128,32,128]{2,1,0:T(8,128)(2,1)S(1)} %collective-permute-done.5.twin_pair) | copy-start | bytes 3145732
  57.4 1.2 %copy-start.1 = (bf16[128,32,128]{2,1,0:T(8,128)(2,1)S(1)}, bf16[128,32,128]{2,1,0:T(8,128)(2,1)}, u32[]{:S(2)}) copy-start(bf16[128,32,128]{2,1,0:T(8,128)(2,1)} %copy-done) | copy-start | bytes 3145732

commit v7 on v6

--- a/solution.py
+++ b/solution.py
@@ -60,9 +60,8 @@
     return near_x, z, core, (y + turn if side else y - turn)
 
 
-def swapped_along_x(value):
-    groups = [[x * NEAR + n for x in range(NX)] for n in range(NEAR)]
-    return lax.all_to_all(value, "row", 0, 0, axis_index_groups=groups)
+def along_x(turn):
+    return lambda x, z, core, y: (x ^ (1 if core == turn else 3), z, core, y)
 
 
 def mask_kernel(place_ref, shifts_ref, masks_ref):
@@ -87,18 +86,39 @@
     lax.fori_loop(0, NEAR, mask_step, 0)
 
 
-def product_kernel(
-    place_ref, shifts_ref, masks, left, pair, far, twin_pair, twin_far, out, right, sems
-):
+def add_targets(place_ref, shifts_ref, masks, left, right, out, turns):
     row = place_ref[0]
     layer = place_ref[2]
-    core = row & 1
-    zl = (row >> 1) & 3
     x = row >> 3
-    near = x * NEAR
 
-    first = jnp.where(core == 0, 1, 3)
-    second = jnp.where(core == 0, 3, 1)
+    def position_step(p, carry):
+        place = layer * SPAN + p
+        for n, turn in enumerate(turns):
+            target = x ^ turn
+            target_row = target * NEAR + (row & (NEAR - 1))
+            steps = (target - x) & (NX - 1)
+            low, high = (2 * x - steps) & (NY - 1), (2 * x + 1 + steps) & (NY - 1)
+            lhs = jnp.concatenate([left[low, p], left[high, p]], axis=1)
+            rows = []
+            for j in range(NEAR):
+                q = (place + shifts_ref[target_row, x * NEAR + j]) & (RANGE - 1)
+                rows.append(right[j, q] * masks[target, j])
+            rhs = jnp.concatenate(rows, axis=0)
+            out[n, p] = jnp.dot(lhs, rhs, preferred_element_type=jnp.float32)
+        return carry
+
+    lax.fori_loop(0, SPAN, position_step, 0)
+
+
+def turns_of(place_ref):
+    core = place_ref[0] & 1
+    return jnp.where(core == 0, 1, 3), jnp.where(core == 0, 3, 1)
+
+
+def sent_kernel(place_ref, shifts_ref, masks, left, pair, far, twin_pair, twin_far, right, out, sems):
+    core = place_ref[0] & 1
+    zl = (place_ref[0] >> 1) & 3
+    first, second = turns_of(place_ref)
     pieces = [(pair, 0, 0, core), (pair, 1, first, core), (far, 0, second, core), (far, 1, 2, core)]
     pieces += [(twin_pair, 0, 0, 1 - core), (twin_pair, 1, second, 1 - core)]
     pieces += [(twin_far, 0, first, 1 - core), (twin_far, 1, 2, 1 - core)]
@@ -110,23 +130,11 @@
         copy.start()
     for copy in copies:
         copy.wait()
+    add_targets(place_ref, shifts_ref, masks, left, right, out, (first, 2))
 
-    def position_step(p, carry):
-        place = layer * SPAN + p
-        for t in range(NX):
-            target = t * NEAR + (row & (NEAR - 1))
-            turn = (t - x) & (NX - 1)
-            low, high = (2 * x - turn) & (NY - 1), (2 * x + 1 + turn) & (NY - 1)
-            lhs = jnp.concatenate([left[low, p], left[high, p]], axis=1)
-            rows = []
-            for j in range(NEAR):
-                q = (place + shifts_ref[target, near + j]) & (RANGE - 1)
-                rows.append(right[j, q] * masks[t, j])
-            rhs = jnp.concatenate(rows, axis=0)
-            out[t, p] = jnp.dot(lhs, rhs, preferred_element_type=jnp.float32)
-        return carry
 
-    lax.fori_loop(0, SPAN, position_step, 0)
+def kept_kernel(place_ref, shifts_ref, masks, left, right, out):
+    add_targets(place_ref, shifts_ref, masks, left, right, out, (0, turns_of(place_ref)[1]))
 
 
 def local(x_blocks, shifts):
@@ -154,19 +162,31 @@
     far = sent(pair, along_z(1)) + sent(pair, to_ends(1))
     twin_pair = sent(pair, other_core)
     twin_far = sent(far, other_core)
-    parts = pl.pallas_call(
-        product_kernel,
-        out_shape=jax.ShapeDtypeStruct((NX, SPAN, BS, LANES), jnp.float32),
+    part = jax.ShapeDtypeStruct((2, SPAN, BS, LANES), jnp.float32)
+    cost = pl.CostEstimate(flops=NX * 2 ** 25, bytes_accessed=6 * 2 ** 20, transcendentals=0)
+    params = pltpu.CompilerParams(vmem_limit_bytes=12 * 1024 * 1024)
+    gathered, leaving = pl.pallas_call(
+        sent_kernel,
+        out_shape=[jax.ShapeDtypeStruct((NEAR, RANGE, BS, LANES), jnp.bfloat16), part],
         in_specs=[smem, smem] + [vmem] * 2 + [anywhere] * 4,
+        out_specs=[vmem] * 2,
+        scratch_shapes=[pltpu.SemaphoreType.DMA((NEAR,))],
+        compiler_params=params,
+        cost_estimate=cost,
+        name="sent_products",
+    )(place, shifts, masks, left, pair, far, twin_pair, twin_far)
+    arrived = sent(leaving, along_x(0))
+    kept = pl.pallas_call(
+        kept_kernel,
+        out_shape=part,
+        in_specs=[smem, smem] + [vmem] * 3,
         out_specs=vmem,
-        scratch_shapes=[
-            pltpu.VMEM((NEAR, RANGE, BS, LANES), jnp.bfloat16),
-            pltpu.SemaphoreType.DMA((NEAR,)),
-        ],
-        compiler_params=pltpu.CompilerParams(vmem_limit_bytes=12 * 1024 * 1024),
-        name="range_products",
-    )(place, shifts, masks, left, pair, far, twin_pair, twin_far)
-    return jnp.sum(swapped_along_x(parts), axis=0).astype(jnp.bfloat16)
+        compiler_params=params,
+        cost_estimate=cost,
+        name="kept_products",
+    )(place, shifts, masks, left, gathered)
+    last = sent(kept[1] + arrived[1], along_x(1))
+    return (kept[0] + arrived[0] + last).astype(jnp.bfloat16)
 
 
 def solution(mesh):

time: 87.7 us -> 91.2 us (1.040)
  the two profiles are of different devices: /device:TPU:1 before, /device:TPU:712 now
where the time goes in v7:
time: 91.2 us; the launch traced here: 90.6 us
  starting transfers between devices  35.6 us (39%)
  waiting for transfers between devices  32.7 us (36%)
  Pallas kernels  10.8 us (12%)
  local copies, waits for them, and re-layouts  7.94 us (9%)
  other arithmetic  3.3 us (4%)
    ppermute x9, starting transfers between devices, sent(): return lax.ppermute(value, AXES, device_pairs(move))  28.1 us
    ppermute x9, waiting for transfers between devices, sent(): return lax.ppermute(value, AXES, device_pairs(move))  17.4 us
    all_to_all x1, waiting for transfers between devices, local(): lax.all_to_all(jnp.broadcast_to(mine[None], (NY, SPAN, BS, LANES)), 'col'...  15.3 us
    all_to_all x1, starting transfers between devices, local(): lax.all_to_all(jnp.broadcast_to(mine[None], (NY, SPAN, BS, LANES)), 'col'...  7.55 us
    pallas_call x1, Pallas kernels, local(): pl.pallas_call(sent_kernel, out_shape=[jax.ShapeDtypeStruct((NEAR, RANGE,...  5 us
    unnamed x15, local copies, waits for them, and re-layouts  4.89 us
    pallas_call x1, Pallas kernels, local(): pl.pallas_call(kept_kernel, out_shape=part, in_specs=[smem, smem] + [vmem...  3.53 us
    pallas_call x1, Pallas kernels, local(): pl.pallas_call(mask_kernel, out_shape=jax.ShapeDtypeStruct((NX, NEAR, BS,...  2.25 us
  transfers between devices with their start and end apart: 10, of which 5 were waited for; matrix products, arithmetic and copies ran while one was open for 7% of the time, Pallas kernels for 6%

profile of v7, /device:TPU:712, one launch (start us, length us, event | category | flops | bytes accessed | tf_op | source)
XLA Modules:
  0.0 90.6 jit_solution(9638616784039455030)
XLA Ops:
  0.0 0.7 collective-permute-start.1
  0.7 2.5 %collective-permute-start = (bf16[64,32,128]{2,1,0:T(8,128)(2,1)}, bf16[64,32,128]{2,1,0:T(8,128)(2,1)S(1)}, u32[]{:S(2)}, u32[]{:S(2)}) collective-permute-start(bf16[64,32,128]{2,1,0:T(8,128)(2,1)} %param.2), channel_id=1, source_target_pairs={{0,64},{4,68},{8,72},{12,76},{16,80},{20,84},{24,88},{28,92},{64,0... | collective-permute-start | bytes 1572872 | tf_op jit(solution)/shard_map/ppermute | solution.py:33
  3.2 0.9 %constant_dynamic-slice_fusion = bf16[16,32,128]{2,1,0:T(8,128)(2,1)S(1)} fusion(bf16[64,32,128]{2,1,0:T(8,128)(2,1)} %param.2, s32[]{:T(128)S(6)} %select_n.3), kind=kLoop, calls=%fused_computation.9 | loop fusion | bytes 262148 | tf_op jit(solution)/shard_map/dynamic_slice | solution.py:149
  5.4 2.2 %masks.1 = bf16[4,8,32,128]{3,2,1,0:T(8,128)(2,1)} custom-call(s32[3]{0:T(128)} %pad_add_fusion.place_ref, s32[32,32]{1,0:T(8,128)} %shifts_ref.5), custom_call_target="tpu_custom_call" | custom-call | tf_op jit(solution)/shard_map/masks/pallas_call | solution.py:151
  7.6 1.1 %constant_dynamic-update-slice_fusion.1 = bf16[128,32,128]{2,1,0:T(8,128)(2,1)S(1)} fusion(bf16[64,32,128]{2,1,0:T(8,128)(2,1)} %param.2), kind=kLoop, calls=%fused_computation.7 | loop fusion | bytes 1048576
  8.7 3.2 %collective-permute-done = bf16[64,32,128]{2,1,0:T(8,128)(2,1)S(1)} collective-permute-done((bf16[64,32,128]{2,1,0:T(8,128)(2,1)}, bf16[64,32,128]{2,1,0:T(8,128)(2,1)S(1)}, u32[]{:S(2)}, u32[]{:S(2)}) %collective-permute-start) | collective-permute-done | bytes 524320 | tf_op jit(solution)/shard_map/ppermute | solution.py:33
  12.9 0.7 collective-permute-start.4
  13.6 13.5 %collective-permute-start.3 = (bf16[128,32,128]{2,1,0:T(8,128)(2,1)S(1)}, bf16[128,32,128]{2,1,0:T(8,128)(2,1)}, u32[]{:S(2)}, u32[]{:S(2)}) collective-permute-start(bf16[128,32,128]{2,1,0:T(8,128)(2,1)S(1)} %constant_dynamic-update-slice_fusion.pair), channel_id=1, source_target_pairs={{32,96},{36,100},{40,104},{44,108},{48,112},{52,116},{56,120},{60,... | collective-permute-start | bytes 3145736 | tf_op jit(solution)/shard_map/ppermute | solution.py:33
  27.1 2.1 %broadcast_in_dim.2 = bf16[8,16,32,128]{3,2,1,0:T(8,128)(2,1)} broadcast(bf16[16,32,128]{2,1,0:T(8,128)(2,1)} %copy-done.6), dimensions={1,2,3} | broadcast | bytes 1179648 | tf_op jit(solution)/shard_map/broadcast_in_dim | solution.py:160
  29.2 7.5 %all-to-all-start = ((bf16[8,16,32,128]{3,2,1,0:T(8,128)(2,1)}), bf16[8,16,32,128]{3,2,1,0:T(8,128)(2,1)S(1)}, u32[]{:S(2)}, u32[]{:S(2)}) async-start(bf16[8,16,32,128]{3,2,1,0:T(8,128)(2,1)} %broadcast_in_dim.2), calls=%async_computation | async-start | bytes 2097152 | tf_op jit(solution)/shard_map/all_to_all | solution.py:160
  36.7 1.9 %collective-permute-start.5 = (bf16[128,32,128]{2,1,0:T(8,128)(2,1)S(1)}, bf16[128,32,128]{2,1,0:T(8,128)(2,1)S(1)}, u32[]{:S(2)}, u32[]{:S(2)}) collective-permute-start(bf16[128,32,128]{2,1,0:T(8,128)(2,1)S(1)} %constant_dynamic-update-slice_fusion.pair), channel_id=1, source_target_pairs={{0,32},{4,36},{8,40},{12,44},{16,48},{20,52},{24,56},{28,60},{32,0... | collective-permute-start | bytes 3145736 | tf_op jit(solution)/shard_map/ppermute | solution.py:33
  38.7 1.0 %copy-done.5 = bf16[128,32,128]{2,1,0:T(8,128)(2,1)} copy-done((bf16[128,32,128]{2,1,0:T(8,128)(2,1)}, bf16[128,32,128]{2,1,0:T(8,128)(2,1)S(1)}, u32[]{:S(2)}) %copy-start.5) | copy-done | bytes 1048600
  40.0 1.8 %add.26.far = bf16[128,32,128]{2,1,0:T(8,128)(2,1)S(1)} add(bf16[128,32,128]{2,1,0:T(8,128)(2,1)} %collective-permute-done.3, bf16[128,32,128]{2,1,0:T(8,128)(2,1)} %copy-done.5) | non-fusion elementwise | flops 524288 | bytes 3145728 | tf_op jit(solution)/shard_map/add | solution.py:162
  41.8 2.1 %collective-permute-start.6 = (bf16[128,32,128]{2,1,0:T(8,128)(2,1)S(1)}, bf16[128,32,128]{2,1,0:T(8,128)(2,1)}, u32[]{:S(2)}, u32[]{:S(2)}) collective-permute-start(bf16[128,32,128]{2,1,0:T(8,128)(2,1)S(1)} %add.26.far), channel_id=1, source_target_pairs={{0,32},{4,36},{8,40},{12,44},{16,48},{20,52},{24,56},{28,60},{32,0... | collective-permute-start | bytes 3145736 | tf_op jit(solution)/shard_map/ppermute | solution.py:33
  43.9 1.0 %copy-done.1 = bf16[128,32,128]{2,1,0:T(8,128)(2,1)} copy-done((bf16[128,32,128]{2,1,0:T(8,128)(2,1)}, bf16[128,32,128]{2,1,0:T(8,128)(2,1)S(1)}, u32[]{:S(2)}) %copy-start.1) | copy-done | bytes 1048600
  44.9 15.3 %all-to-all-done.left = bf16[8,16,32,128]{3,2,1,0:T(8,128)(2,1)S(1)} async-done(((bf16[8,16,32,128]{3,2,1,0:T(8,128)(2,1)}), bf16[8,16,32,128]{3,2,1,0:T(8,128)(2,1)S(1)}, u32[]{:S(2)}, u32[]{:S(2)}) %all-to-all-start) | async-done | bytes 1048608 | tf_op jit(solution)/shard_map/all_to_all | solution.py:160
  60.2 1.2 %copy-done.2 = bf16[128,32,128]{2,1,0:T(8,128)(2,1)S(1)} copy-done((bf16[128,32,128]{2,1,0:T(8,128)(2,1)S(1)}, bf16[128,32,128]{2,1,0:T(8,128)(2,1)}, u32[]{:S(2)}) %copy-start.2) | copy-done | bytes 1048600
  61.5 5.0 %sent_products.1 = (bf16[8,64,32,128]{3,2,1,0:T(8,128)(2,1)S(1)}, f32[2,16,32,128]{3,2,1,0:T(8,128)S(1)}) custom-call(s32[3]{0:T(128)S(1)} %copy-done.4, s32[32,32]{1,0:T(8,128)S(1)} %copy-done.3, bf16[4,8,32,128]{3,2,1,0:T(8,128)(2,1)S(1)} %copy-done, bf16[8,16,32,128]{3,2,1,0:T(8,128)(2,1)S(1)} %all-to-all-done.left, ...), custom_call_target="tpu_custom_call" | custom-call | flops 134217728 | bytes 6291456 | tf_op jit(solution)/shard_map/sent_products/pallas_call | solution.py:168
  66.5 3.3 %collective-permute-start.7 = (f32[2,16,32,128]{3,2,1,0:T(8,128)S(1)}, f32[2,16,32,128]{3,2,1,0:T(8,128)S(1)}, u32[]{:S(2)}, u32[]{:S(2)}) collective-permute-start(f32[2,16,32,128]{3,2,1,0:T(8,128)S(1)} %get-tuple-element.14), channel_id=1, source_target_pairs={{0,256},{4,260},{8,264},{12,268},{16,272},{20,276},{24,280},{28,28... | collective-permute-start | bytes 1572872 | tf_op jit(solution)/shard_map/ppermute | solution.py:33
  69.8 3.5 %kept_products.1 = f32[2,16,32,128]{3,2,1,0:T(8,128)S(1)} custom-call(s32[3]{0:T(128)S(1)} %copy-done.4, s32[32,32]{1,0:T(8,128)S(1)} %copy-done.3, bf16[4,8,32,128]{3,2,1,0:T(8,128)(2,1)S(1)} %copy-done, bf16[8,16,32,128]{3,2,1,0:T(8,128)(2,1)S(1)} %all-to-all-done.left, bf16[8,64,32,128]{3,2,1,0:T(8,128)(2,1)S(1)} %get-tuple-element.13.right), custom_call_target="tpu_custom_call" | custom-call | flops 134217728 | bytes 6291456 | tf_op jit(solution)/shard_map/kept_products/pallas_call | solution.py:179
  73.3 7.0 %collective-permute-done.7 = f32[2,16,32,128]{3,2,1,0:T(8,128)S(1)} collective-permute-done((f32[2,16,32,128]{3,2,1,0:T(8,128)S(1)}, f32[2,16,32,128]{3,2,1,0:T(8,128)S(1)}, u32[]{:S(2)}, u32[]{:S(2)}) %collective-permute-start.7) | collective-permute-done | bytes 524320 | tf_op jit(solution)/shard_map/ppermute | solution.py:33
  80.4 2.8 %collective-permute-start.8 = (f32[16,32,128]{2,1,0:T(8,128)S(1)}, f32[16,32,128]{2,1,0:T(8,128)S(1)}, u32[]{:S(2)}, u32[]{:S(2)}) collective-permute-start(f32[16,32,128]{2,1,0:T(8,128)S(1)} %fusion), channel_id=1, source_target_pairs={{0,768},{4,772},{8,776},{12,780},{16,784},{20,788},{24,792},{28,79... | collective-permute-start | bytes 786440 | tf_op jit(solution)/shard_map/ppermute | solution.py:33
  83.2 6.7 %collective-permute-done.8 = f32[16,32,128]{2,1,0:T(8,128)S(1)} collective-permute-done((f32[16,32,128]{2,1,0:T(8,128)S(1)}, f32[16,32,128]{2,1,0:T(8,128)S(1)}, u32[]{:S(2)}, u32[]{:S(2)}) %collective-permute-start.8) | collective-permute-done | bytes 262176 | tf_op jit(solution)/shard_map/ppermute | solution.py:33
  89.9 0.7 fusion.3
  (22 shorter events, 2.5 us)
Async XLA Ops:
  0.0 8.7 %collective-permute-start.1 = (bf16[64,32,128]{2,1,0:T(8,128)(2,1)}, bf16[64,32,128]{2,1,0:T(8,128)(2,1)S(1)}, u32[]{:S(2)}, u32[]{:S(2)}) collective-permute-start(bf16[64,32,128]{2,1,0:T(8,128)(2,1)} %param.2), channel_id=1, source_target_pairs={{224,32},{228,36},{232,40},{236,44},{240,48},{244,52},{248,56},{25... | collective-permute-start | bytes 1572872 | tf_op jit(solution)/shard_map/ppermute | solution.py:33
  0.7 11.3 %collective-permute-start = (bf16[64,32,128]{2,1,0:T(8,128)(2,1)}, bf16[64,32,128]{2,1,0:T(8,128)(2,1)S(1)}, u32[]{:S(2)}, u32[]{:S(2)}) collective-permute-start(bf16[64,32,128]{2,1,0:T(8,128)(2,1)} %param.2), channel_id=1, source_target_pairs={{0,64},{4,68},{8,72},{12,76},{16,80},{20,84},{24,88},{28,92},{64,0... | collective-permute-start | bytes 1572872 | tf_op jit(solution)/shard_map/ppermute | solution.py:33
  4.1 8.0 %collective-permute-start.2 = (bf16[16,32,128]{2,1,0:T(8,128)(2,1)S(1)}, bf16[16,32,128]{2,1,0:T(8,128)(2,1)S(1)}, u32[]{:S(2)}, u32[]{:S(2)}) collective-permute-start(bf16[16,32,128]{2,1,0:T(8,128)(2,1)S(1)} %constant_dynamic-slice_fusion), channel_id=1, source_target_pairs={{0,0},{4,4},{8,284},{12,280},{16,520},{20,540},{24,788},{28,768},{... | collective-permute-start | bytes 393224 | tf_op jit(solution)/shard_map/ppermute | solution.py:33
  8.7 51.5 %copy-start = (bf16[4,8,32,128]{3,2,1,0:T(8,128)(2,1)S(1)}, bf16[4,8,32,128]{3,2,1,0:T(8,128)(2,1)}, u32[]{:S(2)}) copy-start(bf16[4,8,32,128]{3,2,1,0:T(8,128)(2,1)} %masks.1) | copy-start | bytes 786436
  8.7 51.5 %copy-start.3 = (s32[32,32]{1,0:T(8,128)S(1)}, s32[32,32]{1,0:T(8,128)}, u32[]{:S(2)}) copy-start(s32[32,32]{1,0:T(8,128)} %shifts_ref.5) | copy-start | bytes 12292
  8.7 51.5 %copy-start.4 = (s32[3]{0:T(128)S(1)}, s32[3]{0:T(128)}, u32[]{:S(2)}) copy-start(s32[3]{0:T(128)} %pad_add_fusion.place_ref) | copy-start | bytes 40
  12.1 0.7 copy-start.6
  12.9 25.8 %collective-permute-start.4 = (bf16[128,32,128]{2,1,0:T(8,128)(2,1)S(1)}, bf16[128,32,128]{2,1,0:T(8,128)(2,1)S(1)}, u32[]{:S(2)}, u32[]{:S(2)}) collective-permute-start(bf16[128,32,128]{2,1,0:T(8,128)(2,1)S(1)} %constant_dynamic-update-slice_fusion.pair), channel_id=1, source_target_pairs={{192,0},{196,4},{200,8},{204,12},{208,16},{212,20},{216,24},{220,2... | collective-permute-start | bytes 3145736 | tf_op jit(solution)/shard_map/ppermute | solution.py:33
  13.6 26.4 %collective-permute-start.3 = (bf16[128,32,128]{2,1,0:T(8,128)(2,1)S(1)}, bf16[128,32,128]{2,1,0:T(8,128)(2,1)}, u32[]{:S(2)}, u32[]{:S(2)}) collective-permute-start(bf16[128,32,128]{2,1,0:T(8,128)(2,1)S(1)} %constant_dynamic-update-slice_fusion.pair), channel_id=1, source_target_pairs={{32,96},{36,100},{40,104},{44,108},{48,112},{52,116},{56,120},{60,... | collective-permute-start | bytes 3145736 | tf_op jit(solution)/shard_map/ppermute | solution.py:33
  29.2 31.0 %all-to-all-start = ((bf16[8,16,32,128]{3,2,1,0:T(8,128)(2,1)}), bf16[8,16,32,128]{3,2,1,0:T(8,128)(2,1)S(1)}, u32[]{:S(2)}, u32[]{:S(2)}) async-start(bf16[8,16,32,128]{3,2,1,0:T(8,128)(2,1)} %broadcast_in_dim.2), calls=%async_computation | async-start | bytes 2097152 | tf_op jit(solution)/shard_map/all_to_all | solution.py:160
  36.7 7.1 %collective-permute-start.5 = (bf16[128,32,128]{2,1,0:T(8,128)(2,1)S(1)}, bf16[128,32,128]{2,1,0:T(8,128)(2,1)S(1)}, u32[]{:S(2)}, u32[]{:S(2)}) collective-permute-start(bf16[128,32,128]{2,1,0:T(8,128)(2,1)S(1)} %constant_dynamic-update-slice_fusion.pair), channel_id=1, source_target_pairs={{0,32},{4,36},{8,40},{12,44},{16,48},{20,52},{24,56},{28,60},{32,0... | collective-permute-start | bytes 3145736 | tf_op jit(solution)/shard_map/ppermute | solution.py:33
  38.7 1.0 %copy-start.5 = (bf16[128,32,128]{2,1,0:T(8,128)(2,1)}, bf16[128,32,128]{2,1,0:T(8,128)(2,1)S(1)}, u32[]{:S(2)}) copy-start(bf16[128,32,128]{2,1,0:T(8,128)(2,1)S(1)} %collective-permute-done.4) | copy-start | bytes 3145732
  41.8 18.4 %collective-permute-start.6 = (bf16[128,32,128]{2,1,0:T(8,128)(2,1)S(1)}, bf16[128,32,128]{2,1,0:T(8,128)(2,1)}, u32[]{:S(2)}, u32[]{:S(2)}) collective-permute-start(bf16[128,32,128]{2,1,0:T(8,128)(2,1)S(1)} %add.26.far), channel_id=1, source_target_pairs={{0,32},{4,36},{8,40},{12,44},{16,48},{20,52},{24,56},{28,60},{32,0... | collective-permute-start | bytes 3145736 | tf_op jit(solution)/shard_map/ppermute | solution.py:33
  43.9 1.0 %copy-start.1 = (bf16[128,32,128]{2,1,0:T(8,128)(2,1)}, bf16[128,32,128]{2,1,0:T(8,128)(2,1)S(1)}, u32[]{:S(2)}) copy-start(bf16[128,32,128]{2,1,0:T(8,128)(2,1)S(1)} %collective-permute-done.5.twin_pair) | copy-start | bytes 3145732
  60.2 1.2 %copy-start.2 = (bf16[128,32,128]{2,1,0:T(8,128)(2,1)S(1)}, bf16[128,32,128]{2,1,0:T(8,128)(2,1)}, u32[]{:S(2)}) copy-start(bf16[128,32,128]{2,1,0:T(8,128)(2,1)} %copy-done.1) | copy-start | bytes 3145732
  66.5 13.9 %collective-permute-start.7 = (f32[2,16,32,128]{3,2,1,0:T(8,128)S(1)}, f32[2,16,32,128]{3,2,1,0:T(8,128)S(1)}, u32[]{:S(2)}, u32[]{:S(2)}) collective-permute-start(f32[2,16,32,128]{3,2,1,0:T(8,128)S(1)} %get-tuple-element.14), channel_id=1, source_target_pairs={{0,256},{4,260},{8,264},{12,268},{16,272},{20,276},{24,280},{28,28... | collective-permute-start | bytes 1572872 | tf_op jit(solution)/shard_map/ppermute | solution.py:33
  80.4 9.5 %collective-permute-start.8 = (f32[16,32,128]{2,1,0:T(8,128)S(1)}, f32[16,32,128]{2,1,0:T(8,128)S(1)}, u32[]{:S(2)}, u32[]{:S(2)}) collective-permute-start(f32[16,32,128]{2,1,0:T(8,128)S(1)} %fusion), channel_id=1, source_target_pairs={{0,768},{4,772},{8,776},{12,780},{16,784},{20,788},{24,792},{28,79... | collective-permute-start | bytes 786440 | tf_op jit(solution)/shard_map/ppermute | solution.py:33

commit v8 on v3

--- a/solution.py
+++ b/solution.py
@@ -35,12 +35,7 @@
 
 
 def along_z(turn):
-    def move(x, z, core, y):
-        if core == turn:
-            return x, z ^ 1, core, y
-        return x, (z + 1 if z % 2 else z - 1), core, y
-
-    return move
+    return lambda x, z, core, y: (x, z ^ (1 if core == turn else 3), core, y)
 
 
 def spread(x, z, core, y):
@@ -152,7 +147,7 @@
             pltpu.VMEM((NEAR, RANGE, BS, LANES), jnp.bfloat16),
             pltpu.SemaphoreType.DMA((NEAR,)),
         ],
-        compiler_params=pltpu.CompilerParams(vmem_limit_bytes=20 * 1024 * 1024),
+        compiler_params=pltpu.CompilerParams(vmem_limit_bytes=12 * 1024 * 1024),
         name="range_products",
     )(place, shifts, masks, left, pair, far, twin_pair, twin_far)
     return jnp.sum(swapped_along_x(parts), axis=0).astype(jnp.bfloat16)

time: 92.5 us -> 85.6 us (0.925)
  the two profiles are of different devices: /device:TPU:2 before, /device:TPU:64 now
where the time goes in v8:
time: 85.6 us; the launch traced here: 85.1 us
  waiting for transfers between devices  26.6 us (31%)
  starting transfers between devices  25.2 us (29%)
  blocking collectives  19.2 us (22%)
  Pallas kernels  8.18 us (10%)
  local copies, waits for them, and re-layouts  4.44 us (5%)
  other arithmetic  1.36 us (2%)
    ppermute x5, waiting for transfers between devices, sent(): return lax.ppermute(value, AXES, device_pairs(move))  22.1 us
    ppermute x5, starting transfers between devices, sent(): return lax.ppermute(value, AXES, device_pairs(move))  20.7 us
    all_to_all x1, blocking collectives, swapped_along_x(): return lax.all_to_all(value, 'row', 0, 0, axis_index_groups=groups)  19.2 us
    pallas_call x1, Pallas kernels, local(): pl.pallas_call(product_kernel, out_shape=jax.ShapeDtypeStruct((NX, SPAN,...  5.95 us
    all_to_all x1, waiting for transfers between devices, local(): lax.all_to_all(jnp.broadcast_to(mine[None], (NY, SPAN, BS, LANES)), 'col'...  4.56 us
    all_to_all x1, starting transfers between devices, local(): lax.all_to_all(jnp.broadcast_to(mine[None], (NY, SPAN, BS, LANES)), 'col'...  4.51 us
    unnamed x13, local copies, waits for them, and re-layouts  2.28 us
    pallas_call x1, Pallas kernels, local(): pl.pallas_call(mask_kernel, out_shape=jax.ShapeDtypeStruct((NX, NEAR, BS,...  2.23 us
  transfers between devices with their start and end apart: 6, of which 3 were waited for; matrix products, arithmetic and copies ran while one was open for 3% of the time, Pallas kernels for 3%

profile of v8, /device:TPU:64, one launch (start us, length us, event | category | flops | bytes accessed | tf_op | source)
XLA Modules:
  0.0 85.1 jit_solution(5442950571955213916)
XLA Ops:
  0.0 14.3 %collective-permute-start = (bf16[64,32,128]{2,1,0:T(8,128)(2,1)}, bf16[64,32,128]{2,1,0:T(8,128)(2,1)S(1)}, u32[]{:S(2)}, u32[]{:S(2)}) collective-permute-start(bf16[64,32,128]{2,1,0:T(8,128)(2,1)} %param.2), channel_id=1, source_target_pairs={{0,64},{4,68},{8,72},{12,76},{16,80},{20,84},{24,88},{28,92},{32,2... | collective-permute-start | bytes 1572872 | tf_op jit(solution)/shard_map/ppermute | solution.py:30
  14.3 0.9 %constant_dynamic-slice_fusion = bf16[16,32,128]{2,1,0:T(8,128)(2,1)S(1)} fusion(bf16[64,32,128]{2,1,0:T(8,128)(2,1)} %param.2, s32[]{:T(128)S(6)} %select_n.3), kind=kLoop, calls=%fused_computation.3 | loop fusion | bytes 262148 | tf_op jit(solution)/shard_map/dynamic_slice | solution.py:125
  15.3 0.7 collective-permute-start.1
  16.0 0.6 pad_add_fusion.place_ref
  16.6 2.2 %masks.1 = bf16[4,8,32,128]{3,2,1,0:T(8,128)(2,1)} custom-call(s32[3]{0:T(128)} %pad_add_fusion.place_ref, s32[32,32]{1,0:T(8,128)} %shifts_ref.3), custom_call_target="tpu_custom_call" | custom-call | tf_op jit(solution)/shard_map/masks/pallas_call | solution.py:127
  18.8 0.0 collective-permute-done.1
  18.8 3.7 %collective-permute-done = bf16[64,32,128]{2,1,0:T(8,128)(2,1)S(1)} collective-permute-done((bf16[64,32,128]{2,1,0:T(8,128)(2,1)}, bf16[64,32,128]{2,1,0:T(8,128)(2,1)S(1)}, u32[]{:S(2)}, u32[]{:S(2)}) %collective-permute-start) | collective-permute-done | bytes 524320 | tf_op jit(solution)/shard_map/ppermute | solution.py:30
  22.5 0.1 constant_dynamic-update-slice_fusion.pair
  22.6 1.9 %collective-permute-start.2 = (bf16[128,32,128]{2,1,0:T(8,128)(2,1)S(1)}, bf16[128,32,128]{2,1,0:T(8,128)(2,1)S(1)}, u32[]{:S(2)}, u32[]{:S(2)}) collective-permute-start(bf16[128,32,128]{2,1,0:T(8,128)(2,1)S(1)} %constant_dynamic-update-slice_fusion.pair), channel_id=1, source_target_pairs={{0,192},{4,196},{8,200},{12,204},{16,208},{20,212},{24,216},{28,22... | collective-permute-start | bytes 3145736 | tf_op jit(solution)/shard_map/ppermute | solution.py:30
  24.5 1.2 %broadcast_in_dim.2 = bf16[8,16,32,128]{3,2,1,0:T(8,128)(2,1)} broadcast(bf16[16,32,128]{2,1,0:T(8,128)(2,1)S(1)} %collective-permute-done.1), dimensions={1,2,3} | broadcast | bytes 1179648 | tf_op jit(solution)/shard_map/broadcast_in_dim | solution.py:136
  25.7 4.5 %all-to-all-start = ((bf16[8,16,32,128]{3,2,1,0:T(8,128)(2,1)}), bf16[8,16,32,128]{3,2,1,0:T(8,128)(2,1)S(1)}, u32[]{:S(2)}, u32[]{:S(2)}) async-start(bf16[8,16,32,128]{3,2,1,0:T(8,128)(2,1)} %broadcast_in_dim.2), calls=%async_computation | async-start | bytes 2097152 | tf_op jit(solution)/shard_map/all_to_all | solution.py:136
  30.2 1.9 %collective-permute-start.3 = (bf16[128,32,128]{2,1,0:T(8,128)(2,1)S(1)}, bf16[128,32,128]{2,1,0:T(8,128)(2,1)S(1)}, u32[]{:S(2)}, u32[]{:S(2)}) collective-permute-start(bf16[128,32,128]{2,1,0:T(8,128)(2,1)S(1)} %constant_dynamic-update-slice_fusion.pair), channel_id=1, source_target_pairs={{0,32},{4,36},{8,40},{12,44},{16,48},{20,52},{24,56},{28,60},{32,0... | collective-permute-start | bytes 3145736 | tf_op jit(solution)/shard_map/ppermute | solution.py:30
  32.1 18.4 %collective-permute-done.2.far = bf16[128,32,128]{2,1,0:T(8,128)(2,1)S(1)} collective-permute-done((bf16[128,32,128]{2,1,0:T(8,128)(2,1)S(1)}, bf16[128,32,128]{2,1,0:T(8,128)(2,1)S(1)}, u32[]{:S(2)}, u32[]{:S(2)}) %collective-permute-start.2) | collective-permute-done | bytes 1048608 | tf_op jit(solution)/shard_map/ppermute | solution.py:30
  50.5 1.9 %collective-permute-start.4 = (bf16[128,32,128]{2,1,0:T(8,128)(2,1)S(1)}, bf16[128,32,128]{2,1,0:T(8,128)(2,1)}, u32[]{:S(2)}, u32[]{:S(2)}) collective-permute-start(bf16[128,32,128]{2,1,0:T(8,128)(2,1)S(1)} %collective-permute-done.2.far), channel_id=1, source_target_pairs={{0,32},{4,36},{8,40},{12,44},{16,48},{20,52},{24,56},{28,60},{32,0... | collective-permute-start | bytes 3145736 | tf_op jit(solution)/shard_map/ppermute | solution.py:30
  52.4 0.0 collective-permute-done.3.twin_pair
  52.4 0.0 copy-start
  52.4 1.0 %copy-done = bf16[128,32,128]{2,1,0:T(8,128)(2,1)} copy-done((bf16[128,32,128]{2,1,0:T(8,128)(2,1)}, bf16[128,32,128]{2,1,0:T(8,128)(2,1)S(1)}, u32[]{:S(2)}) %copy-start) | copy-done | bytes 1048600
  53.5 4.6 %all-to-all-done.left = bf16[8,16,32,128]{3,2,1,0:T(8,128)(2,1)S(1)} async-done(((bf16[8,16,32,128]{3,2,1,0:T(8,128)(2,1)}), bf16[8,16,32,128]{3,2,1,0:T(8,128)(2,1)S(1)}, u32[]{:S(2)}, u32[]{:S(2)}) %all-to-all-start) | async-done | bytes 1048608 | tf_op jit(solution)/shard_map/all_to_all | solution.py:136
  58.0 0.0 collective-permute-done.4.twin_far
  58.0 0.0 copy-done.3
  58.0 1.2 %copy-done.1 = bf16[128,32,128]{2,1,0:T(8,128)(2,1)S(1)} copy-done((bf16[128,32,128]{2,1,0:T(8,128)(2,1)S(1)}, bf16[128,32,128]{2,1,0:T(8,128)(2,1)}, u32[]{:S(2)}) %copy-start.1) | copy-done | bytes 1048600
  59.3 6.0 %range_products.1 = f32[4,16,32,128]{3,2,1,0:T(8,128)S(1)} custom-call(s32[3]{0:T(128)S(1)} %copy-done.4, s32[32,32]{1,0:T(8,128)S(1)} %copy-done.3, bf16[4,8,32,128]{3,2,1,0:T(8,128)(2,1)S(1)} %copy-done.2, bf16[8,16,32,128]{3,2,1,0:T(8,128)(2,1)S(1)} %all-to-all-done.left, bf16[128,32,128]{2,1,0:T(8,128)(2,1)S(1)} %constant_dynamic-update-slice_fusion.pair, ...), custom_call_target="tpu_custom_call" | custom-call | tf_op jit(solution)/shard_map/range_products/pallas_call | solution.py:141
  65.2 19.2 %all_to_all.10 = f32[4,16,32,128]{3,2,1,0:T(8,128)S(1)} all-to-all(f32[4,16,32,128]{3,2,1,0:T(8,128)S(1)} %range_products.1), channel_id=1, replica_groups={{0,256,512,768},{32,288,544,800},{64,320,576,832},{96,352,608,864},{128..., dimensions={0} | all-to-all | bytes 2097152 | tf_op jit(solution)/shard_map/all_to_all | solution.py:49
  84.4 0.8 reduce_sum.9
  (9 shorter events, 0.0 us)
Async XLA Ops:
  0.0 18.8 %copy-start.5 = (bf16[64,32,128]{2,1,0:T(8,128)(2,1)S(1)}, bf16[64,32,128]{2,1,0:T(8,128)(2,1)}, u32[]{:S(2)}) copy-start(bf16[64,32,128]{2,1,0:T(8,128)(2,1)} %param.2) | copy-start | bytes 1572868
  0.0 22.5 %collective-permute-start = (bf16[64,32,128]{2,1,0:T(8,128)(2,1)}, bf16[64,32,128]{2,1,0:T(8,128)(2,1)S(1)}, u32[]{:S(2)}, u32[]{:S(2)}) collective-permute-start(bf16[64,32,128]{2,1,0:T(8,128)(2,1)} %param.2), channel_id=1, source_target_pairs={{0,64},{4,68},{8,72},{12,76},{16,80},{20,84},{24,88},{28,92},{32,2... | collective-permute-start | bytes 1572872 | tf_op jit(solution)/shard_map/ppermute | solution.py:30
  15.3 3.6 %collective-permute-start.1 = (bf16[16,32,128]{2,1,0:T(8,128)(2,1)S(1)}, bf16[16,32,128]{2,1,0:T(8,128)(2,1)S(1)}, u32[]{:S(2)}, u32[]{:S(2)}) collective-permute-start(bf16[16,32,128]{2,1,0:T(8,128)(2,1)S(1)} %constant_dynamic-slice_fusion), channel_id=1, source_target_pairs={{0,0},{4,4},{8,284},{12,280},{16,520},{20,540},{24,788},{28,768},{... | collective-permute-start | bytes 393224 | tf_op jit(solution)/shard_map/ppermute | solution.py:30
  22.6 27.9 %collective-permute-start.2 = (bf16[128,32,128]{2,1,0:T(8,128)(2,1)S(1)}, bf16[128,32,128]{2,1,0:T(8,128)(2,1)S(1)}, u32[]{:S(2)}, u32[]{:S(2)}) collective-permute-start(bf16[128,32,128]{2,1,0:T(8,128)(2,1)S(1)} %constant_dynamic-update-slice_fusion.pair), channel_id=1, source_target_pairs={{0,192},{4,196},{8,200},{12,204},{16,208},{20,212},{24,216},{28,22... | collective-permute-start | bytes 3145736 | tf_op jit(solution)/shard_map/ppermute | solution.py:30
  25.7 32.3 %copy-start.2 = (bf16[4,8,32,128]{3,2,1,0:T(8,128)(2,1)S(1)}, bf16[4,8,32,128]{3,2,1,0:T(8,128)(2,1)}, u32[]{:S(2)}) copy-start(bf16[4,8,32,128]{3,2,1,0:T(8,128)(2,1)} %masks.1) | copy-start | bytes 786436
  25.7 32.3 %copy-start.3 = (s32[32,32]{1,0:T(8,128)S(1)}, s32[32,32]{1,0:T(8,128)}, u32[]{:S(2)}) copy-start(s32[32,32]{1,0:T(8,128)} %shifts_ref.3) | copy-start | bytes 12292
  25.7 32.3 %copy-start.4 = (s32[3]{0:T(128)S(1)}, s32[3]{0:T(128)}, u32[]{:S(2)}) copy-start(s32[3]{0:T(128)} %pad_add_fusion.place_ref) | copy-start | bytes 40
  25.7 32.3 %all-to-all-start = ((bf16[8,16,32,128]{3,2,1,0:T(8,128)(2,1)}), bf16[8,16,32,128]{3,2,1,0:T(8,128)(2,1)S(1)}, u32[]{:S(2)}, u32[]{:S(2)}) async-start(bf16[8,16,32,128]{3,2,1,0:T(8,128)(2,1)} %broadcast_in_dim.2), calls=%async_computation | async-start | bytes 2097152 | tf_op jit(solution)/shard_map/all_to_all | solution.py:136
  30.2 22.2 %collective-permute-start.3 = (bf16[128,32,128]{2,1,0:T(8,128)(2,1)S(1)}, bf16[128,32,128]{2,1,0:T(8,128)(2,1)S(1)}, u32[]{:S(2)}, u32[]{:S(2)}) collective-permute-start(bf16[128,32,128]{2,1,0:T(8,128)(2,1)S(1)} %constant_dynamic-update-slice_fusion.pair), channel_id=1, source_target_pairs={{0,32},{4,36},{8,40},{12,44},{16,48},{20,52},{24,56},{28,60},{32,0... | collective-permute-start | bytes 3145736 | tf_op jit(solution)/shard_map/ppermute | solution.py:30
  50.5 7.5 %collective-permute-start.4 = (bf16[128,32,128]{2,1,0:T(8,128)(2,1)S(1)}, bf16[128,32,128]{2,1,0:T(8,128)(2,1)}, u32[]{:S(2)}, u32[]{:S(2)}) collective-permute-start(bf16[128,32,128]{2,1,0:T(8,128)(2,1)S(1)} %collective-permute-done.2.far), channel_id=1, source_target_pairs={{0,32},{4,36},{8,40},{12,44},{16,48},{20,52},{24,56},{28,60},{32,0... | collective-permute-start | bytes 3145736 | tf_op jit(solution)/shard_map/ppermute | solution.py:30
  52.4 1.0 %copy-start = (bf16[128,32,128]{2,1,0:T(8,128)(2,1)}, bf16[128,32,128]{2,1,0:T(8,128)(2,1)S(1)}, u32[]{:S(2)}) copy-start(bf16[128,32,128]{2,1,0:T(8,128)(2,1)S(1)} %collective-permute-done.3.twin_pair) | copy-start | bytes 3145732
  58.0 1.2 %copy-start.1 = (bf16[128,32,128]{2,1,0:T(8,128)(2,1)S(1)}, bf16[128,32,128]{2,1,0:T(8,128)(2,1)}, u32[]{:S(2)}) copy-start(bf16[128,32,128]{2,1,0:T(8,128)(2,1)} %copy-done) | copy-start | bytes 3145732

commit v9 on v8

--- a/solution.py
+++ b/solution.py
@@ -72,24 +72,24 @@
 
 
 def product_kernel(
-    place_ref, shifts_ref, masks, left, pair, far, twin_pair, twin_far, out, right, sems
+    place_ref, shifts_ref, masks, left, own, near, far, last, twins, twin_last, out, right, sems
 ):
     row = place_ref[0]
     layer = place_ref[2]
     core = row & 1
     zl = (row >> 1) & 3
     x = row >> 3
-    near = x * NEAR
+    base = x * NEAR
 
     first = jnp.where(core == 0, 1, 3)
     second = jnp.where(core == 0, 3, 1)
-    pieces = [(pair, 0, 0, core), (pair, 1, first, core), (far, 0, second, core), (far, 1, 2, core)]
-    pieces += [(twin_pair, 0, 0, 1 - core), (twin_pair, 1, second, 1 - core)]
-    pieces += [(twin_far, 0, first, 1 - core), (twin_far, 1, 2, 1 - core)]
+    pieces = [(own, 0, 0, core), (near, 0, first, core), (far, 0, second, core), (last, 0, 2, core)]
+    pieces += [(twins, n, turn, 1 - core) for n, turn in enumerate((0, second, first))]
+    pieces += [(twin_last, 0, 2, 1 - core)]
     copies = []
-    for n, (piece, half, turn, parity) in enumerate(pieces):
+    for n, (piece, block, turn, parity) in enumerate(pieces):
         slot = (zl ^ turn) * 2 + parity
-        copies.append(pltpu.make_async_copy(piece.at[pl.ds(half * RANGE, RANGE)], right.at[slot], sems.at[n]))
+        copies.append(pltpu.make_async_copy(piece.at[pl.ds(block * RANGE, RANGE)], right.at[slot], sems.at[n]))
     for copy in copies:
         copy.start()
     for copy in copies:
@@ -104,7 +104,7 @@
             lhs = jnp.concatenate([left[low, p], left[high, p]], axis=1)
             rows = []
             for j in range(NEAR):
-                q = (place + shifts_ref[target, near + j]) & (RANGE - 1)
+                q = (place + shifts_ref[target, base + j]) & (RANGE - 1)
                 rows.append(right[j, q] * masks[t, j])
             rhs = jnp.concatenate(rows, axis=0)
             out[t, p] = jnp.dot(lhs, rhs, preferred_element_type=jnp.float32)
@@ -132,16 +132,17 @@
         name="masks",
     )(place, shifts)
     near = sent(x_blocks, along_z(0))
-    near, masks, mine = lax.optimization_barrier((near, masks, mine))
-    left = lax.all_to_all(jnp.broadcast_to(mine[None], (NY, SPAN, BS, LANES)), "col", 0, 0)
-    pair = jnp.concatenate([x_blocks, near], axis=0)
-    far = sent(pair, along_z(1))
-    twin_pair = sent(pair, other_core)
-    twin_far = sent(far, other_core)
+    far = sent(x_blocks, along_z(1))
+    mine = jnp.broadcast_to(mine[None], (NY, SPAN, BS, LANES))
+    near, masks = lax.optimization_barrier((near, masks))
+    left = lax.all_to_all(mine, "col", 0, 0)
+    last = sent(near, along_z(1))
+    twins = sent(jnp.concatenate([x_blocks, near, far], axis=0), other_core)
+    twin_last = sent(last, other_core)
     parts = pl.pallas_call(
         product_kernel,
         out_shape=jax.ShapeDtypeStruct((NX, SPAN, BS, LANES), jnp.float32),
-        in_specs=[smem, smem] + [vmem] * 2 + [anywhere] * 4,
+        in_specs=[smem, smem] + [vmem] * 2 + [anywhere] * 6,
         out_specs=vmem,
         scratch_shapes=[
             pltpu.VMEM((NEAR, RANGE, BS, LANES), jnp.bfloat16),
@@ -149,7 +150,7 @@
         ],
         compiler_params=pltpu.CompilerParams(vmem_limit_bytes=12 * 1024 * 1024),
         name="range_products",
-    )(place, shifts, masks, left, pair, far, twin_pair, twin_far)
+    )(place, shifts, masks, left, x_blocks, near, far, last, twins, twin_last)
     return jnp.sum(swapped_along_x(parts), axis=0).astype(jnp.bfloat16)
 
 

time: 85.6 us -> 86.7 us (1.013)
  the two profiles are of different devices: /device:TPU:64 before, /device:TPU:1 now
where the time goes in v9:
time: 86.7 us; the launch traced here: 85.8 us
  starting transfers between devices  39.3 us (45%)
  blocking collectives  18.6 us (21%)
  waiting for transfers between devices  12.8 us (15%)
  Pallas kernels  8.27 us (10%)
  local copies, waits for them, and re-layouts  3.95 us (5%)
  other arithmetic  2.7 us (3%)
    ppermute x6, starting transfers between devices, sent(): return lax.ppermute(value, AXES, device_pairs(move))  22.2 us
    all_to_all x1, blocking collectives, swapped_along_x(): return lax.all_to_all(value, 'row', 0, 0, axis_index_groups=groups)  18.6 us
    all_to_all x1, starting transfers between devices, local(): left = lax.all_to_all(mine, 'col', 0, 0)  17 us
    ppermute x6, waiting for transfers between devices, sent(): return lax.ppermute(value, AXES, device_pairs(move))  12.8 us
    pallas_call x1, Pallas kernels, local(): pl.pallas_call(product_kernel, out_shape=jax.ShapeDtypeStruct((NX, SPAN,...  6.04 us
    pallas_call x1, Pallas kernels, local(): pl.pallas_call(mask_kernel, out_shape=jax.ShapeDtypeStruct((NX, NEAR, BS,...  2.24 us
    unnamed x12, local copies, waits for them, and re-layouts  1.85 us
  transfers between devices with their start and end apart: 7, of which 2 were waited for; matrix products, arithmetic and copies ran while one was open for 5% of the time, Pallas kernels for 3%

profile of v9, /device:TPU:1, one launch (start us, length us, event | category | flops | bytes accessed | tf_op | source)
XLA Modules:
  0.0 85.8 jit_solution(18027840423699419322)
XLA Ops:
  0.0 8.4 %collective-permute-start = (bf16[64,32,128]{2,1,0:T(8,128)(2,1)}, bf16[64,32,128]{2,1,0:T(8,128)(2,1)S(1)}, u32[]{:S(2)}, u32[]{:S(2)}) collective-permute-start(bf16[64,32,128]{2,1,0:T(8,128)(2,1)} %own.1), channel_id=1, source_target_pairs={{0,64},{4,68},{8,72},{12,76},{16,80},{20,84},{24,88},{28,92},{32,2... | collective-permute-start | bytes 1572872 | tf_op jit(solution)/shard_map/ppermute | solution.py:30
  8.4 1.9 %collective-permute-start.2 = (bf16[64,32,128]{2,1,0:T(8,128)(2,1)}, bf16[64,32,128]{2,1,0:T(8,128)(2,1)S(1)}, u32[]{:S(2)}, u32[]{:S(2)}) collective-permute-start(bf16[64,32,128]{2,1,0:T(8,128)(2,1)} %own.1), channel_id=1, source_target_pairs={{0,192},{4,196},{8,200},{12,204},{16,208},{20,212},{24,216},{28,22... | collective-permute-start | bytes 1572872 | tf_op jit(solution)/shard_map/ppermute | solution.py:30
  10.4 0.9 %constant_dynamic-slice_fusion = bf16[16,32,128]{2,1,0:T(8,128)(2,1)S(1)} fusion(bf16[64,32,128]{2,1,0:T(8,128)(2,1)} %own.1, s32[]{:T(128)S(6)} %select_n.3), kind=kLoop, calls=%fused_computation.2 | loop fusion | bytes 262148 | tf_op jit(solution)/shard_map/dynamic_slice | solution.py:125
  11.3 0.7 collective-permute-start.1
  12.0 0.0 copy-start
  12.0 0.0 collective-permute-done.1
  12.0 1.2 %broadcast_in_dim.2 = bf16[8,16,32,128]{3,2,1,0:T(8,128)(2,1)} broadcast(bf16[16,32,128]{2,1,0:T(8,128)(2,1)S(1)} %collective-permute-done.1), dimensions={1,2,3} | broadcast | bytes 1179648 | tf_op jit(solution)/shard_map/broadcast_in_dim | solution.py:136
  13.2 17.0 %all-to-all-start = ((bf16[8,16,32,128]{3,2,1,0:T(8,128)(2,1)}), bf16[8,16,32,128]{3,2,1,0:T(8,128)(2,1)S(1)}, u32[]{:S(2)}, u32[]{:S(2)}) async-start(bf16[8,16,32,128]{3,2,1,0:T(8,128)(2,1)} %broadcast_in_dim.2), calls=%async_computation | async-start | bytes 2097152 | tf_op jit(solution)/shard_map/all_to_all | solution.py:138
  30.2 0.6 pad_add_fusion.place_ref
  30.8 2.2 %masks.1 = bf16[4,8,32,128]{3,2,1,0:T(8,128)(2,1)} custom-call(s32[3]{0:T(128)} %pad_add_fusion.place_ref, s32[32,32]{1,0:T(8,128)} %shifts_ref.3), custom_call_target="tpu_custom_call" | custom-call | tf_op jit(solution)/shard_map/masks/pallas_call | solution.py:127
  33.1 0.0 collective-permute-done.near
  33.1 0.0 collective-permute-done.2.far
  33.1 1.3 %pad_maximum_fusion = bf16[192,32,128]{2,1,0:T(8,128)(2,1)} fusion(bf16[64,32,128]{2,1,0:T(8,128)(2,1)S(1)} %collective-permute-done.2.far, bf16[64,32,128]{2,1,0:T(8,128)(2,1)S(1)} %collective-permute-done.near, bf16[64,32,128]{2,1,0:T(8,128)(2,1)S(1)} %copy-done), kind=kLoop, calls=%fused_computation | loop fusion | flops 1572864 | bytes 3145728 | tf_op jit(solution)/shard_map/concatenate | solution.py:140
  34.4 4.3 %collective-permute-start.4 = (bf16[192,32,128]{2,1,0:T(8,128)(2,1)}, bf16[192,32,128]{2,1,0:T(8,128)(2,1)}, u32[]{:S(2)}, u32[]{:S(2)}) collective-permute-start(bf16[192,32,128]{2,1,0:T(8,128)(2,1)} %pad_maximum_fusion), channel_id=1, source_target_pairs={{0,32},{4,36},{8,40},{12,44},{16,48},{20,52},{24,56},{28,60},{32,0... | collective-permute-start | bytes 4718600 | tf_op jit(solution)/shard_map/ppermute | solution.py:30
  38.7 3.4 %collective-permute-start.3 = (bf16[64,32,128]{2,1,0:T(8,128)(2,1)S(1)}, bf16[64,32,128]{2,1,0:T(8,128)(2,1)S(1)}, u32[]{:S(2)}, u32[]{:S(2)}) collective-permute-start(bf16[64,32,128]{2,1,0:T(8,128)(2,1)S(1)} %collective-permute-done.near), channel_id=1, source_target_pairs={{0,192},{4,196},{8,200},{12,204},{16,208},{20,212},{24,216},{28,22... | collective-permute-start | bytes 1572872 | tf_op jit(solution)/shard_map/ppermute | solution.py:30
  42.1 11.3 %collective-permute-done.3.last = bf16[64,32,128]{2,1,0:T(8,128)(2,1)S(1)} collective-permute-done((bf16[64,32,128]{2,1,0:T(8,128)(2,1)S(1)}, bf16[64,32,128]{2,1,0:T(8,128)(2,1)S(1)}, u32[]{:S(2)}, u32[]{:S(2)}) %collective-permute-start.3) | collective-permute-done | bytes 524320 | tf_op jit(solution)/shard_map/ppermute | solution.py:30
  53.4 3.6 %collective-permute-start.5 = (bf16[64,32,128]{2,1,0:T(8,128)(2,1)S(1)}, bf16[64,32,128]{2,1,0:T(8,128)(2,1)S(1)}, u32[]{:S(2)}, u32[]{:S(2)}) collective-permute-start(bf16[64,32,128]{2,1,0:T(8,128)(2,1)S(1)} %collective-permute-done.3.last), channel_id=1, source_target_pairs={{0,32},{4,36},{8,40},{12,44},{16,48},{20,52},{24,56},{28,60},{32,0... | collective-permute-start | bytes 1572872 | tf_op jit(solution)/shard_map/ppermute | solution.py:30
  57.0 1.5 %collective-permute-done.5.twin_last = bf16[64,32,128]{2,1,0:T(8,128)(2,1)S(1)} collective-permute-done((bf16[64,32,128]{2,1,0:T(8,128)(2,1)S(1)}, bf16[64,32,128]{2,1,0:T(8,128)(2,1)S(1)}, u32[]{:S(2)}, u32[]{:S(2)}) %collective-permute-start.5) | collective-permute-done | bytes 524320 | tf_op jit(solution)/shard_map/ppermute | solution.py:30
  58.5 0.8 copy-done.2
  59.3 0.0 all-to-all-done.left
  59.3 1.0 %copy-done.3 = bf16[64,32,128]{2,1,0:T(8,128)(2,1)S(1)} copy-done((bf16[64,32,128]{2,1,0:T(8,128)(2,1)S(1)}, bf16[64,32,128]{2,1,0:T(8,128)(2,1)}, u32[]{:S(2)}) %copy-start.3) | copy-done | bytes 524312
  60.4 6.0 %range_products.1 = f32[4,16,32,128]{3,2,1,0:T(8,128)S(1)} custom-call(s32[3]{0:T(128)S(1)} %copy-done.5, s32[32,32]{1,0:T(8,128)S(1)} %copy-done.4, bf16[4,8,32,128]{3,2,1,0:T(8,128)(2,1)S(1)} %copy-done.1, bf16[8,16,32,128]{3,2,1,0:T(8,128)(2,1)S(1)} %all-to-all-done.left, bf16[64,32,128]{2,1,0:T(8,128)(2,1)S(1)} %copy-done, ...), custom_call_target="tpu_custom_call" | custom-call | tf_op jit(solution)/shard_map/range_products/pallas_call | solution.py:142
  66.4 18.6 %all_to_all.10 = f32[4,16,32,128]{3,2,1,0:T(8,128)S(1)} all-to-all(f32[4,16,32,128]{3,2,1,0:T(8,128)S(1)} %range_products.1), channel_id=1, replica_groups={{0,256,512,768},{32,288,544,800},{64,320,576,832},{96,352,608,864},{128..., dimensions={0} | all-to-all | bytes 2097152 | tf_op jit(solution)/shard_map/all_to_all | solution.py:49
  85.0 0.8 reduce_sum.9
  (10 shorter events, 0.0 us)
Async XLA Ops:
  0.0 33.1 %collective-permute-start = (bf16[64,32,128]{2,1,0:T(8,128)(2,1)}, bf16[64,32,128]{2,1,0:T(8,128)(2,1)S(1)}, u32[]{:S(2)}, u32[]{:S(2)}) collective-permute-start(bf16[64,32,128]{2,1,0:T(8,128)(2,1)} %own.1), channel_id=1, source_target_pairs={{0,64},{4,68},{8,72},{12,76},{16,80},{20,84},{24,88},{28,92},{32,2... | collective-permute-start | bytes 1572872 | tf_op jit(solution)/shard_map/ppermute | solution.py:30
  8.4 24.7 %collective-permute-start.2 = (bf16[64,32,128]{2,1,0:T(8,128)(2,1)}, bf16[64,32,128]{2,1,0:T(8,128)(2,1)S(1)}, u32[]{:S(2)}, u32[]{:S(2)}) collective-permute-start(bf16[64,32,128]{2,1,0:T(8,128)(2,1)} %own.1), channel_id=1, source_target_pairs={{0,192},{4,196},{8,200},{12,204},{16,208},{20,212},{24,216},{28,22... | collective-permute-start | bytes 1572872 | tf_op jit(solution)/shard_map/ppermute | solution.py:30
  11.3 0.7 collective-permute-start.1
  12.0 21.1 %copy-start = (bf16[64,32,128]{2,1,0:T(8,128)(2,1)S(1)}, bf16[64,32,128]{2,1,0:T(8,128)(2,1)}, u32[]{:S(2)}) copy-start(bf16[64,32,128]{2,1,0:T(8,128)(2,1)} %own.1) | copy-start | bytes 1572868
  13.2 46.1 %all-to-all-start = ((bf16[8,16,32,128]{3,2,1,0:T(8,128)(2,1)}), bf16[8,16,32,128]{3,2,1,0:T(8,128)(2,1)S(1)}, u32[]{:S(2)}, u32[]{:S(2)}) async-start(bf16[8,16,32,128]{3,2,1,0:T(8,128)(2,1)} %broadcast_in_dim.2), calls=%async_computation | async-start | bytes 2097152 | tf_op jit(solution)/shard_map/all_to_all | solution.py:138
  33.1 26.2 %copy-start.1 = (bf16[4,8,32,128]{3,2,1,0:T(8,128)(2,1)S(1)}, bf16[4,8,32,128]{3,2,1,0:T(8,128)(2,1)}, u32[]{:S(2)}) copy-start(bf16[4,8,32,128]{3,2,1,0:T(8,128)(2,1)} %masks.1) | copy-start | bytes 786436
  33.1 26.2 %copy-start.4 = (s32[32,32]{1,0:T(8,128)S(1)}, s32[32,32]{1,0:T(8,128)}, u32[]{:S(2)}) copy-start(s32[32,32]{1,0:T(8,128)} %shifts_ref.3) | copy-start | bytes 12292
  33.1 26.2 %copy-start.5 = (s32[3]{0:T(128)S(1)}, s32[3]{0:T(128)}, u32[]{:S(2)}) copy-start(s32[3]{0:T(128)} %pad_add_fusion.place_ref) | copy-start | bytes 40
  34.4 24.8 %collective-permute-start.4 = (bf16[192,32,128]{2,1,0:T(8,128)(2,1)}, bf16[192,32,128]{2,1,0:T(8,128)(2,1)}, u32[]{:S(2)}, u32[]{:S(2)}) collective-permute-start(bf16[192,32,128]{2,1,0:T(8,128)(2,1)} %pad_maximum_fusion), channel_id=1, source_target_pairs={{0,32},{4,36},{8,40},{12,44},{16,48},{20,52},{24,56},{28,60},{32,0... | collective-permute-start | bytes 4718600 | tf_op jit(solution)/shard_map/ppermute | solution.py:30
  38.7 14.7 %collective-permute-start.3 = (bf16[64,32,128]{2,1,0:T(8,128)(2,1)S(1)}, bf16[64,32,128]{2,1,0:T(8,128)(2,1)S(1)}, u32[]{:S(2)}, u32[]{:S(2)}) collective-permute-start(bf16[64,32,128]{2,1,0:T(8,128)(2,1)S(1)} %collective-permute-done.near), channel_id=1, source_target_pairs={{0,192},{4,196},{8,200},{12,204},{16,208},{20,212},{24,216},{28,22... | collective-permute-start | bytes 1572872 | tf_op jit(solution)/shard_map/ppermute | solution.py:30
  53.4 5.1 %collective-permute-start.5 = (bf16[64,32,128]{2,1,0:T(8,128)(2,1)S(1)}, bf16[64,32,128]{2,1,0:T(8,128)(2,1)S(1)}, u32[]{:S(2)}, u32[]{:S(2)}) collective-permute-start(bf16[64,32,128]{2,1,0:T(8,128)(2,1)S(1)} %collective-permute-done.3.last), channel_id=1, source_target_pairs={{0,32},{4,36},{8,40},{12,44},{16,48},{20,52},{24,56},{28,60},{32,0... | collective-permute-start | bytes 1572872 | tf_op jit(solution)/shard_map/ppermute | solution.py:30
  58.5 0.8 copy-start.2
  59.3 1.0 %copy-start.3 = (bf16[64,32,128]{2,1,0:T(8,128)(2,1)S(1)}, bf16[64,32,128]{2,1,0:T(8,128)(2,1)}, u32[]{:S(2)}) copy-start(bf16[64,32,128]{2,1,0:T(8,128)(2,1)} %copy-done.2) | copy-start | bytes 1572868

commit v10 on v9

--- a/solution.py
+++ b/solution.py
@@ -84,8 +84,8 @@
     first = jnp.where(core == 0, 1, 3)
     second = jnp.where(core == 0, 3, 1)
     pieces = [(own, 0, 0, core), (near, 0, first, core), (far, 0, second, core), (last, 0, 2, core)]
-    pieces += [(twins, n, turn, 1 - core) for n, turn in enumerate((0, second, first))]
-    pieces += [(twin_last, 0, 2, 1 - core)]
+    pieces += [(twins, 0, 0, 1 - core), (twins, 1, second, 1 - core)]
+    pieces += [(twin_last, 0, first, 1 - core), (twin_last, 1, 2, 1 - core)]
     copies = []
     for n, (piece, block, turn, parity) in enumerate(pieces):
         slot = (zl ^ turn) * 2 + parity
@@ -134,11 +134,11 @@
     near = sent(x_blocks, along_z(0))
     far = sent(x_blocks, along_z(1))
     mine = jnp.broadcast_to(mine[None], (NY, SPAN, BS, LANES))
-    near, masks = lax.optimization_barrier((near, masks))
+    near, far, masks = lax.optimization_barrier((near, far, masks))
     left = lax.all_to_all(mine, "col", 0, 0)
     last = sent(near, along_z(1))
-    twins = sent(jnp.concatenate([x_blocks, near, far], axis=0), other_core)
-    twin_last = sent(last, other_core)
+    twins = sent(jnp.concatenate([x_blocks, near], axis=0), other_core)
+    twin_last = sent(jnp.concatenate([far, last], axis=0), other_core)
     parts = pl.pallas_call(
         product_kernel,
         out_shape=jax.ShapeDtypeStruct((NX, SPAN, BS, LANES), jnp.float32),

time: 86.7 us -> 86.9 us (level)
  waiting for transfers between devices: 12.8 us -> 9.44 us
  starting transfers between devices: 39.3 us -> 41.2 us
  blocking collectives: 18.6 us -> 20.1 us
    ppermute x6, waiting for transfers between devices: 12.8 us -> 5.07 us  [sent(): return lax.ppermute(value, AXES, device_pairs(move))]
    all_to_all x1, waiting for transfers between devices: 0.01 us -> 4.36 us  [local(): left = lax.all_to_all(mine, 'col', 0, 0)]
    ppermute x6, starting transfers between devices: 22.2 us -> 24 us  [sent(): return lax.ppermute(value, AXES, device_pairs(move))]
    all_to_all x1, blocking collectives: 18.6 us -> 20.1 us  [swapped_along_x(): return lax.all_to_all(value, 'row', 0, 0, axis_index_groups=groups)]
where the time goes in v10:
time: 86.9 us; the launch traced here: 86 us
  starting transfers between devices  41.2 us (47%)
  blocking collectives  20.1 us (23%)
  waiting for transfers between devices  9.44 us (11%)
  Pallas kernels  8.18 us (9%)
  local copies, waits for them, and re-layouts  4.29 us (5%)
  other arithmetic  2.6 us (3%)
    ppermute x6, starting transfers between devices, sent(): return lax.ppermute(value, AXES, device_pairs(move))  24 us
    all_to_all x1, blocking collectives, swapped_along_x(): return lax.all_to_all(value, 'row', 0, 0, axis_index_groups=groups)  20.1 us
    all_to_all x1, starting transfers between devices, local(): left = lax.all_to_all(mine, 'col', 0, 0)  17.2 us
    pallas_call x1, Pallas kernels, local(): pl.pallas_call(product_kernel, out_shape=jax.ShapeDtypeStruct((NX, SPAN,...  5.95 us
    ppermute x6, waiting for transfers between devices, sent(): return lax.ppermute(value, AXES, device_pairs(move))  5.07 us
    all_to_all x1, waiting for transfers between devices, local(): left = lax.all_to_all(mine, 'col', 0, 0)  4.36 us
    pallas_call x1, Pallas kernels, local(): pl.pallas_call(mask_kernel, out_shape=jax.ShapeDtypeStruct((NX, NEAR, BS,...  2.23 us
    unnamed x12, local copies, waits for them, and re-layouts  2.22 us
  transfers between devices with their start and end apart: 7, of which 2 were waited for; matrix products, arithmetic and copies ran while one was open for 5% of the time, Pallas kernels for 3%

profile of v10, /device:TPU:1, one launch (start us, length us, event | category | flops | bytes accessed | tf_op | source)
XLA Modules:
  0.0 86.0 jit_solution(14317854585397016993)
XLA Ops:
  0.0 4.8 %collective-permute-start.1 = (bf16[64,32,128]{2,1,0:T(8,128)(2,1)}, bf16[64,32,128]{2,1,0:T(8,128)(2,1)S(1)}, u32[]{:S(2)}, u32[]{:S(2)}) collective-permute-start(bf16[64,32,128]{2,1,0:T(8,128)(2,1)} %own.1), channel_id=1, source_target_pairs={{0,192},{4,196},{8,200},{12,204},{16,208},{20,212},{24,216},{28,22... | collective-permute-start | bytes 1572872 | tf_op jit(solution)/shard_map/ppermute | solution.py:30
  4.8 5.5 %collective-permute-start = (bf16[64,32,128]{2,1,0:T(8,128)(2,1)}, bf16[64,32,128]{2,1,0:T(8,128)(2,1)S(1)}, u32[]{:S(2)}, u32[]{:S(2)}) collective-permute-start(bf16[64,32,128]{2,1,0:T(8,128)(2,1)} %own.1), channel_id=1, source_target_pairs={{0,64},{4,68},{8,72},{12,76},{16,80},{20,84},{24,88},{28,92},{32,2... | collective-permute-start | bytes 1572872 | tf_op jit(solution)/shard_map/ppermute | solution.py:30
  10.4 0.9 %constant_dynamic-slice_fusion = bf16[16,32,128]{2,1,0:T(8,128)(2,1)S(1)} fusion(bf16[64,32,128]{2,1,0:T(8,128)(2,1)} %own.1, s32[]{:T(128)S(6)} %select_n.3), kind=kLoop, calls=%fused_computation.3 | loop fusion | bytes 262148 | tf_op jit(solution)/shard_map/dynamic_slice | solution.py:125
  11.3 0.7 collective-permute-start.2
  12.0 0.0 collective-permute-done.2
  12.0 1.1 %broadcast_in_dim.2 = bf16[8,16,32,128]{3,2,1,0:T(8,128)(2,1)} broadcast(bf16[16,32,128]{2,1,0:T(8,128)(2,1)S(1)} %collective-permute-done.2), dimensions={1,2,3} | broadcast | bytes 1179648 | tf_op jit(solution)/shard_map/broadcast_in_dim | solution.py:136
  13.1 17.2 %all-to-all-start = ((bf16[8,16,32,128]{3,2,1,0:T(8,128)(2,1)}), bf16[8,16,32,128]{3,2,1,0:T(8,128)(2,1)S(1)}, u32[]{:S(2)}, u32[]{:S(2)}) async-start(bf16[8,16,32,128]{3,2,1,0:T(8,128)(2,1)} %broadcast_in_dim.2), calls=%async_computation | async-start | bytes 2097152 | tf_op jit(solution)/shard_map/all_to_all | solution.py:138
  30.3 0.7 pad_add_fusion.place_ref
  31.0 2.2 %masks.1 = bf16[4,8,32,128]{3,2,1,0:T(8,128)(2,1)} custom-call(s32[3]{0:T(128)} %pad_add_fusion.place_ref, s32[32,32]{1,0:T(8,128)} %shifts_ref.3), custom_call_target="tpu_custom_call" | custom-call | tf_op jit(solution)/shard_map/masks/pallas_call | solution.py:127
  33.2 0.0 collective-permute-done.1.far
  33.2 0.0 collective-permute-done.near
  33.2 2.5 %collective-permute-start.3 = (bf16[64,32,128]{2,1,0:T(8,128)(2,1)S(1)}, bf16[64,32,128]{2,1,0:T(8,128)(2,1)S(1)}, u32[]{:S(2)}, u32[]{:S(2)}) collective-permute-start(bf16[64,32,128]{2,1,0:T(8,128)(2,1)S(1)} %collective-permute-done.near), channel_id=1, source_target_pairs={{0,192},{4,196},{8,200},{12,204},{16,208},{20,212},{24,216},{28,22... | collective-permute-start | bytes 1572872 | tf_op jit(solution)/shard_map/ppermute | solution.py:30
  35.7 0.1 pad_maximum_fusion
  35.8 0.0 copy-start.4
  35.8 4.2 %collective-permute-start.4 = (bf16[128,32,128]{2,1,0:T(8,128)(2,1)S(1)}, bf16[128,32,128]{2,1,0:T(8,128)(2,1)S(1)}, u32[]{:S(2)}, u32[]{:S(2)}) collective-permute-start(bf16[128,32,128]{2,1,0:T(8,128)(2,1)S(1)} %pad_maximum_fusion), channel_id=1, source_target_pairs={{0,32},{4,36},{8,40},{12,44},{16,48},{20,52},{24,56},{28,60},{32,0... | collective-permute-start | bytes 3145736 | tf_op jit(solution)/shard_map/ppermute | solution.py:30
  40.0 5.1 %collective-permute-done.3.last = bf16[64,32,128]{2,1,0:T(8,128)(2,1)S(1)} collective-permute-done((bf16[64,32,128]{2,1,0:T(8,128)(2,1)S(1)}, bf16[64,32,128]{2,1,0:T(8,128)(2,1)S(1)}, u32[]{:S(2)}, u32[]{:S(2)}) %collective-permute-start.3) | collective-permute-done | bytes 524320 | tf_op jit(solution)/shard_map/ppermute | solution.py:30
  45.1 1.1 %pad_maximum_fusion.1 = bf16[128,32,128]{2,1,0:T(8,128)(2,1)} fusion(bf16[64,32,128]{2,1,0:T(8,128)(2,1)S(1)} %collective-permute-done.3.last, bf16[64,32,128]{2,1,0:T(8,128)(2,1)S(1)} %collective-permute-done.1.far), kind=kLoop, calls=%fused_computation.1 | loop fusion | flops 524288 | bytes 2097152 | tf_op jit(solution)/shard_map/concatenate | solution.py:141
  46.1 6.4 %collective-permute-start.5 = (bf16[128,32,128]{2,1,0:T(8,128)(2,1)}, bf16[128,32,128]{2,1,0:T(8,128)(2,1)}, u32[]{:S(2)}, u32[]{:S(2)}) collective-permute-start(bf16[128,32,128]{2,1,0:T(8,128)(2,1)} %pad_maximum_fusion.1), channel_id=1, source_target_pairs={{0,32},{4,36},{8,40},{12,44},{16,48},{20,52},{24,56},{28,60},{32,0... | collective-permute-start | bytes 3145736 | tf_op jit(solution)/shard_map/ppermute | solution.py:30
  52.6 1.0 %copy-done.1 = bf16[128,32,128]{2,1,0:T(8,128)(2,1)} copy-done((bf16[128,32,128]{2,1,0:T(8,128)(2,1)}, bf16[128,32,128]{2,1,0:T(8,128)(2,1)S(1)}, u32[]{:S(2)}) %copy-start.1) | copy-done | bytes 1048600
  53.6 4.4 %all-to-all-done.left = bf16[8,16,32,128]{3,2,1,0:T(8,128)(2,1)S(1)} async-done(((bf16[8,16,32,128]{3,2,1,0:T(8,128)(2,1)}), bf16[8,16,32,128]{3,2,1,0:T(8,128)(2,1)S(1)}, u32[]{:S(2)}, u32[]{:S(2)}) %all-to-all-start) | async-done | bytes 1048608 | tf_op jit(solution)/shard_map/all_to_all | solution.py:138
  58.0 1.2 %copy-done.2 = bf16[128,32,128]{2,1,0:T(8,128)(2,1)S(1)} copy-done((bf16[128,32,128]{2,1,0:T(8,128)(2,1)S(1)}, bf16[128,32,128]{2,1,0:T(8,128)(2,1)}, u32[]{:S(2)}) %copy-start.2) | copy-done | bytes 1048600
  59.2 5.9 %range_products.1 = f32[4,16,32,128]{3,2,1,0:T(8,128)S(1)} custom-call(s32[3]{0:T(128)S(1)} %copy-done.5, s32[32,32]{1,0:T(8,128)S(1)} %copy-done.4, bf16[4,8,32,128]{3,2,1,0:T(8,128)(2,1)S(1)} %copy-done.3, bf16[8,16,32,128]{3,2,1,0:T(8,128)(2,1)S(1)} %all-to-all-done.left, bf16[64,32,128]{2,1,0:T(8,128)(2,1)S(1)} %copy-done, ...), custom_call_target="tpu_custom_call" | custom-call | tf_op jit(solution)/shard_map/range_products/pallas_call | solution.py:142
  65.1 20.1 %all_to_all.10 = f32[4,16,32,128]{3,2,1,0:T(8,128)S(1)} all-to-all(f32[4,16,32,128]{3,2,1,0:T(8,128)S(1)} %range_products.1), channel_id=1, replica_groups={{0,256,512,768},{32,288,544,800},{64,320,576,832},{96,352,608,864},{128..., dimensions={0} | all-to-all | bytes 2097152 | tf_op jit(solution)/shard_map/all_to_all | solution.py:49
  85.2 0.8 reduce_sum.9
  (11 shorter events, 0.0 us)
Async XLA Ops:
  0.0 33.2 %collective-permute-start.1 = (bf16[64,32,128]{2,1,0:T(8,128)(2,1)}, bf16[64,32,128]{2,1,0:T(8,128)(2,1)S(1)}, u32[]{:S(2)}, u32[]{:S(2)}) collective-permute-start(bf16[64,32,128]{2,1,0:T(8,128)(2,1)} %own.1), channel_id=1, source_target_pairs={{0,192},{4,196},{8,200},{12,204},{16,208},{20,212},{24,216},{28,22... | collective-permute-start | bytes 1572872 | tf_op jit(solution)/shard_map/ppermute | solution.py:30
  4.8 28.4 %collective-permute-start = (bf16[64,32,128]{2,1,0:T(8,128)(2,1)}, bf16[64,32,128]{2,1,0:T(8,128)(2,1)S(1)}, u32[]{:S(2)}, u32[]{:S(2)}) collective-permute-start(bf16[64,32,128]{2,1,0:T(8,128)(2,1)} %own.1), channel_id=1, source_target_pairs={{0,64},{4,68},{8,72},{12,76},{16,80},{20,84},{24,88},{28,92},{32,2... | collective-permute-start | bytes 1572872 | tf_op jit(solution)/shard_map/ppermute | solution.py:30
  11.3 0.7 collective-permute-start.2
  13.1 22.6 %copy-start = (bf16[64,32,128]{2,1,0:T(8,128)(2,1)S(1)}, bf16[64,32,128]{2,1,0:T(8,128)(2,1)}, u32[]{:S(2)}) copy-start(bf16[64,32,128]{2,1,0:T(8,128)(2,1)} %own.1) | copy-start | bytes 1572868
  13.1 44.8 %all-to-all-start = ((bf16[8,16,32,128]{3,2,1,0:T(8,128)(2,1)}), bf16[8,16,32,128]{3,2,1,0:T(8,128)(2,1)S(1)}, u32[]{:S(2)}, u32[]{:S(2)}) async-start(bf16[8,16,32,128]{3,2,1,0:T(8,128)(2,1)} %broadcast_in_dim.2), calls=%async_computation | async-start | bytes 2097152 | tf_op jit(solution)/shard_map/all_to_all | solution.py:138
  33.2 11.8 %collective-permute-start.3 = (bf16[64,32,128]{2,1,0:T(8,128)(2,1)S(1)}, bf16[64,32,128]{2,1,0:T(8,128)(2,1)S(1)}, u32[]{:S(2)}, u32[]{:S(2)}) collective-permute-start(bf16[64,32,128]{2,1,0:T(8,128)(2,1)S(1)} %collective-permute-done.near), channel_id=1, source_target_pairs={{0,192},{4,196},{8,200},{12,204},{16,208},{20,212},{24,216},{28,22... | collective-permute-start | bytes 1572872 | tf_op jit(solution)/shard_map/ppermute | solution.py:30
  35.8 22.1 %copy-start.3 = (bf16[4,8,32,128]{3,2,1,0:T(8,128)(2,1)S(1)}, bf16[4,8,32,128]{3,2,1,0:T(8,128)(2,1)}, u32[]{:S(2)}) copy-start(bf16[4,8,32,128]{3,2,1,0:T(8,128)(2,1)} %masks.1) | copy-start | bytes 786436
  35.8 22.1 %copy-start.4 = (s32[32,32]{1,0:T(8,128)S(1)}, s32[32,32]{1,0:T(8,128)}, u32[]{:S(2)}) copy-start(s32[32,32]{1,0:T(8,128)} %shifts_ref.3) | copy-start | bytes 12292
  35.8 22.1 %copy-start.5 = (s32[3]{0:T(128)S(1)}, s32[3]{0:T(128)}, u32[]{:S(2)}) copy-start(s32[3]{0:T(128)} %pad_add_fusion.place_ref) | copy-start | bytes 40
  35.8 16.7 %collective-permute-start.4 = (bf16[128,32,128]{2,1,0:T(8,128)(2,1)S(1)}, bf16[128,32,128]{2,1,0:T(8,128)(2,1)S(1)}, u32[]{:S(2)}, u32[]{:S(2)}) collective-permute-start(bf16[128,32,128]{2,1,0:T(8,128)(2,1)S(1)} %pad_maximum_fusion), channel_id=1, source_target_pairs={{0,32},{4,36},{8,40},{12,44},{16,48},{20,52},{24,56},{28,60},{32,0... | collective-permute-start | bytes 3145736 | tf_op jit(solution)/shard_map/ppermute | solution.py:30
  46.1 11.8 %collective-permute-start.5 = (bf16[128,32,128]{2,1,0:T(8,128)(2,1)}, bf16[128,32,128]{2,1,0:T(8,128)(2,1)}, u32[]{:S(2)}, u32[]{:S(2)}) collective-permute-start(bf16[128,32,128]{2,1,0:T(8,128)(2,1)} %pad_maximum_fusion.1), channel_id=1, source_target_pairs={{0,32},{4,36},{8,40},{12,44},{16,48},{20,52},{24,56},{28,60},{32,0... | collective-permute-start | bytes 3145736 | tf_op jit(solution)/shard_map/ppermute | solution.py:30
  52.6 1.0 %copy-start.1 = (bf16[128,32,128]{2,1,0:T(8,128)(2,1)}, bf16[128,32,128]{2,1,0:T(8,128)(2,1)S(1)}, u32[]{:S(2)}) copy-start(bf16[128,32,128]{2,1,0:T(8,128)(2,1)S(1)} %collective-permute-done.4.twins) | copy-start | bytes 3145732
  57.9 1.2 %copy-start.2 = (bf16[128,32,128]{2,1,0:T(8,128)(2,1)S(1)}, bf16[128,32,128]{2,1,0:T(8,128)(2,1)}, u32[]{:S(2)}) copy-start(bf16[128,32,128]{2,1,0:T(8,128)(2,1)} %copy-done.1) | copy-start | bytes 3145732

commit v11 on v10

--- a/solution.py
+++ b/solution.py
@@ -134,7 +134,7 @@
     near = sent(x_blocks, along_z(0))
     far = sent(x_blocks, along_z(1))
     mine = jnp.broadcast_to(mine[None], (NY, SPAN, BS, LANES))
-    near, far, masks = lax.optimization_barrier((near, far, masks))
+    near, masks = lax.optimization_barrier((near, masks))
     left = lax.all_to_all(mine, "col", 0, 0)
     last = sent(near, along_z(1))
     twins = sent(jnp.concatenate([x_blocks, near], axis=0), other_core)

time: 86.9 us -> 87.7 us (level)
  waiting for transfers between devices: 9.44 us -> 17.4 us
  starting transfers between devices: 41.2 us -> 36.7 us
  blocking collectives: 20.1 us -> 17.4 us
    ppermute x6, waiting for transfers between devices: 5.07 us -> 17.4 us  [sent(): return lax.ppermute(value, AXES, device_pairs(move))]
    ppermute x6, starting transfers between devices: 24 us -> 19.6 us  [sent(): return lax.ppermute(value, AXES, device_pairs(move))]
    all_to_all x1, waiting for transfers between devices: 4.36 us -> 0.01 us  [local(): left = lax.all_to_all(mine, 'col', 0, 0)]
    all_to_all x1, blocking collectives: 20.1 us -> 17.4 us  [swapped_along_x(): return lax.all_to_all(value, 'row', 0, 0, axis_index_groups=groups)]
  transfers between devices with their start and end apart: 7 -> 7, of which waited for: 2 -> 3; matrix products, arithmetic and copies ran while one was open for 5% -> 5% of each run, Pallas kernels for 3% -> 3%
where the time goes in v11:
time: 87.7 us; the launch traced here: 86.8 us
  starting transfers between devices  36.7 us (42%)
  waiting for transfers between devices  17.4 us (20%)
  blocking collectives  17.4 us (20%)
  Pallas kernels  8.18 us (9%)
  local copies, waits for them, and re-layouts  4.29 us (5%)
  other arithmetic  2.6 us (3%)
    ppermute x6, starting transfers between devices, sent(): return lax.ppermute(value, AXES, device_pairs(move))  19.6 us
    all_to_all x1, blocking collectives, swapped_along_x(): return lax.all_to_all(value, 'row', 0, 0, axis_index_groups=groups)  17.4 us
    ppermute x6, waiting for transfers between devices, sent(): return lax.ppermute(value, AXES, device_pairs(move))  17.4 us
    all_to_all x1, starting transfers between devices, local(): left = lax.all_to_all(mine, 'col', 0, 0)  17.1 us
    pallas_call x1, Pallas kernels, local(): pl.pallas_call(product_kernel, out_shape=jax.ShapeDtypeStruct((NX, SPAN,...  5.95 us
    pallas_call x1, Pallas kernels, local(): pl.pallas_call(mask_kernel, out_shape=jax.ShapeDtypeStruct((NX, NEAR, BS,...  2.23 us
    unnamed x12, local copies, waits for them, and re-layouts  2.22 us
  transfers between devices with their start and end apart: 7, of which 3 were waited for; matrix products, arithmetic and copies ran while one was open for 5% of the time, Pallas kernels for 3%

profile of v11, /device:TPU:1, one launch (start us, length us, event | category | flops | bytes accessed | tf_op | source)
XLA Modules:
  0.0 86.8 jit_solution(4411576436814044819)
XLA Ops:
  0.0 8.4 %collective-permute-start = (bf16[64,32,128]{2,1,0:T(8,128)(2,1)}, bf16[64,32,128]{2,1,0:T(8,128)(2,1)S(1)}, u32[]{:S(2)}, u32[]{:S(2)}) collective-permute-start(bf16[64,32,128]{2,1,0:T(8,128)(2,1)} %own.1), channel_id=1, source_target_pairs={{0,64},{4,68},{8,72},{12,76},{16,80},{20,84},{24,88},{28,92},{32,2... | collective-permute-start | bytes 1572872 | tf_op jit(solution)/shard_map/ppermute | solution.py:30
  8.5 0.9 %constant_dynamic-slice_fusion = bf16[16,32,128]{2,1,0:T(8,128)(2,1)S(1)} fusion(bf16[64,32,128]{2,1,0:T(8,128)(2,1)} %own.1, s32[]{:T(128)S(6)} %select_n.3), kind=kLoop, calls=%fused_computation.3 | loop fusion | bytes 262148 | tf_op jit(solution)/shard_map/dynamic_slice | solution.py:125
  9.4 0.7 collective-permute-start.1
  10.0 0.0 collective-permute-done.1
  10.1 1.1 %broadcast_in_dim.2 = bf16[8,16,32,128]{3,2,1,0:T(8,128)(2,1)} broadcast(bf16[16,32,128]{2,1,0:T(8,128)(2,1)S(1)} %collective-permute-done.1), dimensions={1,2,3} | broadcast | bytes 1179648 | tf_op jit(solution)/shard_map/broadcast_in_dim | solution.py:136
  11.2 17.1 %all-to-all-start = ((bf16[8,16,32,128]{3,2,1,0:T(8,128)(2,1)}), bf16[8,16,32,128]{3,2,1,0:T(8,128)(2,1)S(1)}, u32[]{:S(2)}, u32[]{:S(2)}) async-start(bf16[8,16,32,128]{3,2,1,0:T(8,128)(2,1)} %broadcast_in_dim.2), calls=%async_computation | async-start | bytes 2097152 | tf_op jit(solution)/shard_map/all_to_all | solution.py:138
  28.3 1.9 %collective-permute-start.2 = (bf16[64,32,128]{2,1,0:T(8,128)(2,1)S(1)}, bf16[64,32,128]{2,1,0:T(8,128)(2,1)S(1)}, u32[]{:S(2)}, u32[]{:S(2)}) collective-permute-start(bf16[64,32,128]{2,1,0:T(8,128)(2,1)S(1)} %copy-done), channel_id=1, source_target_pairs={{0,192},{4,196},{8,200},{12,204},{16,208},{20,212},{24,216},{28,22... | collective-permute-start | bytes 1572872 | tf_op jit(solution)/shard_map/ppermute | solution.py:30
  30.3 0.7 pad_add_fusion.place_ref
  30.9 2.2 %masks.1 = bf16[4,8,32,128]{3,2,1,0:T(8,128)(2,1)} custom-call(s32[3]{0:T(128)} %pad_add_fusion.place_ref, s32[32,32]{1,0:T(8,128)} %shifts_ref.3), custom_call_target="tpu_custom_call" | custom-call | tf_op jit(solution)/shard_map/masks/pallas_call | solution.py:127
  33.1 3.4 %collective-permute-start.3 = (bf16[64,32,128]{2,1,0:T(8,128)(2,1)S(1)}, bf16[64,32,128]{2,1,0:T(8,128)(2,1)S(1)}, u32[]{:S(2)}, u32[]{:S(2)}) collective-permute-start(bf16[64,32,128]{2,1,0:T(8,128)(2,1)S(1)} %collective-permute-done.near), channel_id=1, source_target_pairs={{0,192},{4,196},{8,200},{12,204},{16,208},{20,212},{24,216},{28,22... | collective-permute-start | bytes 1572872 | tf_op jit(solution)/shard_map/ppermute | solution.py:30
  36.5 0.1 pad_maximum_fusion
  36.6 0.0 copy-start.4
  36.6 3.3 %collective-permute-start.4 = (bf16[128,32,128]{2,1,0:T(8,128)(2,1)S(1)}, bf16[128,32,128]{2,1,0:T(8,128)(2,1)S(1)}, u32[]{:S(2)}, u32[]{:S(2)}) collective-permute-start(bf16[128,32,128]{2,1,0:T(8,128)(2,1)S(1)} %pad_maximum_fusion), channel_id=1, source_target_pairs={{0,32},{4,36},{8,40},{12,44},{16,48},{20,52},{24,56},{28,60},{32,0... | collective-permute-start | bytes 3145736 | tf_op jit(solution)/shard_map/ppermute | solution.py:30
  40.0 2.9 %collective-permute-done.2.far = bf16[64,32,128]{2,1,0:T(8,128)(2,1)S(1)} collective-permute-done((bf16[64,32,128]{2,1,0:T(8,128)(2,1)S(1)}, bf16[64,32,128]{2,1,0:T(8,128)(2,1)S(1)}, u32[]{:S(2)}, u32[]{:S(2)}) %collective-permute-start.2) | collective-permute-done | bytes 524320 | tf_op jit(solution)/shard_map/ppermute | solution.py:30
  42.9 12.5 %collective-permute-done.3.last = bf16[64,32,128]{2,1,0:T(8,128)(2,1)S(1)} collective-permute-done((bf16[64,32,128]{2,1,0:T(8,128)(2,1)S(1)}, bf16[64,32,128]{2,1,0:T(8,128)(2,1)S(1)}, u32[]{:S(2)}, u32[]{:S(2)}) %collective-permute-start.3) | collective-permute-done | bytes 524320 | tf_op jit(solution)/shard_map/ppermute | solution.py:30
  55.4 1.1 %pad_maximum_fusion.1 = bf16[128,32,128]{2,1,0:T(8,128)(2,1)} fusion(bf16[64,32,128]{2,1,0:T(8,128)(2,1)S(1)} %collective-permute-done.3.last, bf16[64,32,128]{2,1,0:T(8,128)(2,1)S(1)} %collective-permute-done.2.far), kind=kLoop, calls=%fused_computation.1 | loop fusion | flops 524288 | bytes 2097152 | tf_op jit(solution)/shard_map/concatenate | solution.py:141
  56.5 1.9 %collective-permute-start.5 = (bf16[128,32,128]{2,1,0:T(8,128)(2,1)}, bf16[128,32,128]{2,1,0:T(8,128)(2,1)}, u32[]{:S(2)}, u32[]{:S(2)}) collective-permute-start(bf16[128,32,128]{2,1,0:T(8,128)(2,1)} %pad_maximum_fusion.1), channel_id=1, source_target_pairs={{0,32},{4,36},{8,40},{12,44},{16,48},{20,52},{24,56},{28,60},{32,0... | collective-permute-start | bytes 3145736 | tf_op jit(solution)/shard_map/ppermute | solution.py:30
  58.4 0.0 collective-permute-done.4.twins
  58.4 1.0 %copy-done.1 = bf16[128,32,128]{2,1,0:T(8,128)(2,1)} copy-done((bf16[128,32,128]{2,1,0:T(8,128)(2,1)}, bf16[128,32,128]{2,1,0:T(8,128)(2,1)S(1)}, u32[]{:S(2)}) %copy-start.1) | copy-done | bytes 1048600
  59.4 2.0 %collective-permute-done.5.twin_last = bf16[128,32,128]{2,1,0:T(8,128)(2,1)} collective-permute-done((bf16[128,32,128]{2,1,0:T(8,128)(2,1)}, bf16[128,32,128]{2,1,0:T(8,128)(2,1)}, u32[]{:S(2)}, u32[]{:S(2)}) %collective-permute-start.5) | collective-permute-done | bytes 1048608 | tf_op jit(solution)/shard_map/ppermute | solution.py:30
  61.4 1.2 %copy-done.2 = bf16[128,32,128]{2,1,0:T(8,128)(2,1)S(1)} copy-done((bf16[128,32,128]{2,1,0:T(8,128)(2,1)S(1)}, bf16[128,32,128]{2,1,0:T(8,128)(2,1)}, u32[]{:S(2)}) %copy-start.2) | copy-done | bytes 1048600
  62.6 5.9 %range_products.1 = f32[4,16,32,128]{3,2,1,0:T(8,128)S(1)} custom-call(s32[3]{0:T(128)S(1)} %copy-done.5, s32[32,32]{1,0:T(8,128)S(1)} %copy-done.4, bf16[4,8,32,128]{3,2,1,0:T(8,128)(2,1)S(1)} %copy-done.3, bf16[8,16,32,128]{3,2,1,0:T(8,128)(2,1)S(1)} %all-to-all-done.left, bf16[64,32,128]{2,1,0:T(8,128)(2,1)S(1)} %copy-done, ...), custom_call_target="tpu_custom_call" | custom-call | tf_op jit(solution)/shard_map/range_products/pallas_call | solution.py:142
  68.6 17.4 %all_to_all.10 = f32[4,16,32,128]{3,2,1,0:T(8,128)S(1)} all-to-all(f32[4,16,32,128]{3,2,1,0:T(8,128)S(1)} %range_products.1), channel_id=1, replica_groups={{0,256,512,768},{32,288,544,800},{64,320,576,832},{96,352,608,864},{128..., dimensions={0} | all-to-all | bytes 2097152 | tf_op jit(solution)/shard_map/all_to_all | solution.py:49
  86.0 0.8 reduce_sum.9
  (11 shorter events, 0.0 us)
Async XLA Ops:
  0.0 33.1 %collective-permute-start = (bf16[64,32,128]{2,1,0:T(8,128)(2,1)}, bf16[64,32,128]{2,1,0:T(8,128)(2,1)S(1)}, u32[]{:S(2)}, u32[]{:S(2)}) collective-permute-start(bf16[64,32,128]{2,1,0:T(8,128)(2,1)} %own.1), channel_id=1, source_target_pairs={{0,64},{4,68},{8,72},{12,76},{16,80},{20,84},{24,88},{28,92},{32,2... | collective-permute-start | bytes 1572872 | tf_op jit(solution)/shard_map/ppermute | solution.py:30
  9.4 0.7 collective-permute-start.1
  11.2 17.1 %copy-start = (bf16[64,32,128]{2,1,0:T(8,128)(2,1)S(1)}, bf16[64,32,128]{2,1,0:T(8,128)(2,1)}, u32[]{:S(2)}) copy-start(bf16[64,32,128]{2,1,0:T(8,128)(2,1)} %own.1) | copy-start | bytes 1572868
  11.2 48.2 %all-to-all-start = ((bf16[8,16,32,128]{3,2,1,0:T(8,128)(2,1)}), bf16[8,16,32,128]{3,2,1,0:T(8,128)(2,1)S(1)}, u32[]{:S(2)}, u32[]{:S(2)}) async-start(bf16[8,16,32,128]{3,2,1,0:T(8,128)(2,1)} %broadcast_in_dim.2), calls=%async_computation | async-start | bytes 2097152 | tf_op jit(solution)/shard_map/all_to_all | solution.py:138
  28.3 14.6 %collective-permute-start.2 = (bf16[64,32,128]{2,1,0:T(8,128)(2,1)S(1)}, bf16[64,32,128]{2,1,0:T(8,128)(2,1)S(1)}, u32[]{:S(2)}, u32[]{:S(2)}) collective-permute-start(bf16[64,32,128]{2,1,0:T(8,128)(2,1)S(1)} %copy-done), channel_id=1, source_target_pairs={{0,192},{4,196},{8,200},{12,204},{16,208},{20,212},{24,216},{28,22... | collective-permute-start | bytes 1572872 | tf_op jit(solution)/shard_map/ppermute | solution.py:30
  33.1 22.2 %collective-permute-start.3 = (bf16[64,32,128]{2,1,0:T(8,128)(2,1)S(1)}, bf16[64,32,128]{2,1,0:T(8,128)(2,1)S(1)}, u32[]{:S(2)}, u32[]{:S(2)}) collective-permute-start(bf16[64,32,128]{2,1,0:T(8,128)(2,1)S(1)} %collective-permute-done.near), channel_id=1, source_target_pairs={{0,192},{4,196},{8,200},{12,204},{16,208},{20,212},{24,216},{28,22... | collective-permute-start | bytes 1572872 | tf_op jit(solution)/shard_map/ppermute | solution.py:30
  36.6 24.8 %copy-start.3 = (bf16[4,8,32,128]{3,2,1,0:T(8,128)(2,1)S(1)}, bf16[4,8,32,128]{3,2,1,0:T(8,128)(2,1)}, u32[]{:S(2)}) copy-start(bf16[4,8,32,128]{3,2,1,0:T(8,128)(2,1)} %masks.1) | copy-start | bytes 786436
  36.6 24.8 %copy-start.4 = (s32[32,32]{1,0:T(8,128)S(1)}, s32[32,32]{1,0:T(8,128)}, u32[]{:S(2)}) copy-start(s32[32,32]{1,0:T(8,128)} %shifts_ref.3) | copy-start | bytes 12292
  36.6 24.8 %copy-start.5 = (s32[3]{0:T(128)S(1)}, s32[3]{0:T(128)}, u32[]{:S(2)}) copy-start(s32[3]{0:T(128)} %pad_add_fusion.place_ref) | copy-start | bytes 40
  36.6 21.8 %collective-permute-start.4 = (bf16[128,32,128]{2,1,0:T(8,128)(2,1)S(1)}, bf16[128,32,128]{2,1,0:T(8,128)(2,1)S(1)}, u32[]{:S(2)}, u32[]{:S(2)}) collective-permute-start(bf16[128,32,128]{2,1,0:T(8,128)(2,1)S(1)} %pad_maximum_fusion), channel_id=1, source_target_pairs={{0,32},{4,36},{8,40},{12,44},{16,48},{20,52},{24,56},{28,60},{32,0... | collective-permute-start | bytes 3145736 | tf_op jit(solution)/shard_map/ppermute | solution.py:30
  56.5 4.9 %collective-permute-start.5 = (bf16[128,32,128]{2,1,0:T(8,128)(2,1)}, bf16[128,32,128]{2,1,0:T(8,128)(2,1)}, u32[]{:S(2)}, u32[]{:S(2)}) collective-permute-start(bf16[128,32,128]{2,1,0:T(8,128)(2,1)} %pad_maximum_fusion.1), channel_id=1, source_target_pairs={{0,32},{4,36},{8,40},{12,44},{16,48},{20,52},{24,56},{28,60},{32,0... | collective-permute-start | bytes 3145736 | tf_op jit(solution)/shard_map/ppermute | solution.py:30
  58.4 1.0 %copy-start.1 = (bf16[128,32,128]{2,1,0:T(8,128)(2,1)}, bf16[128,32,128]{2,1,0:T(8,128)(2,1)S(1)}, u32[]{:S(2)}) copy-start(bf16[128,32,128]{2,1,0:T(8,128)(2,1)S(1)} %collective-permute-done.4.twins) | copy-start | bytes 3145732
  61.4 1.2 %copy-start.2 = (bf16[128,32,128]{2,1,0:T(8,128)(2,1)S(1)}, bf16[128,32,128]{2,1,0:T(8,128)(2,1)}, u32[]{:S(2)}) copy-start(bf16[128,32,128]{2,1,0:T(8,128)(2,1)} %copy-done.1) | copy-start | bytes 3145732

commit v12 on v8

--- a/solution.py
+++ b/solution.py
@@ -110,7 +110,7 @@
             out[t, p] = jnp.dot(lhs, rhs, preferred_element_type=jnp.float32)
         return carry
 
-    lax.fori_loop(0, SPAN, position_step, 0)
+    lax.fori_loop(0, SPAN, position_step, 0, unroll=4)
 
 
 def local(x_blocks, shifts):

time: 85.6 us -> 83.8 us (0.979)
  Pallas kernels: 8.18 us -> 6.41 us
    pallas_call x1, Pallas kernels: 5.95 us -> 4.18 us  [local(): pl.pallas_call(product_kernel, out_shape=jax.ShapeDtypeStruct((NX, SPAN,...]
where the time goes in v12:
time: 83.8 us; the launch traced here: 83.4 us
  waiting for transfers between devices  26.6 us (32%)
  starting transfers between devices  25.2 us (30%)
  blocking collectives  19.2 us (23%)
  Pallas kernels  6.41 us (8%)
  local copies, waits for them, and re-layouts  4.44 us (5%)
  other arithmetic  1.36 us (2%)
    ppermute x5, waiting for transfers between devices, sent(): return lax.ppermute(value, AXES, device_pairs(move))  22.1 us
    ppermute x5, starting transfers between devices, sent(): return lax.ppermute(value, AXES, device_pairs(move))  20.7 us
    all_to_all x1, blocking collectives, swapped_along_x(): return lax.all_to_all(value, 'row', 0, 0, axis_index_groups=groups)  19.2 us
    all_to_all x1, waiting for transfers between devices, local(): lax.all_to_all(jnp.broadcast_to(mine[None], (NY, SPAN, BS, LANES)), 'col'...  4.56 us
    all_to_all x1, starting transfers between devices, local(): lax.all_to_all(jnp.broadcast_to(mine[None], (NY, SPAN, BS, LANES)), 'col'...  4.51 us
    pallas_call x1, Pallas kernels, local(): pl.pallas_call(product_kernel, out_shape=jax.ShapeDtypeStruct((NX, SPAN,...  4.18 us
    unnamed x13, local copies, waits for them, and re-layouts  2.28 us
    pallas_call x1, Pallas kernels, local(): pl.pallas_call(mask_kernel, out_shape=jax.ShapeDtypeStruct((NX, NEAR, BS,...  2.23 us
  transfers between devices with their start and end apart: 6, of which 3 were waited for; matrix products, arithmetic and copies ran while one was open for 3% of the time, Pallas kernels for 3%

profile of v12, /device:TPU:64, one launch (start us, length us, event | category | flops | bytes accessed | tf_op | source)
XLA Modules:
  0.0 83.4 jit_solution(9991567601642080617)
XLA Ops:
  0.0 14.3 %collective-permute-start = (bf16[64,32,128]{2,1,0:T(8,128)(2,1)}, bf16[64,32,128]{2,1,0:T(8,128)(2,1)S(1)}, u32[]{:S(2)}, u32[]{:S(2)}) collective-permute-start(bf16[64,32,128]{2,1,0:T(8,128)(2,1)} %param.2), channel_id=1, source_target_pairs={{0,64},{4,68},{8,72},{12,76},{16,80},{20,84},{24,88},{28,92},{32,2... | collective-permute-start | bytes 1572872 | tf_op jit(solution)/shard_map/ppermute | solution.py:30
  14.3 0.9 %constant_dynamic-slice_fusion = bf16[16,32,128]{2,1,0:T(8,128)(2,1)S(1)} fusion(bf16[64,32,128]{2,1,0:T(8,128)(2,1)} %param.2, s32[]{:T(128)S(6)} %select_n.3), kind=kLoop, calls=%fused_computation.3 | loop fusion | bytes 262148 | tf_op jit(solution)/shard_map/dynamic_slice | solution.py:125
  15.3 0.7 collective-permute-start.1
  16.0 0.6 pad_add_fusion.place_ref
  16.6 2.2 %masks.1 = bf16[4,8,32,128]{3,2,1,0:T(8,128)(2,1)} custom-call(s32[3]{0:T(128)} %pad_add_fusion.place_ref, s32[32,32]{1,0:T(8,128)} %shifts_ref.3), custom_call_target="tpu_custom_call" | custom-call | tf_op jit(solution)/shard_map/masks/pallas_call | solution.py:127
  18.8 0.0 copy-done.5
  18.8 0.0 collective-permute-done.1
  18.8 3.7 %collective-permute-done = bf16[64,32,128]{2,1,0:T(8,128)(2,1)S(1)} collective-permute-done((bf16[64,32,128]{2,1,0:T(8,128)(2,1)}, bf16[64,32,128]{2,1,0:T(8,128)(2,1)S(1)}, u32[]{:S(2)}, u32[]{:S(2)}) %collective-permute-start) | collective-permute-done | bytes 524320 | tf_op jit(solution)/shard_map/ppermute | solution.py:30
  22.5 0.1 constant_dynamic-update-slice_fusion.pair
  22.6 1.9 %collective-permute-start.2 = (bf16[128,32,128]{2,1,0:T(8,128)(2,1)S(1)}, bf16[128,32,128]{2,1,0:T(8,128)(2,1)S(1)}, u32[]{:S(2)}, u32[]{:S(2)}) collective-permute-start(bf16[128,32,128]{2,1,0:T(8,128)(2,1)S(1)} %constant_dynamic-update-slice_fusion.pair), channel_id=1, source_target_pairs={{0,192},{4,196},{8,200},{12,204},{16,208},{20,212},{24,216},{28,22... | collective-permute-start | bytes 3145736 | tf_op jit(solution)/shard_map/ppermute | solution.py:30
  24.5 1.2 %broadcast_in_dim.2 = bf16[8,16,32,128]{3,2,1,0:T(8,128)(2,1)} broadcast(bf16[16,32,128]{2,1,0:T(8,128)(2,1)S(1)} %collective-permute-done.1), dimensions={1,2,3} | broadcast | bytes 1179648 | tf_op jit(solution)/shard_map/broadcast_in_dim | solution.py:136
  25.7 4.5 %all-to-all-start = ((bf16[8,16,32,128]{3,2,1,0:T(8,128)(2,1)}), bf16[8,16,32,128]{3,2,1,0:T(8,128)(2,1)S(1)}, u32[]{:S(2)}, u32[]{:S(2)}) async-start(bf16[8,16,32,128]{3,2,1,0:T(8,128)(2,1)} %broadcast_in_dim.2), calls=%async_computation | async-start | bytes 2097152 | tf_op jit(solution)/shard_map/all_to_all | solution.py:136
  30.2 1.9 %collective-permute-start.3 = (bf16[128,32,128]{2,1,0:T(8,128)(2,1)S(1)}, bf16[128,32,128]{2,1,0:T(8,128)(2,1)S(1)}, u32[]{:S(2)}, u32[]{:S(2)}) collective-permute-start(bf16[128,32,128]{2,1,0:T(8,128)(2,1)S(1)} %constant_dynamic-update-slice_fusion.pair), channel_id=1, source_target_pairs={{0,32},{4,36},{8,40},{12,44},{16,48},{20,52},{24,56},{28,60},{32,0... | collective-permute-start | bytes 3145736 | tf_op jit(solution)/shard_map/ppermute | solution.py:30
  32.1 18.4 %collective-permute-done.2.far = bf16[128,32,128]{2,1,0:T(8,128)(2,1)S(1)} collective-permute-done((bf16[128,32,128]{2,1,0:T(8,128)(2,1)S(1)}, bf16[128,32,128]{2,1,0:T(8,128)(2,1)S(1)}, u32[]{:S(2)}, u32[]{:S(2)}) %collective-permute-start.2) | collective-permute-done | bytes 1048608 | tf_op jit(solution)/shard_map/ppermute | solution.py:30
  50.5 1.9 %collective-permute-start.4 = (bf16[128,32,128]{2,1,0:T(8,128)(2,1)S(1)}, bf16[128,32,128]{2,1,0:T(8,128)(2,1)}, u32[]{:S(2)}, u32[]{:S(2)}) collective-permute-start(bf16[128,32,128]{2,1,0:T(8,128)(2,1)S(1)} %collective-permute-done.2.far), channel_id=1, source_target_pairs={{0,32},{4,36},{8,40},{12,44},{16,48},{20,52},{24,56},{28,60},{32,0... | collective-permute-start | bytes 3145736 | tf_op jit(solution)/shard_map/ppermute | solution.py:30
  52.4 0.0 collective-permute-done.3.twin_pair
  52.4 1.0 %copy-done = bf16[128,32,128]{2,1,0:T(8,128)(2,1)} copy-done((bf16[128,32,128]{2,1,0:T(8,128)(2,1)}, bf16[128,32,128]{2,1,0:T(8,128)(2,1)S(1)}, u32[]{:S(2)}) %copy-start) | copy-done | bytes 1048600
  53.5 4.6 %all-to-all-done.left = bf16[8,16,32,128]{3,2,1,0:T(8,128)(2,1)S(1)} async-done(((bf16[8,16,32,128]{3,2,1,0:T(8,128)(2,1)}), bf16[8,16,32,128]{3,2,1,0:T(8,128)(2,1)S(1)}, u32[]{:S(2)}, u32[]{:S(2)}) %all-to-all-start) | async-done | bytes 1048608 | tf_op jit(solution)/shard_map/all_to_all | solution.py:136
  58.0 0.0 collective-permute-done.4.twin_far
  58.0 0.0 copy-done.2
  58.0 1.2 %copy-done.1 = bf16[128,32,128]{2,1,0:T(8,128)(2,1)S(1)} copy-done((bf16[128,32,128]{2,1,0:T(8,128)(2,1)S(1)}, bf16[128,32,128]{2,1,0:T(8,128)(2,1)}, u32[]{:S(2)}) %copy-start.1) | copy-done | bytes 1048600
  59.3 4.2 %range_products.1 = f32[4,16,32,128]{3,2,1,0:T(8,128)S(1)} custom-call(s32[3]{0:T(128)S(1)} %copy-done.4, s32[32,32]{1,0:T(8,128)S(1)} %copy-done.3, bf16[4,8,32,128]{3,2,1,0:T(8,128)(2,1)S(1)} %copy-done.2, bf16[8,16,32,128]{3,2,1,0:T(8,128)(2,1)S(1)} %all-to-all-done.left, bf16[128,32,128]{2,1,0:T(8,128)(2,1)S(1)} %constant_dynamic-update-slice_fusion.pair, ...), custom_call_target="tpu_custom_call" | custom-call | tf_op jit(solution)/shard_map/range_products/pallas_call | solution.py:141
  63.5 19.2 %all_to_all.10 = f32[4,16,32,128]{3,2,1,0:T(8,128)S(1)} all-to-all(f32[4,16,32,128]{3,2,1,0:T(8,128)S(1)} %range_products.1), channel_id=1, replica_groups={{0,256,512,768},{32,288,544,800},{64,320,576,832},{96,352,608,864},{128..., dimensions={0} | all-to-all | bytes 2097152 | tf_op jit(solution)/shard_map/all_to_all | solution.py:49
  82.6 0.8 reduce_sum.9
  (9 shorter events, 0.0 us)
Async XLA Ops:
  0.0 18.8 %copy-start.5 = (bf16[64,32,128]{2,1,0:T(8,128)(2,1)S(1)}, bf16[64,32,128]{2,1,0:T(8,128)(2,1)}, u32[]{:S(2)}) copy-start(bf16[64,32,128]{2,1,0:T(8,128)(2,1)} %param.2) | copy-start | bytes 1572868
  0.0 22.5 %collective-permute-start = (bf16[64,32,128]{2,1,0:T(8,128)(2,1)}, bf16[64,32,128]{2,1,0:T(8,128)(2,1)S(1)}, u32[]{:S(2)}, u32[]{:S(2)}) collective-permute-start(bf16[64,32,128]{2,1,0:T(8,128)(2,1)} %param.2), channel_id=1, source_target_pairs={{0,64},{4,68},{8,72},{12,76},{16,80},{20,84},{24,88},{28,92},{32,2... | collective-permute-start | bytes 1572872 | tf_op jit(solution)/shard_map/ppermute | solution.py:30
  15.3 3.6 %collective-permute-start.1 = (bf16[16,32,128]{2,1,0:T(8,128)(2,1)S(1)}, bf16[16,32,128]{2,1,0:T(8,128)(2,1)S(1)}, u32[]{:S(2)}, u32[]{:S(2)}) collective-permute-start(bf16[16,32,128]{2,1,0:T(8,128)(2,1)S(1)} %constant_dynamic-slice_fusion), channel_id=1, source_target_pairs={{0,0},{4,4},{8,284},{12,280},{16,520},{20,540},{24,788},{28,768},{... | collective-permute-start | bytes 393224 | tf_op jit(solution)/shard_map/ppermute | solution.py:30
  22.6 27.9 %collective-permute-start.2 = (bf16[128,32,128]{2,1,0:T(8,128)(2,1)S(1)}, bf16[128,32,128]{2,1,0:T(8,128)(2,1)S(1)}, u32[]{:S(2)}, u32[]{:S(2)}) collective-permute-start(bf16[128,32,128]{2,1,0:T(8,128)(2,1)S(1)} %constant_dynamic-update-slice_fusion.pair), channel_id=1, source_target_pairs={{0,192},{4,196},{8,200},{12,204},{16,208},{20,212},{24,216},{28,22... | collective-permute-start | bytes 3145736 | tf_op jit(solution)/shard_map/ppermute | solution.py:30
  25.7 32.3 %copy-start.2 = (bf16[4,8,32,128]{3,2,1,0:T(8,128)(2,1)S(1)}, bf16[4,8,32,128]{3,2,1,0:T(8,128)(2,1)}, u32[]{:S(2)}) copy-start(bf16[4,8,32,128]{3,2,1,0:T(8,128)(2,1)} %masks.1) | copy-start | bytes 786436
  25.7 32.3 %copy-start.3 = (s32[32,32]{1,0:T(8,128)S(1)}, s32[32,32]{1,0:T(8,128)}, u32[]{:S(2)}) copy-start(s32[32,32]{1,0:T(8,128)} %shifts_ref.3) | copy-start | bytes 12292
  25.7 32.3 %copy-start.4 = (s32[3]{0:T(128)S(1)}, s32[3]{0:T(128)}, u32[]{:S(2)}) copy-start(s32[3]{0:T(128)} %pad_add_fusion.place_ref) | copy-start | bytes 40
  25.7 32.3 %all-to-all-start = ((bf16[8,16,32,128]{3,2,1,0:T(8,128)(2,1)}), bf16[8,16,32,128]{3,2,1,0:T(8,128)(2,1)S(1)}, u32[]{:S(2)}, u32[]{:S(2)}) async-start(bf16[8,16,32,128]{3,2,1,0:T(8,128)(2,1)} %broadcast_in_dim.2), calls=%async_computation | async-start | bytes 2097152 | tf_op jit(solution)/shard_map/all_to_all | solution.py:136
  30.2 22.2 %collective-permute-start.3 = (bf16[128,32,128]{2,1,0:T(8,128)(2,1)S(1)}, bf16[128,32,128]{2,1,0:T(8,128)(2,1)S(1)}, u32[]{:S(2)}, u32[]{:S(2)}) collective-permute-start(bf16[128,32,128]{2,1,0:T(8,128)(2,1)S(1)} %constant_dynamic-update-slice_fusion.pair), channel_id=1, source_target_pairs={{0,32},{4,36},{8,40},{12,44},{16,48},{20,52},{24,56},{28,60},{32,0... | collective-permute-start | bytes 3145736 | tf_op jit(solution)/shard_map/ppermute | solution.py:30
  50.5 7.5 %collective-permute-start.4 = (bf16[128,32,128]{2,1,0:T(8,128)(2,1)S(1)}, bf16[128,32,128]{2,1,0:T(8,128)(2,1)}, u32[]{:S(2)}, u32[]{:S(2)}) collective-permute-start(bf16[128,32,128]{2,1,0:T(8,128)(2,1)S(1)} %collective-permute-done.2.far), channel_id=1, source_target_pairs={{0,32},{4,36},{8,40},{12,44},{16,48},{20,52},{24,56},{28,60},{32,0... | collective-permute-start | bytes 3145736 | tf_op jit(solution)/shard_map/ppermute | solution.py:30
  52.4 1.0 %copy-start = (bf16[128,32,128]{2,1,0:T(8,128)(2,1)}, bf16[128,32,128]{2,1,0:T(8,128)(2,1)S(1)}, u32[]{:S(2)}) copy-start(bf16[128,32,128]{2,1,0:T(8,128)(2,1)S(1)} %collective-permute-done.3.twin_pair) | copy-start | bytes 3145732
  58.0 1.2 %copy-start.1 = (bf16[128,32,128]{2,1,0:T(8,128)(2,1)S(1)}, bf16[128,32,128]{2,1,0:T(8,128)(2,1)}, u32[]{:S(2)}) copy-start(bf16[128,32,128]{2,1,0:T(8,128)(2,1)} %copy-done) | copy-start | bytes 3145732
